TPU v7x, 32 devices: a whole 2x2x4 slice. The times are simulated.
32 devices in a mesh: dp: 16 (over z, x, core), blk: 2 (over y).
Axes of the slice: x: 2, y: 2, z: 4, core: 2. Of those that a mesh axis runs over, the one named last changes fastest.
Arguments:
- latents: bfloat16 [64, 64, 768], P('dp', 'blk'), may hold values from -6 to 6
- restore: int32 [64, 256], P('dp', 'blk'), may hold values from 0 to 64, as said below
- bucket: int32 [64], P('dp'), may hold values from 0 to 2, as said below
- cotangent: bfloat16 [64, 256, 512], P('dp', 'blk'), may hold values from -6 to 6
- flat_weights: float32 [3538944], P(('dp', 'blk')), may hold values from -1 to 1
- flat_first: float32 [3538944], P(('dp', 'blk')), may hold values from -0.0008544922 to 0.0008544922
- flat_second: float32 [3538944], P(('dp', 'blk')), may hold values from 1.4833147e-08 to 5.9219786e-08
- vectors: float32 [14, 512], replicated, may hold values from -3 to 3
- vector_first: float32 [14, 512], replicated, may hold values from -0.0034179688 to 0.0034179688
- vector_second: float32 [14, 512], replicated, may hold values from 2.3687915e-07 to 9.587966e-07
Outputs:
- block_out: float32 [64, 256, 512], P('dp', 'blk')
- latent_grad: float32 [64, 64, 768], P('dp', 'blk')
- new_first: float32 [3538944], P(('dp', 'blk'))
- new_second: float32 [3538944], P(('dp', 'blk'))
- new_weights: float32 [3538944], P(('dp', 'blk'))
- vector_first_new: float32 [14, 512], replicated
- vector_second_new: float32 [14, 512], replicated
- vectors_new: float32 [14, 512], replicated
- reduce_bias_grad: float32 [512], replicated
- grad_norm: float32 [], replicated
Inputs may be any that keep to these rules, and one draw needn't show every extreme that they name: In each micro-batch of the images of one index of dp, images m * 2 to (m+1) * 2 - 1 of that index, at least one image has bucket 2. `restore`: for an image of length L, the L // 4 valid slots whose values are below 64 hold 0 to L // 4 - 1, each once; every other slot holds 64; latent rows from L // 4 on are never named.
All inputs are finite; a program needn't handle non-finite values.
Results may differ from a plain program's by a relative error of at most 0.014.
Values may be sent and summed in bfloat16 or wider, within the bound.
No kernel may reach another device: no remote copies, remote signals or barrier semaphores. Data moves between devices by JAX's collectives and lax.ppermute only.
A program may use at most 128 MiB of HBM per device.

v0:
```python
import math

import jax
import jax.numpy as jnp
from jax import lax
from jax.sharding import PartitionSpec as P

DIN = 768
D = 512
HEADS = 16
HD = 32
FF = 2048
SLOTS = 256
KMAX = 64
MB = 2
STEP = 10
NPARAM = 3538944


first_decay = 0.9
second_decay = 0.95
learn_rate = 0.05
vector_rate = 0.5
decay_weight = 0.05
adam_eps = 1e-08
clip_norm = 1.0


def unpack(flat):
    shapes = [(DIN, D), (D, 3 * D), (D, D), (D, FF), (FF, D)]
    pieces = []
    offset = 0
    for height, width in shapes:
        pieces.append(flat[offset : offset + height * width].reshape(height, width))
        offset = offset + height * width
    return pieces


def image_lengths(bucket):
    return jnp.where(
        bucket == 0, SLOTS * 100 // 256, jnp.where(bucket == 1, SLOTS * 196 // 256, SLOTS)
    ).astype(jnp.int32)


def position_rows(first_slot, count):
    slot = (first_slot + jnp.arange(count, dtype=jnp.int32)).astype(jnp.float32)[:, None]
    column = jnp.arange(D // 2, dtype=jnp.int32).astype(jnp.float32)[None, :]
    angle = slot * jnp.exp(-math.log(10000.0) * column / (D // 2))
    return jnp.concatenate([jnp.sin(angle), jnp.cos(angle)], axis=1)


def layer_norm(value, gain, shift):
    centred = value - jnp.mean(value, axis=-1, keepdims=True)
    spread = jnp.mean(centred * centred, axis=-1, keepdims=True)
    return centred * lax.rsqrt(spread + 1e-06) * gain + shift


def smooth_gate(value):
    return jax.nn.gelu(value, approximate=False)


def column_sum(value):
    return jnp.sum(value.astype(jnp.float32), axis=(0, 1))


def adam_update(grad, first, second, weight, rate, shrink):
    first_new = first_decay * first + (1.0 - first_decay) * grad
    second_new = second_decay * second + (1.0 - second_decay) * grad * grad
    first_hat = first_new / (1.0 - first_decay**STEP)
    second_hat = second_new / (1.0 - second_decay**STEP)
    weight_new = weight - rate * (first_hat / (jnp.sqrt(second_hat) + adam_eps) + shrink * weight)
    return (first_new, second_new, weight_new)


def one_batch(weights, vectors, encoder_rows, restore_rows, lengths, cot_rows, side):
    embedding_matrix, joint_weight, output_weight, expand_weight, reduce_weight = weights
    images, local_slots = restore_rows.shape
    scale = HD ** (-0.5)
    table = position_rows(side * local_slots, local_slots)
    embedded_rows = (
        jnp.einsum(
            "tqx,xj->tqj", encoder_rows, embedding_matrix, preferred_element_type=jnp.float32
        )
        + vectors[0]
    ).astype(jnp.bfloat16)
    every_row = lax.all_gather(embedded_rows, "blk", axis=1, tiled=True)
    select_rows = restore_rows[:, :, None] == jnp.arange(KMAX, dtype=jnp.int32)[None, None, :]
    mask_token_rows = (restore_rows >= KMAX).astype(jnp.float32)[:, :, None]
    start_offset = (
        jnp.einsum(
            "ywq,yqj->ywj",
            select_rows.astype(jnp.bfloat16),
            every_row,
            preferred_element_type=jnp.float32,
        )
        + mask_token_rows * vectors[1]
        + table[None]
    )
    normed, pull_first = jax.vjp(layer_norm, start_offset, vectors[2], vectors[3])
    normed_low = normed.astype(jnp.bfloat16)
    joint_bias = jnp.concatenate([vectors[4], jnp.zeros_like(vectors[4]), vectors[5]])
    joint = (
        jnp.einsum("bsd,de->bse", normed_low, joint_weight, preferred_element_type=jnp.float32)
        + joint_bias
    ).astype(jnp.bfloat16)
    query = joint[:, :, :D].reshape(images, local_slots, HEADS, HD)
    pairs = lax.all_gather(joint[:, :, D:], "blk", axis=1, tiled=True)
    key_valid = jnp.arange(SLOTS, dtype=jnp.int32)[None, :] < lengths[:, None]

    def attend(gathered):
        keys = gathered[:, :, :D].reshape(images, SLOTS, HEADS, HD)
        values = gathered[:, :, D:].reshape(images, SLOTS, HEADS, HD)
        scores = (
            jnp.einsum("bqhe,bkhe->bhqk", query, keys, preferred_element_type=jnp.float32) * scale
        )
        scores = jnp.where(key_valid[:, None, None, :], scores, -1e30)
        return (keys, values, scores)

    keys, values, scores = attend(pairs)
    top = jnp.max(scores, axis=-1, keepdims=True)
    total = jnp.sum(jnp.exp(scores - top), axis=-1, keepdims=True)
    probs_low = (jnp.exp(scores - top) / total).astype(jnp.bfloat16)
    mixed = (
        jnp.einsum("bhqk,bkhe->bqhe", probs_low, values, preferred_element_type=jnp.float32)
        .reshape(images, local_slots, D)
        .astype(jnp.bfloat16)
    )
    middle = (
        start_offset
        + jnp.einsum("bsd,de->bse", mixed, output_weight, preferred_element_type=jnp.float32)
        + vectors[6]
    )
    normed_two, pull_second = jax.vjp(layer_norm, middle, vectors[7], vectors[8])
    normed_two_low = normed_two.astype(jnp.bfloat16)
    hidden = jnp.einsum(
        "bsd,df->bsf", normed_two_low, expand_weight, preferred_element_type=jnp.float32
    ) + vectors[10:14].reshape(-1)
    active, pull_gate = jax.vjp(smooth_gate, hidden)
    active_low = active.astype(jnp.bfloat16)
    result = (
        middle
        + jnp.einsum("bsf,fd->bsd", active_low, reduce_weight, preferred_element_type=jnp.float32)
        + vectors[9]
    )
    slot_ids = side * local_slots + jnp.arange(local_slots, dtype=jnp.int32)
    row_valid = (slot_ids[None, :] < lengths[:, None]).astype(jnp.float32)[:, :, None]
    back = cot_rows.astype(jnp.float32) * row_valid
    back_out = back.astype(jnp.bfloat16)
    grad_reduce = jnp.einsum(
        "bsf,bsd->fd", active_low, back_out, preferred_element_type=jnp.float32
    )
    bias_reduce = column_sum(back_out)
    back_active = jnp.einsum(
        "bsd,fd->bsf", back_out, reduce_weight, preferred_element_type=jnp.float32
    )
    (back_hidden,) = pull_gate(back_active)
    back_hidden_low = back_hidden.astype(jnp.bfloat16)
    grad_expand = jnp.einsum(
        "bsd,bsf->df", normed_two_low, back_hidden_low, preferred_element_type=jnp.float32
    )
    bias_expand = column_sum(back_hidden_low)
    back_normed_two = jnp.einsum(
        "bsf,df->bsd", back_hidden_low, expand_weight, preferred_element_type=jnp.float32
    )
    back_middle, gain_two, shift_two = pull_second(back_normed_two)
    back_middle = back_middle + back
    back_branch = back_middle.astype(jnp.bfloat16)
    grad_output = jnp.einsum("bsd,bse->de", mixed, back_branch, preferred_element_type=jnp.float32)
    bias_output = column_sum(back_branch)
    back_mixed = jnp.einsum(
        "bse,de->bsd", back_branch, output_weight, preferred_element_type=jnp.float32
    ).astype(jnp.bfloat16)
    back_mixed = back_mixed.reshape(images, local_slots, HEADS, HD)
    keys, values, scores = attend(pairs)
    probs = jnp.exp(scores - top) / total
    probs_low = probs.astype(jnp.bfloat16)
    back_probs = jnp.einsum(
        "bqhe,bkhe->bhqk", back_mixed, values, preferred_element_type=jnp.float32
    )
    back_scores = probs * (back_probs - jnp.sum(probs * back_probs, axis=-1, keepdims=True))
    back_scores_low = (back_scores * scale).astype(jnp.bfloat16)
    back_query = jnp.einsum(
        "bhqk,bkhe->bqhe", back_scores_low, keys, preferred_element_type=jnp.float32
    ).astype(jnp.bfloat16)
    back_keys = jnp.einsum(
        "bhqk,bqhe->bkhe", back_scores_low, query, preferred_element_type=jnp.float32
    ).reshape(images, SLOTS, D)
    back_values = jnp.einsum(
        "bhqk,bqhe->bkhe", probs_low, back_mixed, preferred_element_type=jnp.float32
    ).reshape(images, SLOTS, D)
    key_terms = jnp.concatenate([back_keys, back_values], axis=2)
    back_pairs = lax.psum_scatter(
        key_terms.astype(jnp.bfloat16), "blk", scatter_dimension=1, tiled=True
    )
    back_joint = jnp.concatenate([back_query.reshape(images, local_slots, D), back_pairs], axis=2)
    grad_joint = jnp.einsum(
        "bsd,bse->de", normed_low, back_joint, preferred_element_type=jnp.float32
    )
    bias_query = column_sum(back_joint[:, :, :D])
    bias_value = column_sum(back_joint[:, :, 2 * D :])
    back_normed = jnp.einsum(
        "bse,de->bsd", back_joint, joint_weight, preferred_element_type=jnp.float32
    )
    back_start, gain_one, shift_one = pull_first(back_normed)
    back_start = back_start + back_middle
    back_rows = jnp.einsum(
        "con,col->cnl",
        select_rows.astype(jnp.float32),
        back_start,
        precision=lax.Precision.HIGHEST,
        preferred_element_type=jnp.float32,
    )
    token_grad = jnp.sum(mask_token_rows * back_start, axis=(0, 1))
    embedded_gradient = lax.psum_scatter(
        back_rows.astype(jnp.bfloat16), "blk", scatter_dimension=1, tiled=True
    )
    grad_embed = jnp.einsum(
        "moy,moa->ya", encoder_rows, embedded_gradient, preferred_element_type=jnp.float32
    )
    bias_embed = column_sum(embedded_gradient)
    latent_grad = jnp.einsum(
        "ntp,jp->ntj", embedded_gradient, embedding_matrix, preferred_element_type=jnp.float32
    )
    vector_grad = jnp.concatenate(
        [
            jnp.stack(
                [
                    bias_embed,
                    token_grad,
                    gain_one,
                    shift_one,
                    bias_query,
                    bias_value,
                    bias_output,
                    gain_two,
                    shift_two,
                    bias_reduce,
                ]
            ),
            bias_expand.reshape(4, D),
        ],
        axis=0,
    )
    matrix_grad = jnp.concatenate(
        [
            grad_embed.reshape(-1),
            grad_joint.reshape(-1),
            grad_output.reshape(-1),
            grad_expand.reshape(-1),
            grad_reduce.reshape(-1),
        ]
    )
    return (result, latent_grad, matrix_grad, vector_grad)


def local(
    latents,
    restore,
    bucket,
    cotangent,
    flat_weights,
    flat_first,
    flat_second,
    vectors,
    vector_first,
    vector_second,
):
    gathered = lax.all_gather(flat_weights.astype(jnp.bfloat16), ("dp", "blk"), axis=0, tiled=True)
    weights = unpack(gathered)
    side = lax.axis_index("blk")
    lengths = image_lengths(bucket)
    per_batch = restore.shape[0] // MB
    results = []
    latent_grads = []
    vector_total = jnp.zeros(vectors.shape, jnp.float32)
    matrix_total = jnp.zeros((NPARAM,), jnp.float32)
    for micro in range(MB):
        first_image = micro * per_batch
        picked = slice(first_image, first_image + per_batch)
        result, latent_grad, matrix_grad, vector_grad = one_batch(
            weights,
            vectors,
            latents[picked],
            restore[picked],
            lengths[picked],
            cotangent[picked],
            side,
        )
        results.append(result)
        latent_grads.append(latent_grad)
        vector_total = vector_total + vector_grad
        matrix_total = matrix_total + matrix_grad
    shard_grad = lax.psum_scatter(matrix_total, ("dp", "blk"), scatter_dimension=0, tiled=True)
    vector_sum, square_sum = lax.psum(
        (vector_total, jnp.sum(shard_grad * shard_grad)), ("dp", "blk")
    )
    grad_norm = jnp.sqrt(square_sum + jnp.sum(vector_sum * vector_sum))
    factor = jnp.minimum(1.0, clip_norm / (grad_norm + 1e-06))
    new_first, new_second, new_weights = adam_update(
        shard_grad * factor, flat_first, flat_second, flat_weights, learn_rate, decay_weight
    )
    vector_first_new, vector_second_new, vectors_new = adam_update(
        vector_sum * factor, vector_first, vector_second, vectors, vector_rate, 0.0
    )
    reduce_bias_grad = vector_sum[9] * factor
    block_out = jnp.concatenate(results, axis=0)
    latent_out = jnp.concatenate(latent_grads, axis=0)
    return (
        block_out,
        latent_out,
        new_first,
        new_second,
        new_weights,
        vector_first_new,
        vector_second_new,
        vectors_new,
        reduce_bias_grad,
        grad_norm,
    )


def solution(mesh):
    return jax.shard_map(
        local,
        mesh=mesh,
        in_specs=(
            P("dp", "blk", None),
            P("dp", "blk"),
            P("dp"),
            P("dp", "blk", None),
            P(("dp", "blk")),
            P(("dp", "blk")),
            P(("dp", "blk")),
            P(),
            P(),
            P(),
        ),
        out_specs=(
            P("dp", "blk", None),
            P("dp", "blk", None),
            P(("dp", "blk")),
            P(("dp", "blk")),
            P(("dp", "blk")),
            P(),
            P(),
            P(),
            P(),
            P(),
        ),
        check_vma=False,
    )
```

profile of v0, /device:TPU:0, one launch (start us, length us, event | category | flops | bytes accessed | tf_op | source)
XLA Modules:
  0.0 727.7 jit_solution(2196091158819557888)
XLA Ops:
  18.0 68.9 %all-gather.4.cloned.1.call-done = bf16[3538944]{0:T(1024)(128)(2,1)} async-done(((bf16[110592]{0:T(1024)(128)(2,1)}), bf16[3538944]{0:T(1024)(128)(2,1)}) %all-gather.4.cloned.1.call-update) | async-done | bytes 7077904 | tf_op jit(solution)/shard_map/all_gather | solution.py:268
  88.8 5.1 all_gather.18
  100.5 4.9 all_gather.16
  105.5 4.9 fusion.131
  114.7 4.2 reshape.445
  118.9 4.4 reshape.446
  128.8 4.6 fusion.138
  137.9 6.3 all-gather.6.cloned.1.call-done
  149.9 4.6 fusion.141
  162.0 5.7 multiply_convert_fusion.2
  169.8 5.5 multiply_convert_fusion.3
  183.9 3.9 convolution_convert_fusion.1
  192.6 29.6 %fusion.51 = bf16[2,16,32,256]{3,2,1,0:T(8,128)(2,1)} fusion(bf16[2,128,16,32]{1,3,2,0:T(8,128)(2,1)} %bitcast.205, f32[2,16,128,256]{3,2,1,0:T(8,128)} %fusion.147, f32[2,16,128,256]{3,2,1,0:T(8,128)} %get-tuple-element.103, f32[2,16,128]{2,1,0:T(8,128)S(1)} %copy-done.86), kind=kOutput, calls=%fused_computation.92 | convolution fusion | flops 74715392 | bytes 9191424 | tf_op jit(solution)/shard_map/bhqk,bqhe->bkhe/dot_general | solution.py:185
  230.9 4.3 convolution_convert_fusion
  237.2 3.7 fusion.150
  240.9 29.6 %fusion.48 = bf16[2,16,32,256]{3,2,1,0:T(8,128)(2,1)} fusion(bf16[2,128,16,32]{1,3,2,0:T(8,128)(2,1)} %bitcast.203, f32[2,16,128,256]{3,2,1,0:T(8,128)} %fusion.150, f32[2,16,128,256]{3,2,1,0:T(8,128)} %get-tuple-element.96, f32[2,16,128]{2,1,0:T(8,128)S(1)} %copy-done.84), kind=kOutput, calls=%fused_computation.91 | convolution fusion | flops 74715392 | bytes 9191424 | tf_op jit(solution)/shard_map/bhqk,bqhe->bkhe/dot_general | solution.py:185
  275.0 29.1 %convert_reduce_fusion.9 = (f32[16,32]{1,0:T(8,128)S(1)}, bf16[2,16,32,128]{3,2,1,0:T(8,128)(2,1)S(1)}) fusion(bf16[2,256,16,32]{1,3,2,0:T(8,128)(2,1)} %bitcast.197, f32[2,16,128,256]{3,2,1,0:T(8,128)} %fusion.147, f32[2,16,128,256]{3,2,1,0:T(8,128)} %get-tuple-element.103, f32[2,16,128]{2,1,0:T(8,128)} %copy-done.85), kind=kOutput, calls=%fused_computation.144 | convolution fusion | flops 74845952 | bytes 9193472 | tf_op jit(solution)/shard_map/bhqk,bkhe->bqhe/dot_general | solution.py:182
  305.0 29.5 %convert_reduce_fusion.5 = (f32[16,32]{1,0:T(8,128)S(1)}, bf16[2,16,32,128]{3,2,1,0:T(8,128)(2,1)}) fusion(bf16[2,256,16,32]{1,3,2,0:T(8,128)(2,1)} %bitcast.195, f32[2,16,128,256]{3,2,1,0:T(8,128)} %fusion.150, f32[2,16,128,256]{3,2,1,0:T(8,128)} %get-tuple-element.96, f32[2,16,128]{2,1,0:T(8,128)} %copy-done.83), kind=kOutput, calls=%fused_computation.137 | convolution fusion | flops 74845952 | bytes 9193472 | tf_op jit(solution)/shard_map/bhqk,bkhe->bqhe/dot_general | solution.py:182
  370.5 4.3 reshape.431
  374.9 4.4 reshape.436
  414.9 3.7 copy-done
  418.6 5.5 add.316
  431.3 239.6 %all-reduce.4.cloned.1.call-done = f32[3538944]{0:T(1024)} async-done(((f32[3538944]{0:T(1024)}), f32[3538944]{0:T(1024)}) %all-reduce.4.cloned.1.call-update) | async-done | bytes 14155792
  673.4 40.5 %all-reduce.1 = (f32[]{:T(128)}, f32[14,512]{1,0:T(8,128)S(1)}) all-reduce(f32[]{:T(128)} %multiply_reduce_fusion.16, f32[14,512]{1,0:T(8,128)S(1)} %add.317), channel_id=1, replica_groups=mesh['dp'=16,'blk'=2] {'dp','blk'}, use_global_device_ids=true, to_apply=%region_28.29 | all-reduce | flops 7169 | bytes 57352 | tf_op jit(solution)/shard_map/psum | solution.py:294
  (342 shorter events, 162.9 us)
Async XLA Ops:
  7.2 79.7 %all-gather.4.cloned.1.call-start = ((), (), s32[]{:S(2)}) async-start(), calls=%async_computation.4 | async-start | bytes 7299072 | tf_op jit(solution)/shard_map/all_gather | solution.py:268
  8.9 79.5 %copy-start.36 = (bf16[4,32,768]{2,1,0:T(8,128)(2,1)S(1)}, bf16[4,32,768]{2,1,0:T(8,128)(2,1)}, u32[]{:S(2)}) copy-start(bf16[4,32,768]{2,1,0:T(8,128)(2,1)} %param.10) | copy-start | bytes 589828
  9.0 115.4 %all-gather.8.cloned.1.call-start = ((), (), s32[]{:S(2)}) async-start(), calls=%async_computation.6 | async-start | bytes 1572864 | tf_op jit(solution)/shard_map/all_gather | solution.py:107
  12.0 76.5 %copy-start.65 = (f32[1,512]{1,0:T(1,128)}, f32[1,512]{1,0:T(1,128)S(1)}, u32[]{:S(2)}) copy-start(f32[1,512]{1,0:T(1,128)S(1)} %get-tuple-element.73) | copy-start | bytes 6148
  13.2 83.3 %copy-start.20 = (f32[128,512]{1,0:T(8,128)}, f32[128,512]{1,0:T(8,128)S(1)}, u32[]{:S(2)}) copy-start(f32[128,512]{1,0:T(8,128)S(1)} %pad_maximum_fusion.10) | copy-start | bytes 786436
  99.2 11.3 %copy-start.49 = (bf16[2,128,1536]{2,1,0:T(8,128)(2,1)}, bf16[2,128,1536]{2,1,0:T(8,128)(2,1)S(1)}, u32[]{:S(2)}) copy-start(bf16[2,128,1536]{2,1,0:T(8,128)(2,1)S(1)} %fusion.13) | copy-start | bytes 2359300
  100.5 43.7 %all-gather.6.cloned.1.call-start = ((), (), s32[]{:S(2)}) async-start(), calls=%async_computation.5 | async-start | bytes 1572864 | tf_op jit(solution)/shard_map/all_gather | solution.py:107
  124.2 231.0 %reduce-scatter.5.cloned.1.call-start = ((), (), s32[]{:S(2)}) async-start(), calls=%async_computation.7 | async-start | bytes 1572864 | tf_op jit(solution)/shard_map/reduce_scatter | solution.py:192
  137.9 12.0 %copy-start.81 = (pred[2,256]{1,0:T(4,128)(4,1)S(1)}, pred[2,256]{1,0:T(4,128)(4,1)}, u32[]{:S(2)}) copy-start(pred[2,256]{1,0:T(4,128)(4,1)} %get-tuple-element.121) | copy-start | bytes 1540
  147.7 6.8 copy-start.28
  224.3 6.6 copy-start.84
  226.6 131.6 %reduce-scatter.9.cloned.1.call-start = ((), (), s32[]{:S(2)}) async-start(), calls=%async_computation.9 | async-start | bytes 1572864 | tf_op jit(solution)/shard_map/reduce_scatter | solution.py:192
  240.9 31.7 %copy-start.33 = (bf16[2,256,512]{2,1,0:T(8,128)(2,1)S(1)}, bf16[2,256,512]{2,1,0:T(8,128)(2,1)}, u32[]{:S(2)}) copy-start(bf16[2,256,512]{2,1,0:T(8,128)(2,1)} %copy.88) | copy-start | bytes 1572868
  274.8 105.8 %reduce-scatter.7.cloned.1.call-start = ((), (), s32[]{:S(2)}) async-start(), calls=%async_computation.8 | async-start | bytes 196608 | tf_op jit(solution)/shard_map/reduce_scatter | solution.py:214
  305.0 31.3 %copy-start.24 = (bf16[2,128,512]{2,1,0:T(8,128)(2,1)S(1)}, bf16[2,128,512]{2,1,0:T(8,128)(2,1)}, u32[]{:S(2)}) copy-start(bf16[2,128,512]{2,1,0:T(8,128)(2,1)} %copy-done.23) | copy-start | bytes 786436
  305.0 31.3 %copy-start.54 = (bf16[2,16,32,128]{3,2,1,0:T(8,128)(2,1)S(1)}, bf16[2,16,32,128]{3,2,1,0:T(8,128)(2,1)}, u32[]{:S(2)}) copy-start(bf16[2,16,32,128]{3,2,1,0:T(8,128)(2,1)} %copy-done.53) | copy-start | bytes 786436
  364.5 25.8 %reduce-scatter.11.cloned.1.call-start = ((), (), s32[]{:S(2)}) async-start(), calls=%async_computation.10 | async-start | bytes 196608 | tf_op jit(solution)/shard_map/reduce_scatter | solution.py:214
  380.3 290.6 %all-reduce.4.cloned.1.call-start = ((), (), s32[]{:S(2)}) async-start(), calls=%async_computation.11 | async-start | bytes 28311552
  430.2 286.3 %copy-start.60 = (f32[14,512]{1,0:T(8,128)S(1)}, f32[14,512]{1,0:T(8,128)}, u32[]{:S(2)}) copy-start(f32[14,512]{1,0:T(8,128)} %param.17) | copy-start | bytes 86020
  430.2 286.3 %copy-start.61 = (f32[14,512]{1,0:T(8,128)S(1)}, f32[14,512]{1,0:T(8,128)}, u32[]{:S(2)}) copy-start(f32[14,512]{1,0:T(8,128)} %param.19) | copy-start | bytes 86020
  430.2 286.3 %copy-start.62 = (f32[14,512]{1,0:T(8,128)S(1)}, f32[14,512]{1,0:T(8,128)}, u32[]{:S(2)}) copy-start(f32[14,512]{1,0:T(8,128)} %param.18) | copy-start | bytes 86020
  430.2 287.0 %copy-start.34 = (f32[110592]{0:T(1024)S(1)}, f32[110592]{0:T(1024)}, u32[]{:S(2)}) copy-start(f32[110592]{0:T(1024)} %param.14) | copy-start | bytes 1327108
  430.2 287.0 %copy-start.58 = (f32[110592]{0:T(1024)S(1)}, f32[110592]{0:T(1024)}, u32[]{:S(2)}) copy-start(f32[110592]{0:T(1024)} %param.16) | copy-start | bytes 1327108
  430.2 287.0 %copy-start.59 = (f32[110592]{0:T(1024)S(1)}, f32[110592]{0:T(1024)}, u32[]{:S(2)}) copy-start(f32[110592]{0:T(1024)} %param.15) | copy-start | bytes 1327108
  (76 other events, 240.2 us)
Sparse Core Ops, SparseCore 0:
  11.5 75.3 all-gather.3
  100.6 19.8 all-gather.7
  124.3 19.8 all-gather.5
  226.7 20.3 reduce-scatter.4
  274.9 20.1 reduce-scatter.8
  364.6 9.8 reduce-scatter.6
  380.4 9.8 reduce-scatter.10
  424.2 246.6 all-reduce.3
where the time goes:
time: 735 us; the launch traced here: 728 us
  waiting for transfers between devices  316 us (43%)
  matrix products  190 us (26%)
  local copies, waits for them, and re-layouts  113 us (15%)
  blocking collectives  50.6 us (7%)
  other arithmetic  39.5 us (5%)
  between operations  17.8 us (2%)
    unnamed x9, waiting for transfers between devices  240 us
    all_gather x1, waiting for transfers between devices, local(): lax.all_gather(flat_weights.astype(jnp.bfloat16), ('dp', 'blk'), axis=0,...  68.9 us
    dot_general x2, matrix products, one_batch(): jnp.einsum('bhqk,bqhe->bkhe', back_scores_low, query, preferred_element_t...  59.2 us
    dot_general x2, matrix products, one_batch(): jnp.einsum('bhqk,bkhe->bqhe', back_scores_low, keys, preferred_element_ty...  58.7 us
    unnamed x192, local copies, waits for them, and re-layouts  45.4 us
    psum x1, blocking collectives, local(): lax.psum((vector_total, jnp.sum(shard_grad * shard_grad)), ('dp', 'blk'))  40.5 us
    slice x12, local copies, waits for them, and re-layouts, unpack(): pieces.append(flat[offset:offset + height * width].reshape(height, width))  18.1 us
  transfers between devices with their start and end apart: 8, of which 4 were waited for; matrix products, arithmetic and copies ran while one was open for 27% of the time, Pallas kernels for 0%

commit v1 on v0

v1 whole, which is shorter than its diff:
```python
import math

import jax
import jax.numpy as jnp
from jax import lax
from jax.experimental import pallas as pl
from jax.experimental.pallas import tpu as pltpu
from jax.sharding import PartitionSpec as P

DIN = 768
D = 512
HEADS = 16
HD = 32
FF = 2048
SLOTS = 256
KMAX = 64
STEP = 10
NPARAM = 3538944

first_decay = 0.9
second_decay = 0.95
learn_rate = 0.05
vector_rate = 0.5
decay_weight = 0.05
adam_eps = 1e-08
clip_norm = 1.0

BF = jnp.bfloat16
F32 = jnp.float32

LANES = 128
LINES = NPARAM // LANES
EMBED_AT = 0
JOINT_AT = EMBED_AT + DIN * D // LANES
OUTPUT_AT = JOINT_AT + 3 * D * D // LANES
EXPAND_AT = OUTPUT_AT + D * D // LANES
REDUCE_AT = EXPAND_AT + D * FF // LANES
BLOCK = LINES // 32
HALF = 16 * BLOCK
FIRST_BLOCKS = -(-EXPAND_AT // BLOCK)
SECOND_FROM = EXPAND_AT // BLOCK
SECOND_BLOCKS = 32 - SECOND_FROM
TILE = 256
TILES = FF // TILE
GROUP = 4
GROUPS = HEADS // GROUP
MINE = 2
TOKENS = MINE * SLOTS
VMEM = pl.BlockSpec(memory_space=pltpu.VMEM)
SMEM = pl.BlockSpec(memory_space=pltpu.SMEM)
ANY = pl.BlockSpec(memory_space=pl.ANY)


def image_lengths(bucket):
    return jnp.where(
        bucket == 0, SLOTS * 100 // 256, jnp.where(bucket == 1, SLOTS * 196 // 256, SLOTS)
    ).astype(jnp.int32)


def position_rows(slot):
    column = jnp.arange(D // 2, dtype=jnp.int32).astype(F32)[None, :]
    angle = slot.astype(F32)[:, None] * jnp.exp(-math.log(10000.0) * column / (D // 2))
    return jnp.concatenate([jnp.sin(angle), jnp.cos(angle)], axis=1)


def adam_update(grad, first, second, weight, rate, shrink):
    first_new = first_decay * first + (1.0 - first_decay) * grad
    second_new = second_decay * second + (1.0 - second_decay) * grad * grad
    first_hat = first_new / (1.0 - first_decay**STEP)
    second_hat = second_new / (1.0 - second_decay**STEP)
    weight_new = weight - rate * (first_hat / (jnp.sqrt(second_hat) + adam_eps) + shrink * weight)
    return (first_new, second_new, weight_new)


def dot(left, right, over=(1, 0)):
    return lax.dot_general(
        left, right, (((over[0],), (over[1],)), ((), ())), preferred_element_type=F32
    )


def fetch_lines(table, pieces, lines, sem, low, high):
    span = pieces[0].shape[0]
    if len(pieces) == 1:
        pltpu.make_async_copy(
            pieces[0].at[pl.ds(low * BLOCK, (high - low) * BLOCK)], lines, sem
        ).start()
        return
    for index, piece in enumerate(pieces):
        block = table[index]

        @pl.when((block >= low) & (block < high))
        def _(piece=piece, block=block):
            at = pl.multiple_of((block - low) * span, 16)
            pltpu.make_async_copy(piece, lines.at[pl.ds(at, span)], sem).start()


def wait_lines(lines, sem):
    pltpu.make_async_copy(lines, lines, sem).wait()


def lines_to_matrix(lines, stage, matrix, at, rows, wide, batch):
    size = batch * wide

    def body(index, carry):
        for part in range(2):
            row = pl.multiple_of((2 * index + part) * batch, batch)
            source = pl.multiple_of(at + (2 * index + part) * size, 16)
            stage[part, :size, :] = lines[pl.ds(source, size), :].astype(F32)
            for j in range(wide):
                matrix[pl.ds(row, batch), j * LANES : (j + 1) * LANES] = stage[
                    part, pl.ds(j, batch, stride=wide), :
                ].astype(BF)
        return carry

    lax.fori_loop(0, rows // batch // 2, body, 0)


def norm_parts(value):
    centred = value - jnp.mean(value, axis=-1, keepdims=True)
    scale = lax.rsqrt(jnp.mean(centred * centred, axis=-1, keepdims=True) + 1e-06)
    return centred * scale, scale


def norm_back(grad, hat, scale, gain):
    inner = grad * gain
    return scale * (
        inner
        - jnp.mean(inner, axis=-1, keepdims=True)
        - hat * jnp.mean(inner * hat, axis=-1, keepdims=True)
    )


def total(value):
    return jnp.sum(value.astype(F32), axis=0, keepdims=True)


def slot_column(side):
    local = lax.broadcasted_iota(jnp.int32, (SLOTS, 1), 0)
    return (local + side * (SLOTS // 2)) & (SLOTS - 1)


def select_rows(restore, side):
    rows = (lax.broadcasted_iota(jnp.int32, (1, KMAX), 1) + side * (KMAX // 2)) & (KMAX - 1)
    return (restore == rows).astype(F32).astype(BF)


def head_mask(head):
    lane = lax.broadcasted_iota(jnp.int32, (1, LANES), 1)
    return (lane // HD) == head


def mask_head(value, head):
    return jnp.where(head_mask(head), value, jnp.zeros_like(value))


def forward_kernel(
    meta, table, latents, restore, position, vectors, *rest, pieces
):
    sources = rest[:pieces]
    (
        probs,
        joint,
        normed,
        start,
        middle,
        mixed,
        embed_w,
        joint_w,
        output_w,
        lines,
        stage,
        query_t,
        value_t,
        mixed_t,
        sem,
    ) = rest[pieces:]
    step = pl.program_id(0)
    side = meta[0]

    @pl.when(step == 0)
    def _():
        fetch_lines(table, sources, lines, sem, 0, FIRST_BLOCKS)
        wait_lines(lines, sem)
        lines_to_matrix(lines, stage, embed_w, EMBED_AT, DIN, 4, 128)
        lines_to_matrix(lines, stage, joint_w, JOINT_AT, D, 12, 64)
        lines_to_matrix(lines, stage, output_w, OUTPUT_AT, D, 4, 128)
        embedded = (dot(latents[...], embed_w[...]) + vectors[0:1, :]).astype(BF)
        for image in range(MINE):
            rows = slice(image * SLOTS, (image + 1) * SLOTS)
            picked = restore[rows, :]
            chosen = dot(
                select_rows(picked, side), embedded[image * KMAX : (image + 1) * KMAX, :]
            )
            value = (
                chosen + (picked >= KMAX).astype(F32) * vectors[1:2, :] + position[...]
            )
            start[rows, :] = value
            hat, _ = norm_parts(value)
            normed[rows, :] = (hat * vectors[2:3, :] + vectors[3:4, :]).astype(BF)
        for part, bias in enumerate((4, None, 5)):
            columns = slice(part * D, (part + 1) * D)
            out = dot(normed[...], joint_w[:, columns])
            if bias is not None:
                out = out + vectors[bias : bias + 1, :]
            joint[:, columns] = out.astype(BF)
        query_t[...] = joint[:, :D].T
        value_t[...] = joint[:, 2 * D :].T

    image = step // GROUPS
    group = step % GROUPS
    rows = pl.ds(pl.multiple_of(image * SLOTS, SLOTS), SLOTS)
    lanes = pl.ds(pl.multiple_of(group * LANES, LANES), LANES)
    keys = joint[rows, pl.ds(pl.multiple_of(D + group * LANES, LANES), LANES)]
    queries = query_t[lanes, rows]
    hidden_key = jnp.where(slot_column(side) < meta[1 + image], 0.0, -1e30)
    rate = HD**-0.5 * math.log2(math.e)
    for head in range(GROUP):
        scores = dot(mask_head(keys, head), queries) + hidden_key
        top = jnp.max(scores, axis=0, keepdims=True)
        raised = jnp.exp2((scores - top) * rate)
        low = (raised * (1.0 / jnp.sum(raised, axis=0, keepdims=True))).astype(BF)
        probs[head] = low
        features = pl.ds(pl.multiple_of(group * LANES + head * HD, HD), HD)
        mixed_t[features, rows] = dot(value_t[features, rows], low).astype(BF)

    @pl.when(step == MINE * GROUPS - 1)
    def _():
        mixed[...] = mixed_t[...].T
        middle[...] = start[...] + dot(mixed[...], output_w[...]) + vectors[6:7, :]


def forward_call(meta, table, latents, restore, position, vectors, sources):
    shape = jax.ShapeDtypeStruct
    count = len(sources)
    whole = lambda *dims: pl.BlockSpec(dims, lambda i: (0,) * len(dims))
    return pl.pallas_call(
        lambda *refs: forward_kernel(*refs, pieces=count),
        grid=(MINE * GROUPS,),
        in_specs=[SMEM, SMEM, VMEM, VMEM, VMEM, VMEM] + [ANY] * count,
        out_shape=(
            shape((MINE * HEADS, SLOTS, SLOTS), BF),
            shape((TOKENS, 3 * D), BF),
            shape((TOKENS, D), BF),
            shape((TOKENS, D), F32),
            shape((TOKENS, D), F32),
            shape((TOKENS, D), BF),
            shape((DIN, D), BF),
            shape((D, 3 * D), BF),
            shape((D, D), BF),
        ),
        out_specs=(
            pl.BlockSpec((GROUP, SLOTS, SLOTS), lambda i: (i, 0, 0)),
            whole(TOKENS, 3 * D),
            whole(TOKENS, D),
            whole(TOKENS, D),
            whole(TOKENS, D),
            whole(TOKENS, D),
            whole(DIN, D),
            whole(D, 3 * D),
            whole(D, D),
        ),
        scratch_shapes=[
            pltpu.VMEM((FIRST_BLOCKS * BLOCK, LANES), BF),
            pltpu.VMEM((2, 768, LANES), F32),
            pltpu.VMEM((D, TOKENS), BF),
            pltpu.VMEM((D, TOKENS), BF),
            pltpu.VMEM((D, TOKENS), BF),
            pltpu.SemaphoreType.DMA,
        ],
        compiler_params=pltpu.CompilerParams(vmem_limit_bytes=56 * 2**20),
        cost_estimate=pl.CostEstimate(
            flops=6 * 10**9, bytes_accessed=16 * 2**20, transcendentals=2 * 10**6
        ),
    )(meta, table, latents, restore, position, vectors, *sources)


def middle_kernel(meta, table, slots, middle, mixed, cotangent, output_w, vectors, *rest, pieces):
    sources = rest[:pieces]
    (
        own_out,
        far_out,
        back_middle,
        back_mixed,
        low_lines,
        far_lines,
        near_lines,
        rows_out,
        expand_out,
        lines,
        stage,
        expand_w,
        reduce_w,
        hat,
        scale,
        normed,
        normed_t,
        back_out,
        acc,
        acc_back,
        grads,
        out_grads,
        sem,
    ) = rest[pieces:]
    step = pl.program_id(0)
    side = meta[0]
    base = SECOND_FROM * BLOCK

    @pl.when(step == 0)
    def _():
        fetch_lines(table, sources, lines, sem, SECOND_FROM, 32)
        value, spread = norm_parts(middle[...])
        hat[...] = value
        scale[...] = spread
        normed[...] = (value * vectors[7:8, :] + vectors[8:9, :]).astype(BF)
        normed_t[...] = normed[...].T
        for image in range(MINE):
            rows = slice(image * SLOTS, (image + 1) * SLOTS)
            valid = slot_column(side) < meta[1 + image]
            back_out[rows, :] = jnp.where(valid, cotangent[rows, :].astype(F32), 0.0).astype(BF)
        acc[...] = jnp.zeros_like(acc)
        acc_back[...] = jnp.zeros_like(acc_back)
        wait_lines(lines, sem)
        lines_to_matrix(lines, stage, expand_w, EXPAND_AT - base, D, 16, 32)
        lines_to_matrix(lines, stage, reduce_w, REDUCE_AT - base, FF, 4, 128)

    columns = pl.ds(pl.multiple_of(step * TILE, TILE), TILE)
    expand = expand_w[:, columns]
    reduce = reduce_w[columns, :]
    bias = jnp.concatenate(
        [
            vectors[pl.ds(10 + step // 2, 1), pl.ds(pl.multiple_of((step % 2) * TILE, TILE), TILE)]
        ],
        axis=1,
    )
    hidden = dot(normed[...], expand) + bias
    density = jnp.exp(hidden * hidden * -0.5) * (1.0 / math.sqrt(2.0 * math.pi))
    below = 0.5 + 0.5 * lax.erf(hidden * math.sqrt(0.5))
    active = (hidden * below).astype(BF)
    back_active = dot(back_out[...], reduce, (1, 1))
    back_hidden = (back_active * (below + hidden * density)).astype(BF)
    acc[...] += dot(active, reduce)
    acc_back[...] += dot(back_hidden, expand, (1, 1))
    grad_reduce = dot(active, back_out[...], (0, 0))
    for j in range(4):
        grads[pl.ds(D * 16 + step * (TILE * 4) + j, TILE, stride=4), :] = grad_reduce[
            :, j * LANES : (j + 1) * LANES
        ]
    grad_expand = dot(normed_t[...], back_hidden)
    for j in range(TILE // LANES):
        grads[pl.ds(step * (TILE // LANES) + j, D, stride=16), :] = grad_expand[
            :, j * LANES : (j + 1) * LANES
        ]
    expand_out[pl.ds(step, 1), :] = total(back_hidden)

    @pl.when(step == TILES - 1)
    def _():
        for image in range(MINE):
            near = slice(image * SLOTS, image * SLOTS + SLOTS // 2)
            far = slice(image * SLOTS + SLOTS // 2, (image + 1) * SLOTS)
            own_out[image] = middle[near, :] + acc[near, :] + vectors[9:10, :]
            far_out[image] = (middle[far, :] + acc[far, :] + vectors[9:10, :]).astype(BF)
        grad = acc_back[...]
        rows_out[...] = jnp.zeros_like(rows_out)
        rows_out[1:2, :] = total(grad * hat[...])
        rows_out[2:3, :] = total(grad)
        rows_out[3:4, :] = total(back_out[...])
        back = back_out[...].astype(F32) + norm_back(grad, hat[...], scale[...], vectors[7:8, :])
        back_middle[...] = back
        branch = back.astype(BF)
        rows_out[0:1, :] = total(branch)
        back_mixed[...] = dot(branch, output_w[...], (1, 1)).astype(BF)
        grad_output = dot(mixed[...], branch, (0, 0))
        for j in range(4):
            out_grads[pl.ds(j, D, stride=4), :] = grad_output[:, j * LANES : (j + 1) * LANES]
        head = EXPAND_AT - OUTPUT_AT
        low_lines[:head, :] = out_grads[...].astype(BF)
        low_lines[head:, :] = grads[: HALF - EXPAND_AT, :].astype(BF)
        put_blocks(slots, far_lines, near_lines, lambda q: grads[pl.ds(HALF - EXPAND_AT + q * BLOCK, BLOCK), :].astype(BF))


def put_blocks(slots, far_lines, near_lines, block_of):
    def body(index, carry):
        slot = slots[index]
        value = block_of(index)

        @pl.when(slot < 8)
        def _():
            far_lines[pl.ds(pl.multiple_of(slot * BLOCK, 16), BLOCK), :] = value

        @pl.when(slot >= 8)
        def _():
            near_lines[pl.ds(pl.multiple_of((slot - 8) * BLOCK, 16), BLOCK), :] = value

        return carry

    lax.fori_loop(0, 16, body, 0)


def middle_call(meta, table, slots, middle, mixed, cotangent, output_w, vectors, sources):
    shape = jax.ShapeDtypeStruct
    count = len(sources)
    outs = (
        shape((MINE, SLOTS // 2, D), F32),
        shape((MINE, SLOTS // 2, D), BF),
        shape((TOKENS, D), F32),
        shape((TOKENS, D), BF),
        shape((HALF - OUTPUT_AT, LANES), BF),
        shape((8 * BLOCK, LANES), BF),
        shape((8 * BLOCK, LANES), BF),
        shape((8, D), F32),
        shape((TILES, TILE), F32),
    )
    return pl.pallas_call(
        lambda *refs: middle_kernel(*refs, pieces=count),
        grid=(TILES,),
        in_specs=[SMEM, SMEM, SMEM] + [VMEM] * 5 + [ANY] * count,
        out_shape=outs,
        out_specs=tuple(VMEM for _ in outs),
        scratch_shapes=[
            pltpu.VMEM((SECOND_BLOCKS * BLOCK, LANES), BF),
            pltpu.VMEM((2, 768, LANES), F32),
            pltpu.VMEM((D, FF), BF),
            pltpu.VMEM((FF, D), BF),
            pltpu.VMEM((TOKENS, D), F32),
            pltpu.VMEM((TOKENS, 1), F32),
            pltpu.VMEM((TOKENS, D), BF),
            pltpu.VMEM((D, TOKENS), BF),
            pltpu.VMEM((TOKENS, D), BF),
            pltpu.VMEM((TOKENS, D), F32),
            pltpu.VMEM((TOKENS, D), F32),
            pltpu.VMEM((2 * D * 16, LANES), F32),
            pltpu.VMEM((D * 4, LANES), F32),
            pltpu.SemaphoreType.DMA,
        ],
        compiler_params=pltpu.CompilerParams(vmem_limit_bytes=56 * 2**20),
        cost_estimate=pl.CostEstimate(
            flops=8 * 10**9, bytes_accessed=16 * 2**20, transcendentals=2 * 10**6
        ),
    )(meta, table, slots, middle, mixed, cotangent, output_w, vectors, *sources)


def backward_kernel(
    meta,
    slots,
    probs,
    joint,
    normed,
    start,
    back_middle,
    back_mixed,
    latents,
    restore,
    vectors,
    embed_w,
    joint_w,
    low_lines,
    far_lines,
    near_lines,
    rows_out,
    own_latent,
    far_latent,
    key_t,
    back_t,
    query_back_t,
    joint_back,
    grads,
):
    step = pl.program_id(0)
    side = meta[0]

    @pl.when(step == 0)
    def _():
        key_t[...] = joint[:, D : 2 * D].T
        back_t[...] = back_mixed[...].T

    image = step // GROUPS
    group = step % GROUPS
    rows = pl.ds(pl.multiple_of(image * SLOTS, SLOTS), SLOTS)
    lanes = pl.ds(pl.multiple_of(group * LANES, LANES), LANES)
    queries = joint[rows, lanes]
    values = joint[rows, pl.ds(pl.multiple_of(2 * D + group * LANES, LANES), LANES)]
    back = back_mixed[rows, lanes]
    back_lanes = back_t[lanes, rows]
    key_back = jnp.zeros((SLOTS, LANES), F32)
    value_back = jnp.zeros((SLOTS, LANES), F32)
    for head in range(GROUP):
        low = probs[head]
        wide = low.astype(F32)
        back_probs = dot(mask_head(values, head), back_lanes)
        pull = jnp.sum(wide * back_probs, axis=0, keepdims=True)
        score_back = (wide * (back_probs - pull) * HD**-0.5).astype(BF)
        value_back = value_back + dot(low, mask_head(back, head))
        key_back = key_back + dot(score_back, mask_head(queries, head))
        features = pl.ds(pl.multiple_of(group * LANES + head * HD, HD), HD)
        query_back_t[features, rows] = dot(key_t[features, rows], score_back).astype(BF)
    joint_back[rows, pl.ds(pl.multiple_of(D + group * LANES, LANES), LANES)] = key_back.astype(BF)
    joint_back[rows, pl.ds(pl.multiple_of(2 * D + group * LANES, LANES), LANES)] = (
        value_back.astype(BF)
    )

    @pl.when(step == MINE * GROUPS - 1)
    def _():
        joint_back[:, :D] = query_back_t[...].T
        rows_out[...] = jnp.zeros_like(rows_out)
        rows_out[4:5, :] = total(joint_back[:, :D])
        rows_out[5:6, :] = total(joint_back[:, 2 * D :])
        normed_t = normed[...].T
        for part in range(3):
            grad_joint = dot(normed_t, joint_back[:, part * D : (part + 1) * D])
            for j in range(4):
                grads[pl.ds(JOINT_AT + part * 4 + j, D, stride=12), :] = grad_joint[
                    :, j * LANES : (j + 1) * LANES
                ]
        grad = dot(joint_back[...], joint_w[...], (1, 1))
        hat, scale = norm_parts(start[...])
        rows_out[2:3, :] = total(grad * hat)
        rows_out[3:4, :] = total(grad)
        back_start = back_middle[...] + norm_back(grad, hat, scale, vectors[2:3, :])
        masked = (restore[...] >= KMAX).astype(F32)
        rows_out[1:2, :] = total(masked * back_start)
        low_start = back_start.astype(BF)
        picked = []
        for image_at in range(MINE):
            part = slice(image_at * SLOTS, (image_at + 1) * SLOTS)
            picked.append(
                dot(select_rows(restore[part, :], side), low_start[part, :], (0, 0)).astype(BF)
            )
        embedded_back = jnp.concatenate(picked, axis=0)
        rows_out[0:1, :] = total(embedded_back)
        grad_embed = dot(latents[...], embedded_back, (0, 0))
        for j in range(4):
            grads[pl.ds(EMBED_AT + j, DIN, stride=4), :] = grad_embed[:, j * LANES : (j + 1) * LANES]
        latent_back = dot(embedded_back, embed_w[...], (1, 1))
        for image_at in range(MINE):
            at = image_at * KMAX
            own_latent[image_at] = latent_back[at : at + KMAX // 2, :]
            far_latent[image_at] = latent_back[at + KMAX // 2 : at + KMAX, :].astype(BF)
        whole = OUTPUT_AT // BLOCK

        def block_of(index):
            return grads[pl.ds(index * BLOCK, BLOCK), :].astype(BF)

        put_low(slots, far_lines, near_lines, block_of, grads, low_lines, whole)


def put_low(slots, far_lines, near_lines, block_of, grads, low_lines, whole):
    def store(slot, value):
        @pl.when(slot < 8)
        def _():
            far_lines[pl.ds(pl.multiple_of(slot * BLOCK, 16), BLOCK), :] = value

        @pl.when(slot >= 8)
        def _():
            near_lines[pl.ds(pl.multiple_of((slot - 8) * BLOCK, 16), BLOCK), :] = value

    def early(index, carry):
        store(slots[index], block_of(index))
        return carry

    def late(index, carry):
        at = pl.multiple_of(index * BLOCK - OUTPUT_AT, 16)
        store(slots[index], low_lines[pl.ds(at, BLOCK), :])
        return carry

    lax.fori_loop(0, whole, early, 0)
    cut = OUTPUT_AT - whole * BLOCK
    store(
        slots[whole],
        jnp.concatenate(
            [grads[whole * BLOCK : OUTPUT_AT, :].astype(BF), low_lines[: BLOCK - cut, :]], axis=0
        ),
    )
    lax.fori_loop(whole + 1, 16, late, 0)


def backward_call(
    meta, slots, probs, joint, normed, start, back_middle, back_mixed, latents, restore, vectors,
    embed_w, joint_w, low_lines,
):
    shape = jax.ShapeDtypeStruct
    outs = (
        shape((8 * BLOCK, LANES), BF),
        shape((8 * BLOCK, LANES), BF),
        shape((8, D), F32),
        shape((MINE, KMAX // 2, DIN), F32),
        shape((MINE, KMAX // 2, DIN), BF),
    )
    return pl.pallas_call(
        backward_kernel,
        grid=(MINE * GROUPS,),
        in_specs=[SMEM, SMEM, pl.BlockSpec((GROUP, SLOTS, SLOTS), lambda i: (i, 0, 0))]
        + [VMEM] * 11,
        out_shape=outs,
        out_specs=tuple(VMEM for _ in outs),
        scratch_shapes=[
            pltpu.VMEM((D, TOKENS), BF),
            pltpu.VMEM((D, TOKENS), BF),
            pltpu.VMEM((D, TOKENS), BF),
            pltpu.VMEM((TOKENS, 3 * D), BF),
            pltpu.VMEM((OUTPUT_AT, LANES), F32),
        ],
        compiler_params=pltpu.CompilerParams(vmem_limit_bytes=56 * 2**20),
        cost_estimate=pl.CostEstimate(
            flops=8 * 10**9, bytes_accessed=16 * 2**20, transcendentals=10**5
        ),
    )(
        meta, slots, probs, joint, normed, start, back_middle, back_mixed, latents, restore,
        vectors, embed_w, joint_w, low_lines,
    )


class Grid:
    def __init__(self, mesh):
        self.axes = ("dp", "blk")
        self.count = mesh.shape["dp"] * mesh.shape["blk"]
        self.by_hand = self.count == 32 and mesh.shape["blk"] == 2

    def send(self, value, bits, other=None, only=None):
        other = bits if other is None else other
        pairs = [(i, i ^ (other if i & 2 else bits)) for i in range(self.count)]
        if only is not None:
            pairs = [(i, j) for i, j in pairs if (i & 16 == 0) == (only == 0)]
        return lax.ppermute(value, self.axes, pairs)

    def place(self):
        return (lax.axis_index("dp") * lax.axis_size("blk") + lax.axis_index("blk")).astype(
            jnp.int32
        )

    def gather(self, block):
        if not self.by_hand:
            whole = lax.all_gather(block, self.axes, axis=0, tiled=True)
            return [whole.reshape(LINES, LANES)], jnp.zeros((1,), jnp.int32)
        me = self.place()
        odd = (me >> 1) & 1
        held = {0: block}
        near, side, far = {}, {}, {}

        def plane(k):
            near[k] = self.send(held[k], 4, 1)
            side[k] = self.send(held[k], 1, 4)

        def corner(k):
            far[k] = self.send(near[k], 1, 4)

        held[16] = self.send(block, 16)
        plane(0)
        held[8] = self.send(block, 8)
        corner(0)
        plane(8)
        held[24] = self.send(held[16], 8)
        plane(16)
        corner(16)
        far[8] = self.send(far[0], 8)
        plane(24)
        far[24] = self.send(far[16], 8)
        pieces, table = [], []
        for k in (0, 8, 16, 24):
            for value, even, uneven in (
                (held[k], 0, 0),
                (near[k], 4, 1),
                (side[k], 1, 4),
                (far[k], 5, 5),
            ):
                pieces.append(value)
                table.append(me ^ k ^ jnp.where(odd == 0, even, uneven))
                pieces.append(self.send(value, 2))
                table.append(me ^ k ^ 2 ^ jnp.where(odd == 0, uneven, even))
        return pieces, jnp.stack(table).astype(jnp.int32)

    def slots(self):
        index = jnp.arange(16, dtype=jnp.int32)
        if not self.by_hand:
            return index
        me = self.place()
        rel = index ^ (me & 15)
        other = (rel >> 1) & 1
        odd = ((me >> 1) & 1) ^ other
        cross = rel & 5
        side = jnp.where(odd == 0, 1, 4)
        kind = jnp.where(cross == 5, 0, jnp.where(cross == 0, 3, jnp.where(cross == side, 1, 2)))
        return ((rel >> 3) * 4 + kind + jnp.where(other == 1, 0, 8)).astype(jnp.int32)

    def reduce_half(self, far_lines, near_lines, half):
        def add(left, right):
            return (left.astype(F32) + right.astype(F32)).astype(BF)

        both = add(near_lines, self.send(far_lines, 2)).reshape(2, 4, BLOCK, LANES)
        level = []
        for k in (1, 0):
            quarter = both[k]
            pair = add(quarter[2:], self.send(quarter[:2], 1, 4))
            level.append(add(pair[1], self.send(pair[0], 4, 1)))
        chip = add(level[1], self.send(level[0], 8))
        return chip.astype(F32) + self.send(chip, 16, only=1 - half).astype(F32)

    def sum_all(self, value):
        if not self.by_hand:
            return lax.psum(value, self.axes)
        for bits in (2, 1, 4, 8, 16):
            value = value + self.send(value, bits)
        return value


def local(
    grid,
    latents,
    restore,
    bucket,
    cotangent,
    flat_weights,
    flat_first,
    flat_second,
    vectors,
    vector_first,
    vector_second,
):
    me = grid.place()
    side = lax.axis_index("blk").astype(jnp.int32)
    swap = [(0, 1), (1, 0)]

    def mine(value):
        return lax.dynamic_slice_in_dim(value, side * MINE, MINE, axis=0)

    def trade(value):
        sent = lax.dynamic_slice_in_dim(value, (1 - side) * MINE, MINE, axis=0)
        return jnp.concatenate([mine(value), lax.ppermute(sent, "blk", swap)], axis=1)

    own_weights = flat_weights.reshape(-1, LANES)
    pieces, table = grid.gather(own_weights.astype(BF))
    slots = grid.slots()
    meta = jnp.concatenate([side[None], image_lengths(mine(bucket))]).astype(jnp.int32)
    my_latents = trade(latents).reshape(MINE * KMAX, DIN)
    my_restore = trade(restore).reshape(TOKENS, 1)
    my_cotangent = trade(cotangent).reshape(TOKENS, D)
    slot = (jnp.arange(SLOTS, dtype=jnp.int32) + side * (SLOTS // 2)) & (SLOTS - 1)
    position = position_rows(slot)

    probs, joint, normed, start, middle, mixed, embed_w, joint_w, output_w = forward_call(
        meta, table, my_latents, my_restore, position, vectors, pieces
    )
    (
        own_out, far_out, back_middle, back_mixed, low_lines, far_high, near_high, rows_b, expand_b,
    ) = middle_call(meta, table, slots, middle, mixed, my_cotangent, output_w, vectors, pieces)
    far_low, near_low, rows_c, own_latent, far_latent = backward_call(
        meta, slots, probs, joint, normed, start, back_middle, back_mixed, my_latents, my_restore,
        vectors, embed_w, joint_w, low_lines,
    )

    def join(own, far):
        other = lax.ppermute(far, "blk", swap).astype(F32)
        return jnp.where(
            side == 0,
            jnp.concatenate([own, other], axis=0),
            jnp.concatenate([other, own], axis=0),
        )

    block_out = join(own_out, far_out)
    latent_out = join(own_latent, far_latent)

    vector_sum = grid.sum_all(
        jnp.concatenate([rows_c[:6], rows_b[:4], expand_b.reshape(4, D)], axis=0)
    )
    if grid.by_hand:
        high = grid.reduce_half(far_high, near_high, 1)
        low = grid.reduce_half(far_low, near_low, 0)
        shard_grad = jnp.where(me & 16 == 0, low, high)
    else:
        flat = jnp.concatenate([far_low, near_low, far_high, near_high], axis=0).reshape(-1)
        shard_grad = lax.psum_scatter(
            flat, grid.axes, scatter_dimension=0, tiled=True
        ).astype(F32).reshape(-1, LANES)
    square_sum = grid.sum_all(jnp.sum(shard_grad * shard_grad))
    grad_norm = jnp.sqrt(square_sum + jnp.sum(vector_sum * vector_sum))
    factor = jnp.minimum(1.0, clip_norm / (grad_norm + 1e-06))
    new_first, new_second, new_weights = adam_update(
        shard_grad.reshape(-1) * factor,
        flat_first,
        flat_second,
        flat_weights,
        learn_rate,
        decay_weight,
    )
    vector_first_new, vector_second_new, vectors_new = adam_update(
        vector_sum * factor, vector_first, vector_second, vectors, vector_rate, 0.0
    )
    reduce_bias_grad = vector_sum[9] * factor
    return (
        block_out,
        latent_out,
        new_first,
        new_second,
        new_weights,
        vector_first_new,
        vector_second_new,
        vectors_new,
        reduce_bias_grad,
        grad_norm,
    )


def solution(mesh):
    grid = Grid(mesh)
    return jax.shard_map(
        lambda *args: local(grid, *args),
        mesh=mesh,
        in_specs=(
            P("dp", "blk", None),
            P("dp", "blk"),
            P("dp"),
            P("dp", "blk", None),
            P(("dp", "blk")),
            P(("dp", "blk")),
            P(("dp", "blk")),
            P(),
            P(),
            P(),
        ),
        out_specs=(
            P("dp", "blk", None),
            P("dp", "blk", None),
            P(("dp", "blk")),
            P(("dp", "blk")),
            P(("dp", "blk")),
            P(),
            P(),
            P(),
            P(),
            P(),
        ),
        check_vma=False,
    )
```

time: 735 us -> 228 us (0.31)
  waiting for transfers between devices: 316 us -> 60.8 us
  matrix products: 190 us -> 0 us
  local copies, waits for them, and re-layouts: 113 us -> 5.44 us
  starting transfers between devices: 1.33 us -> 73.8 us
  Pallas kernels: 0 us -> 62.2 us
  blocking collectives: 50.6 us -> 0 us
  other arithmetic: 39.5 us -> 17.2 us
  between operations: 17.8 us -> 7.19 us
    unnamed x9 -> x0, waiting for transfers between devices: 240 us -> none
    dot_general x44 -> x0, matrix products: 181 us -> none  [the longest x2 59.2 us: one_batch(): jnp.einsum('bhqk,bqhe->bkhe', back_scores_low, query, preferred_element_t...]
    all_gather x3 -> x0, waiting for transfers between devices: 75.2 us -> none  [the longest x1 68.9 us: local(): lax.all_gather(flat_weights.astype(jnp.bfloat16), ('dp', 'blk'), axis=0,...]
    ppermute x0 -> x60, starting transfers between devices: none -> 73.8 us  [the longest x55 66.5 us: send(): return lax.ppermute(value, self.axes, pairs)]
    pallas_call x0 -> x3, Pallas kernels: none -> 62.2 us  [the longest x1 21.6 us: middle_call(): pl.pallas_call(lambda *refs: middle_kernel(*refs, pieces=count), grid=(TI...]
    ppermute x0 -> x60, waiting for transfers between devices: none -> 60.8 us  [the longest x55 55.3 us: send(): return lax.ppermute(value, self.axes, pairs)]
    unnamed x192 -> x78, local copies, waits for them, and re-layouts: 45.4 us -> 2.41 us
    psum x1 -> x0, blocking collectives: 40.5 us -> none  [local(): lax.psum((vector_total, jnp.sum(shard_grad * shard_grad)), ('dp', 'blk'))]
  transfers between devices with their start and end apart: 8 -> 60, of which waited for: 4 -> 29; matrix products, arithmetic and copies ran while one was open for 27% -> 7% of each run, Pallas kernels for 0% -> 0%
where the time goes in v1:
time: 228 us; the launch traced here: 227 us
  starting transfers between devices  73.8 us (32%)
  Pallas kernels  62.2 us (27%)
  waiting for transfers between devices  60.8 us (27%)
  other arithmetic  17.2 us (8%)
  between operations  7.19 us (3%)
  local copies, waits for them, and re-layouts  5.44 us (2%)
    ppermute x55, starting transfers between devices, send(): return lax.ppermute(value, self.axes, pairs)  66.5 us
    ppermute x55, waiting for transfers between devices, send(): return lax.ppermute(value, self.axes, pairs)  55.3 us
    pallas_call x1, Pallas kernels, middle_call(): pl.pallas_call(lambda *refs: middle_kernel(*refs, pieces=count), grid=(TI...  21.6 us
    pallas_call x1, Pallas kernels, forward_call(): pl.pallas_call(lambda *refs: forward_kernel(*refs, pieces=count), grid=(M...  20.8 us
    pallas_call x1, Pallas kernels, backward_call(): pl.pallas_call(backward_kernel, grid=(MINE * GROUPS,), in_specs=[SMEM, SM...  19.8 us
    ppermute x3, waiting for transfers between devices, trade(): lax.ppermute(sent, 'blk', swap)  5.54 us
  transfers between devices with their start and end apart: 60, of which 29 were waited for; matrix products, arithmetic and copies ran while one was open for 7% of the time, Pallas kernels for 0%

profile of v1, /device:TPU:0, one launch (start us, length us, event | category | flops | bytes accessed | tf_op | source)
XLA Modules:
  0.0 226.7 jit_solution(4414563845633950210)
XLA Ops:
  1.7 4.1 %collective-permute-start.17 = (bf16[864,128]{1,0:T(8,128)(2,1)S(1)}, bf16[864,128]{1,0:T(8,128)(2,1)S(1)}, u32[]{:S(2)}, u32[]{:S(2)}) collective-permute-start(bf16[864,128]{1,0:T(8,128)(2,1)S(1)} %convert_bitcast_fusion.refs_6_.refs_8_), channel_id=1, source_target_pairs={{0,16},{1,17},{2,18},{3,19},{4,20},{5,21},{6,22},{7,23},{8,24},{9,... | collective-permute-start | bytes 663560 | tf_op jit(solution)/shard_map/ppermute | solution.py:623
  13.2 5.5 %collective-permute-done.1 = s32[2,128]{1,0:T(2,128)S(1)} collective-permute-done((s32[2,128]{1,0:T(2,128)S(1)}, s32[2,128]{1,0:T(2,128)S(1)}, u32[]{:S(2)}, u32[]{:S(2)}) %collective-permute-start.1) | collective-permute-done | bytes 1056 | tf_op jit(solution)/shard_map/ppermute | solution.py:727
  22.7 3.0 %collective-permute-done.5.refs_10_.refs_12_ = bf16[864,128]{1,0:T(8,128)(2,1)S(1)} collective-permute-done((bf16[864,128]{1,0:T(8,128)(2,1)S(1)}, bf16[864,128]{1,0:T(8,128)(2,1)S(1)}, u32[]{:S(2)}, u32[]{:S(2)}) %collective-permute-start.5) | collective-permute-done | bytes 221216 | tf_op jit(solution)/shard_map/ppermute | solution.py:623
  31.9 2.5 %collective-permute-done.19.refs_24_.refs_26_ = bf16[864,128]{1,0:T(8,128)(2,1)S(1)} collective-permute-done((bf16[864,128]{1,0:T(8,128)(2,1)S(1)}, bf16[864,128]{1,0:T(8,128)(2,1)S(1)}, u32[]{:S(2)}, u32[]{:S(2)}) %collective-permute-start.19) | collective-permute-done | bytes 221216 | tf_op jit(solution)/shard_map/ppermute | solution.py:623
  40.2 2.5 %collective-permute-start.27 = (bf16[864,128]{1,0:T(8,128)(2,1)S(1)}, bf16[864,128]{1,0:T(8,128)(2,1)S(1)}, u32[]{:S(2)}, u32[]{:S(2)}) collective-permute-start(bf16[864,128]{1,0:T(8,128)(2,1)S(1)} %collective-permute-done.25.refs_30_.refs_32_), channel_id=1, source_target_pairs={{0,4},{1,5},{2,3},{3,2},{4,0},{5,1},{6,7},{7,6},{8,12},{9,13},{10,... | collective-permute-start | bytes 663560 | tf_op jit(solution)/shard_map/ppermute | solution.py:623
  53.0 3.3 %collective-permute-done.15.refs_20_.refs_22_ = bf16[864,128]{1,0:T(8,128)(2,1)} collective-permute-done((bf16[864,128]{1,0:T(8,128)(2,1)}, bf16[864,128]{1,0:T(8,128)(2,1)}, u32[]{:S(2)}, u32[]{:S(2)}) %collective-permute-start.15) | collective-permute-done | bytes 221216 | tf_op jit(solution)/shard_map/ppermute | solution.py:623
  56.8 3.0 %collective-permute-done.31.refs_36_.refs_38_ = bf16[864,128]{1,0:T(8,128)(2,1)} collective-permute-done((bf16[864,128]{1,0:T(8,128)(2,1)}, bf16[864,128]{1,0:T(8,128)(2,1)}, u32[]{:S(2)}, u32[]{:S(2)}) %collective-permute-start.31) | collective-permute-done | bytes 221216 | tf_op jit(solution)/shard_map/ppermute | solution.py:623
  62.4 20.8 %shard_map.177 = (bf16[32,256,256]{2,1,0:T(8,128)(2,1)}, bf16[512,1536]{1,0:T(8,128)(2,1)}, bf16[512,512]{1,0:T(8,128)(2,1)}, f32[512,512]{1,0:T(8,128)}, f32[51...) custom-call(s32[3]{0:T(128)} %pad_add_fusion.refs_0_.meta, ...), custom_call_target="tpu_custom_call" | custom-call | flops 6000000000 | bytes 16777216 | tf_op jit(solution)/shard_map/pallas_call | solution.py:236
  83.2 21.6 %shard_map.178 = (f32[2,128,512]{2,1,0:T(8,128)}, bf16[2,128,512]{2,1,0:T(8,128)(2,1)}, f32[512,512]{1,0:T(8,128)}, bf16[512,512]{1,0:T(8,128)(2,1)}, bf16[4608,...) custom-call(s32[3]{0:T(128)} %pad_add_fusion.refs_0_.meta, ...), custom_call_target="tpu_custom_call" | custom-call | flops 8000000000 | bytes 16777216 | tf_op jit(solution)/shard_map/pallas_call | solution.py:413
  104.9 19.8 %shard_map.179 = (bf16[6912,128]{1,0:T(8,128)(2,1)}, bf16[6912,128]{1,0:T(8,128)(2,1)}, f32[8,512]{1,0:T(8,128)}, f32[2,32,768]{2,1,0:T(8,128)}, bf16[2,32,768]{2,1,0:T(8,128)(2,1)}) custom-call(s32[3]{0:T(128)} %pad_add_fusion.refs_0_.meta, s32[16]{0:T(128)} %fusion.12.refs_2_.slots, bf16[32,256,256]{2,1,0:T(8,128)(2,1)} %get-tuple-element.38.probs, ...), custom_call_target="tpu_custom_call" | custom-call | flops 8000000000 | bytes 16777216 | tf_op jit(solution)/shard_map/pallas_call | solution.py:588
  148.4 3.8 %collective-permute-done.39 = bf16[2,864,128]{2,1,0:T(8,128)(2,1)S(1)} collective-permute-done((bf16[2,864,128]{2,1,0:T(8,128)(2,1)S(1)}, bf16[2,864,128]{2,1,0:T(8,128)(2,1)S(1)}, u32[]{:S(2)}, u32[]{:S(2)}) %collective-permute-start.39) | collective-permute-done | bytes 442400 | tf_op jit(solution)/shard_map/ppermute | solution.py:623
  154.2 2.8 %collective-permute-done.37 = bf16[2,864,128]{2,1,0:T(8,128)(2,1)S(1)} collective-permute-done((bf16[2,864,128]{2,1,0:T(8,128)(2,1)S(1)}, bf16[2,864,128]{2,1,0:T(8,128)(2,1)S(1)}, u32[]{:S(2)}, u32[]{:S(2)}) %collective-permute-start.37) | collective-permute-done | bytes 442400 | tf_op jit(solution)/shard_map/ppermute | solution.py:623
  156.9 2.6 %collective-permute-start.40 = (bf16[864,128]{1,0:T(8,128)(2,1)S(1)}, bf16[864,128]{1,0:T(8,128)(2,1)S(1)}, u32[]{:S(2)}, u32[]{:S(2)}) collective-permute-start(bf16[864,128]{1,0:T(8,128)(2,1)S(1)} %slice_bitcast_fusion.4), channel_id=1, source_target_pairs={{0,4},{1,5},{2,3},{3,2},{4,0},{5,1},{6,7},{7,6},{8,12},{9,13},{10,... | collective-permute-start | bytes 663560 | tf_op jit(solution)/shard_map/ppermute | solution.py:623
  159.7 6.0 %collective-permute-done.46 = bf16[2,864,128]{2,1,0:T(8,128)(2,1)S(1)} collective-permute-done((bf16[2,864,128]{2,1,0:T(8,128)(2,1)S(1)}, bf16[2,864,128]{2,1,0:T(8,128)(2,1)S(1)}, u32[]{:S(2)}, u32[]{:S(2)}) %collective-permute-start.46) | collective-permute-done | bytes 442400 | tf_op jit(solution)/shard_map/ppermute | solution.py:623
  165.8 2.5 %collective-permute-start.38 = (bf16[864,128]{1,0:T(8,128)(2,1)S(1)}, bf16[864,128]{1,0:T(8,128)(2,1)S(1)}, u32[]{:S(2)}, u32[]{:S(2)}) collective-permute-start(bf16[864,128]{1,0:T(8,128)(2,1)S(1)} %slice_bitcast_fusion.6), channel_id=1, source_target_pairs={{0,4},{1,5},{2,3},{3,2},{4,0},{5,1},{6,7},{7,6},{8,12},{9,13},{10,... | collective-permute-start | bytes 663560 | tf_op jit(solution)/shard_map/ppermute | solution.py:623
  168.4 4.8 %collective-permute-done.44 = bf16[2,864,128]{2,1,0:T(8,128)(2,1)S(1)} collective-permute-done((bf16[2,864,128]{2,1,0:T(8,128)(2,1)S(1)}, bf16[2,864,128]{2,1,0:T(8,128)(2,1)S(1)}, u32[]{:S(2)}, u32[]{:S(2)}) %collective-permute-start.44) | collective-permute-done | bytes 442400 | tf_op jit(solution)/shard_map/ppermute | solution.py:623
  173.2 4.0 %collective-permute-start.47 = (bf16[864,128]{1,0:T(8,128)(2,1)S(1)}, bf16[864,128]{1,0:T(8,128)(2,1)S(1)}, u32[]{:S(2)}, u32[]{:S(2)}) collective-permute-start(bf16[864,128]{1,0:T(8,128)(2,1)S(1)} %slice_bitcast_fusion), channel_id=1, source_target_pairs={{0,4},{1,5},{2,3},{3,2},{4,0},{5,1},{6,7},{7,6},{8,12},{9,13},{10,... | collective-permute-start | bytes 663560 | tf_op jit(solution)/shard_map/ppermute | solution.py:623
  177.6 3.6 %collective-permute-done.47 = bf16[864,128]{1,0:T(8,128)(2,1)S(1)} collective-permute-done((bf16[864,128]{1,0:T(8,128)(2,1)S(1)}, bf16[864,128]{1,0:T(8,128)(2,1)S(1)}, u32[]{:S(2)}, u32[]{:S(2)}) %collective-permute-start.47) | collective-permute-done | bytes 221216 | tf_op jit(solution)/shard_map/ppermute | solution.py:623
  183.4 5.5 %collective-permute-done.41 = bf16[864,128]{1,0:T(8,128)(2,1)S(1)} collective-permute-done((bf16[864,128]{1,0:T(8,128)(2,1)S(1)}, bf16[864,128]{1,0:T(8,128)(2,1)S(1)}, u32[]{:S(2)}, u32[]{:S(2)}) %collective-permute-start.41) | collective-permute-done | bytes 221216 | tf_op jit(solution)/shard_map/ppermute | solution.py:623
  191.3 4.5 %collective-permute-start.49 = (bf16[864,128]{1,0:T(8,128)(2,1)S(1)}, bf16[864,128]{1,0:T(8,128)(2,1)S(1)}, u32[]{:S(2)}, u32[]{:S(2)}) collective-permute-start(bf16[864,128]{1,0:T(8,128)(2,1)S(1)} %add_convert_fusion.2), channel_id=1, source_target_pairs={{0,16},{1,17},{2,18},{3,19},{4,20},{5,21},{6,22},{7,23},{8,24},{9,... | collective-permute-start | bytes 663560 | tf_op jit(solution)/shard_map/ppermute | solution.py:623
  202.6 4.1 %collective-permute-start.51 = (f32[]{:T(128)}, f32[]{:T(128)}, u32[]{:S(2)}, u32[]{:S(2)}) collective-permute-start(f32[]{:T(128)} %add.161), channel_id=1, source_target_pairs={{0,1},{1,0},{2,3},{3,2},{4,5},{5,4},{6,7},{7,6},{8,9},{9,8},{10,11... | collective-permute-start | bytes 20 | tf_op jit(solution)/shard_map/ppermute | solution.py:623
  207.5 3.0 %collective-permute-start.52 = (f32[]{:T(128)}, f32[]{:T(128)}, u32[]{:S(2)}, u32[]{:S(2)}) collective-permute-start(f32[]{:T(128)} %add.162), channel_id=1, source_target_pairs={{0,4},{1,5},{2,6},{3,7},{4,0},{5,1},{6,2},{7,3},{8,12},{9,13},{10,... | collective-permute-start | bytes 20 | tf_op jit(solution)/shard_map/ppermute | solution.py:623
  211.8 4.1 %collective-permute-start.53 = (f32[]{:T(128)}, f32[]{:T(128)}, u32[]{:S(2)}, u32[]{:S(2)}) collective-permute-start(f32[]{:T(128)} %add.163), channel_id=1, source_target_pairs={{0,8},{1,9},{2,10},{3,11},{4,12},{5,13},{6,14},{7,15},{8,0},{9,1},... | collective-permute-start | bytes 20 | tf_op jit(solution)/shard_map/ppermute | solution.py:623
  216.7 4.7 %collective-permute-start.54 = (f32[]{:T(128)}, f32[]{:T(128)}, u32[]{:S(2)}, u32[]{:S(2)}) collective-permute-start(f32[]{:T(128)} %add.164), channel_id=1, source_target_pairs={{0,16},{1,17},{2,18},{3,19},{4,20},{5,21},{6,22},{7,23},{8,24},{9,... | collective-permute-start | bytes 20 | tf_op jit(solution)/shard_map/ppermute | solution.py:623
  (224 shorter events, 77.2 us)
Async XLA Ops:
  1.7 19.7 %collective-permute-start.17 = (bf16[864,128]{1,0:T(8,128)(2,1)S(1)}, bf16[864,128]{1,0:T(8,128)(2,1)S(1)}, u32[]{:S(2)}, u32[]{:S(2)}) collective-permute-start(bf16[864,128]{1,0:T(8,128)(2,1)S(1)} %convert_bitcast_fusion.refs_6_.refs_8_), channel_id=1, source_target_pairs={{0,16},{1,17},{2,18},{3,19},{4,20},{5,21},{6,22},{7,23},{8,24},{9,... | collective-permute-start | bytes 663560 | tf_op jit(solution)/shard_map/ppermute | solution.py:623
  5.8 15.6 %collective-permute-start.9 = (bf16[864,128]{1,0:T(8,128)(2,1)S(1)}, bf16[864,128]{1,0:T(8,128)(2,1)S(1)}, u32[]{:S(2)}, u32[]{:S(2)}) collective-permute-start(bf16[864,128]{1,0:T(8,128)(2,1)S(1)} %convert_bitcast_fusion.refs_6_.refs_8_), channel_id=1, source_target_pairs={{0,8},{1,9},{2,10},{3,11},{4,12},{5,13},{6,14},{7,15},{8,0},{9,1},... | collective-permute-start | bytes 663560 | tf_op jit(solution)/shard_map/ppermute | solution.py:623
  8.4 11.6 %collective-permute-start = (bf16[2,32,768]{2,1,0:T(8,128)(2,1)S(1)}, bf16[2,32,768]{2,1,0:T(8,128)(2,1)S(1)}, u32[]{:S(2)}, u32[]{:S(2)}) collective-permute-start(bf16[2,32,768]{2,1,0:T(8,128)(2,1)S(1)} %get-tuple-element.77), channel_id=1, source_target_pairs={{0,1},{1,0},{2,3},{3,2},{4,5},{5,4},{6,7},{7,6},{8,9},{9,8},{10,11... | collective-permute-start | bytes 294920 | tf_op jit(solution)/shard_map/ppermute | solution.py:727
  11.0 17.7 %collective-permute-start.33 = (bf16[2,128,512]{2,1,0:T(8,128)(2,1)S(1)}, bf16[2,128,512]{2,1,0:T(8,128)(2,1)S(1)}, u32[]{:S(2)}, u32[]{:S(2)}) collective-permute-start(bf16[2,128,512]{2,1,0:T(8,128)(2,1)S(1)} %get-tuple-element.75), channel_id=1, source_target_pairs={{0,1},{1,0},{2,3},{3,2},{4,5},{5,4},{6,7},{7,6},{8,9},{9,8},{10,11... | collective-permute-start | bytes 786440 | tf_op jit(solution)/shard_map/ppermute | solution.py:727
  29.3 9.9 %collective-permute-start.11 = (bf16[864,128]{1,0:T(8,128)(2,1)S(1)}, bf16[864,128]{1,0:T(8,128)(2,1)S(1)}, u32[]{:S(2)}, u32[]{:S(2)}) collective-permute-start(bf16[864,128]{1,0:T(8,128)(2,1)S(1)} %collective-permute-done.9.refs_14_.refs_16_), channel_id=1, source_target_pairs={{0,4},{1,5},{2,3},{3,2},{4,0},{5,1},{6,7},{7,6},{8,12},{9,13},{10,... | collective-permute-start | bytes 663560 | tf_op jit(solution)/shard_map/ppermute | solution.py:623
  34.4 8.3 %collective-permute-start.7 = (bf16[864,128]{1,0:T(8,128)(2,1)S(1)}, bf16[864,128]{1,0:T(8,128)(2,1)}, u32[]{:S(2)}, u32[]{:S(2)}) collective-permute-start(bf16[864,128]{1,0:T(8,128)(2,1)S(1)} %collective-permute-done.3.refs_8_.refs_10_), channel_id=1, source_target_pairs={{0,1},{1,0},{2,6},{3,7},{4,5},{5,4},{6,2},{7,3},{8,9},{9,8},{10,14... | collective-permute-start | bytes 663560 | tf_op jit(solution)/shard_map/ppermute | solution.py:623
  35.7 9.1 %collective-permute-start.4 = (bf16[864,128]{1,0:T(8,128)(2,1)S(1)}, bf16[864,128]{1,0:T(8,128)(2,1)S(1)}, u32[]{:S(2)}, u32[]{:S(2)}) collective-permute-start(bf16[864,128]{1,0:T(8,128)(2,1)S(1)} %collective-permute-done.3.refs_8_.refs_10_), channel_id=1, source_target_pairs={{0,2},{1,3},{2,0},{3,1},{4,6},{5,7},{6,4},{7,5},{8,10},{9,11},{10,... | collective-permute-start | bytes 663560 | tf_op jit(solution)/shard_map/ppermute | solution.py:623
  50.4 9.4 %collective-permute-start.31 = (bf16[864,128]{1,0:T(8,128)(2,1)}, bf16[864,128]{1,0:T(8,128)(2,1)}, u32[]{:S(2)}, u32[]{:S(2)}) collective-permute-start(bf16[864,128]{1,0:T(8,128)(2,1)} %collective-permute-done.23.refs_28_.refs_30_), channel_id=1, source_target_pairs={{0,8},{1,9},{2,10},{3,11},{4,12},{5,13},{6,14},{7,15},{8,0},{9,1},... | collective-permute-start | bytes 663560 | tf_op jit(solution)/shard_map/ppermute | solution.py:623
  52.5 8.8 %collective-permute-start.24 = (bf16[864,128]{1,0:T(8,128)(2,1)}, bf16[864,128]{1,0:T(8,128)(2,1)S(1)}, u32[]{:S(2)}, u32[]{:S(2)}) collective-permute-start(bf16[864,128]{1,0:T(8,128)(2,1)} %collective-permute-done.23.refs_28_.refs_30_), channel_id=1, source_target_pairs={{0,2},{1,3},{2,0},{3,1},{4,6},{5,7},{6,4},{7,5},{8,10},{9,11},{10,... | collective-permute-start | bytes 663560 | tf_op jit(solution)/shard_map/ppermute | solution.py:623
  52.7 8.6 %collective-permute-start.30 = (bf16[864,128]{1,0:T(8,128)(2,1)}, bf16[864,128]{1,0:T(8,128)(2,1)S(1)}, u32[]{:S(2)}, u32[]{:S(2)}) collective-permute-start(bf16[864,128]{1,0:T(8,128)(2,1)} %copy-done.27), channel_id=1, source_target_pairs={{0,2},{1,3},{2,0},{3,1},{4,6},{5,7},{6,4},{7,5},{8,10},{9,11},{10,... | collective-permute-start | bytes 663560 | tf_op jit(solution)/shard_map/ppermute | solution.py:623
  124.7 17.1 %collective-permute-start.36 = (bf16[6912,128]{1,0:T(8,128)(2,1)}, bf16[6912,128]{1,0:T(8,128)(2,1)S(1)}, u32[]{:S(2)}, u32[]{:S(2)}) collective-permute-start(bf16[6912,128]{1,0:T(8,128)(2,1)} %get-tuple-element.50), channel_id=1, source_target_pairs={{0,2},{1,3},{2,0},{3,1},{4,6},{5,7},{6,4},{7,5},{8,10},{9,11},{10,... | collective-permute-start | bytes 5308424 | tf_op jit(solution)/shard_map/ppermute | solution.py:623
  126.1 12.2 %collective-permute-start.35 = (bf16[2,32,768]{2,1,0:T(8,128)(2,1)}, bf16[2,32,768]{2,1,0:T(8,128)(2,1)S(1)}, u32[]{:S(2)}, u32[]{:S(2)}) collective-permute-start(bf16[2,32,768]{2,1,0:T(8,128)(2,1)} %get-tuple-element.48), channel_id=1, source_target_pairs={{0,1},{1,0},{2,3},{3,2},{4,5},{5,4},{6,7},{7,6},{8,9},{9,8},{10,11... | collective-permute-start | bytes 294920 | tf_op jit(solution)/shard_map/ppermute | solution.py:751
  135.4 61.1 %collective-permute-start.34 = (bf16[2,128,512]{2,1,0:T(8,128)(2,1)S(1)}, bf16[2,128,512]{2,1,0:T(8,128)(2,1)S(1)}, u32[]{:S(2)}, u32[]{:S(2)}) collective-permute-start(bf16[2,128,512]{2,1,0:T(8,128)(2,1)S(1)} %copy-done.12), channel_id=1, source_target_pairs={{0,1},{1,0},{2,3},{3,2},{4,5},{5,4},{6,7},{7,6},{8,9},{9,8},{10,11... | collective-permute-start | bytes 786440 | tf_op jit(solution)/shard_map/ppermute | solution.py:751
  137.4 8.5 %collective-permute-start.43 = (bf16[6912,128]{1,0:T(8,128)(2,1)}, bf16[6912,128]{1,0:T(8,128)(2,1)S(1)}, u32[]{:S(2)}, u32[]{:S(2)}) collective-permute-start(bf16[6912,128]{1,0:T(8,128)(2,1)} %get-tuple-element.52), channel_id=1, source_target_pairs={{0,2},{1,3},{2,0},{3,1},{4,6},{5,7},{6,4},{7,5},{8,10},{9,11},{10,... | collective-permute-start | bytes 5308424 | tf_op jit(solution)/shard_map/ppermute | solution.py:623
  141.4 54.5 %collective-permute-start.59 = (f32[14,512]{1,0:T(8,128)S(1)}, f32[14,512]{1,0:T(8,128)S(1)}, u32[]{:S(2)}, u32[]{:S(2)}) collective-permute-start(f32[14,512]{1,0:T(8,128)S(1)} %add.169), channel_id=1, source_target_pairs={{0,16},{1,17},{2,18},{3,19},{4,20},{5,21},{6,22},{7,23},{8,24},{9,... | collective-permute-start | bytes 86024 | tf_op jit(solution)/shard_map/ppermute | solution.py:623
  143.8 8.4 %collective-permute-start.39 = (bf16[2,864,128]{2,1,0:T(8,128)(2,1)S(1)}, bf16[2,864,128]{2,1,0:T(8,128)(2,1)S(1)}, u32[]{:S(2)}, u32[]{:S(2)}) collective-permute-start(bf16[2,864,128]{2,1,0:T(8,128)(2,1)S(1)} %bitcast.99), channel_id=1, source_target_pairs={{0,1},{1,0},{2,6},{3,7},{4,5},{5,4},{6,2},{7,3},{8,9},{9,8},{10,14... | collective-permute-start | bytes 1327112 | tf_op jit(solution)/shard_map/ppermute | solution.py:623
  145.7 11.2 %collective-permute-start.37 = (bf16[2,864,128]{2,1,0:T(8,128)(2,1)S(1)}, bf16[2,864,128]{2,1,0:T(8,128)(2,1)S(1)}, u32[]{:S(2)}, u32[]{:S(2)}) collective-permute-start(bf16[2,864,128]{2,1,0:T(8,128)(2,1)S(1)} %bitcast.97), channel_id=1, source_target_pairs={{0,1},{1,0},{2,6},{3,7},{4,5},{5,4},{6,2},{7,3},{8,9},{9,8},{10,14... | collective-permute-start | bytes 1327112 | tf_op jit(solution)/shard_map/ppermute | solution.py:623
  146.5 19.2 %collective-permute-start.46 = (bf16[2,864,128]{2,1,0:T(8,128)(2,1)S(1)}, bf16[2,864,128]{2,1,0:T(8,128)(2,1)S(1)}, u32[]{:S(2)}, u32[]{:S(2)}) collective-permute-start(bf16[2,864,128]{2,1,0:T(8,128)(2,1)S(1)} %bitcast.98), channel_id=1, source_target_pairs={{0,1},{1,0},{2,6},{3,7},{4,5},{5,4},{6,2},{7,3},{8,9},{9,8},{10,14... | collective-permute-start | bytes 1327112 | tf_op jit(solution)/shard_map/ppermute | solution.py:623
  152.2 21.0 %collective-permute-start.44 = (bf16[2,864,128]{2,1,0:T(8,128)(2,1)S(1)}, bf16[2,864,128]{2,1,0:T(8,128)(2,1)S(1)}, u32[]{:S(2)}, u32[]{:S(2)}) collective-permute-start(bf16[2,864,128]{2,1,0:T(8,128)(2,1)S(1)} %bitcast.96), channel_id=1, source_target_pairs={{0,1},{1,0},{2,6},{3,7},{4,5},{5,4},{6,2},{7,3},{8,9},{9,8},{10,14... | collective-permute-start | bytes 1327112 | tf_op jit(solution)/shard_map/ppermute | solution.py:623
  156.9 20.5 %collective-permute-start.40 = (bf16[864,128]{1,0:T(8,128)(2,1)S(1)}, bf16[864,128]{1,0:T(8,128)(2,1)S(1)}, u32[]{:S(2)}, u32[]{:S(2)}) collective-permute-start(bf16[864,128]{1,0:T(8,128)(2,1)S(1)} %slice_bitcast_fusion.4), channel_id=1, source_target_pairs={{0,4},{1,5},{2,3},{3,2},{4,0},{5,1},{6,7},{7,6},{8,12},{9,13},{10,... | collective-permute-start | bytes 663560 | tf_op jit(solution)/shard_map/ppermute | solution.py:623
  165.8 15.5 %collective-permute-start.38 = (bf16[864,128]{1,0:T(8,128)(2,1)S(1)}, bf16[864,128]{1,0:T(8,128)(2,1)S(1)}, u32[]{:S(2)}, u32[]{:S(2)}) collective-permute-start(bf16[864,128]{1,0:T(8,128)(2,1)S(1)} %slice_bitcast_fusion.6), channel_id=1, source_target_pairs={{0,4},{1,5},{2,3},{3,2},{4,0},{5,1},{6,7},{7,6},{8,12},{9,13},{10,... | collective-permute-start | bytes 663560 | tf_op jit(solution)/shard_map/ppermute | solution.py:623
  177.4 12.8 %collective-permute-start.45 = (bf16[864,128]{1,0:T(8,128)(2,1)S(1)}, bf16[864,128]{1,0:T(8,128)(2,1)S(1)}, u32[]{:S(2)}, u32[]{:S(2)}) collective-permute-start(bf16[864,128]{1,0:T(8,128)(2,1)S(1)} %slice_bitcast_fusion.2), channel_id=1, source_target_pairs={{0,4},{1,5},{2,3},{3,2},{4,0},{5,1},{6,7},{7,6},{8,12},{9,13},{10,... | collective-permute-start | bytes 663560 | tf_op jit(solution)/shard_map/ppermute | solution.py:623
  181.3 10.0 %collective-permute-start.48 = (bf16[864,128]{1,0:T(8,128)(2,1)S(1)}, bf16[864,128]{1,0:T(8,128)(2,1)S(1)}, u32[]{:S(2)}, u32[]{:S(2)}) collective-permute-start(bf16[864,128]{1,0:T(8,128)(2,1)S(1)} %fusion.5), channel_id=1, source_target_pairs={{0,8},{1,9},{2,10},{3,11},{4,12},{5,13},{6,14},{7,15},{8,0},{9,1},... | collective-permute-start | bytes 663560 | tf_op jit(solution)/shard_map/ppermute | solution.py:623
  189.0 10.1 %collective-permute-start.42 = (bf16[864,128]{1,0:T(8,128)(2,1)S(1)}, bf16[864,128]{1,0:T(8,128)(2,1)S(1)}, u32[]{:S(2)}, u32[]{:S(2)}) collective-permute-start(bf16[864,128]{1,0:T(8,128)(2,1)S(1)} %add_convert_fusion.3), channel_id=1, source_target_pairs={{16,0},{17,1},{18,2},{19,3},{20,4},{21,5},{22,6},{23,7},{24,8},{25... | collective-permute-start | bytes 663560 | tf_op jit(solution)/shard_map/ppermute | solution.py:623
  (74 other events, 946.0 us)

commit v2 on v1

v2 whole, which is shorter than its diff:
```python
import math

import jax
import jax.numpy as jnp
from jax import lax
from jax.experimental import pallas as pl
from jax.experimental.pallas import tpu as pltpu
from jax.sharding import PartitionSpec as P

DIN = 768
D = 512
HEADS = 16
HD = 32
FF = 2048
SLOTS = 256
KMAX = 64
STEP = 10
NPARAM = 3538944

first_decay = 0.9
second_decay = 0.95
learn_rate = 0.05
vector_rate = 0.5
decay_weight = 0.05
adam_eps = 1e-08
clip_norm = 1.0

BF = jnp.bfloat16
F32 = jnp.float32

LANES = 128
LINES = NPARAM // LANES
EMBED_AT = 0
JOINT_AT = EMBED_AT + DIN * D // LANES
OUTPUT_AT = JOINT_AT + 3 * D * D // LANES
EXPAND_AT = OUTPUT_AT + D * D // LANES
REDUCE_AT = EXPAND_AT + D * FF // LANES
BLOCK = LINES // 32
HALF = 16 * BLOCK
TAIL = 16
ROWS = 16
PART = BLOCK // 2
PARTS = (PART, PART + TAIL)
FIRST_BLOCKS = -(-EXPAND_AT // BLOCK)
SECOND_FROM = EXPAND_AT // BLOCK
SECOND_BLOCKS = 32 - SECOND_FROM
TILE = 256
TILES = FF // TILE
GROUP = 4
GROUPS = HEADS // GROUP
MINE = 2
TOKENS = MINE * SLOTS
PICKS = KMAX + 16
VMEM = pl.BlockSpec(memory_space=pltpu.VMEM)
SMEM = pl.BlockSpec(memory_space=pltpu.SMEM)
ANY = pl.BlockSpec(memory_space=pl.ANY)


def position_rows(slot):
    column = jnp.arange(D // 2, dtype=jnp.int32).astype(F32)[None, :]
    angle = slot.astype(F32)[:, None] * jnp.exp(-math.log(10000.0) * column / (D // 2))
    return jnp.concatenate([jnp.sin(angle), jnp.cos(angle)], axis=1)


def adam_update(grad, first, second, weight, rate, shrink):
    first_new = first_decay * first + (1.0 - first_decay) * grad
    second_new = second_decay * second + (1.0 - second_decay) * grad * grad
    first_hat = first_new / (1.0 - first_decay**STEP)
    second_hat = second_new / (1.0 - second_decay**STEP)
    weight_new = weight - rate * (first_hat / (jnp.sqrt(second_hat) + adam_eps) + shrink * weight)
    return (first_new, second_new, weight_new)


def dot(left, right, over=(1, 0)):
    return lax.dot_general(
        left, right, (((over[0],), (over[1],)), ((), ())), preferred_element_type=F32
    )


def place():
    return lax.axis_index("dp") * lax.axis_size("blk") + lax.axis_index("blk")


def fetch_lines(places, pieces, low_lines, high_lines, low_sem, high_sem):
    if places is None:
        for lines, low, sem in ((low_lines, 0, low_sem), (high_lines, SECOND_FROM, high_sem)):
            rows = pl.ds(low * BLOCK, lines.shape[0])
            pltpu.make_async_copy(pieces[0].at[rows], lines, sem).start()
            wait_lines(lines, sem)
        return
    me = place()
    odd = (me >> 1) & 1
    for (bits, even, uneven), piece in zip(places, pieces, strict=True):
        block = me ^ bits ^ jnp.where(odd == 0, even, uneven)

        @pl.when(block < FIRST_BLOCKS)
        def _(piece=piece, block=block):
            low_lines[pl.ds(pl.multiple_of(block * BLOCK, 16), BLOCK), :] = piece[...]

        @pl.when(block >= SECOND_FROM)
        def _(piece=piece, block=block):
            at = pl.multiple_of((block - SECOND_FROM) * BLOCK, 16)
            high_lines[pl.ds(at, BLOCK), :] = piece[...]


def wait_lines(lines, sem):
    pltpu.make_async_copy(lines, lines, sem).wait()


def lines_to_matrix(lines, stage, matrix, at, rows, wide, batch):
    size = batch * wide

    def body(index, carry):
        for part in range(2):
            row = pl.multiple_of((2 * index + part) * batch, batch)
            source = pl.multiple_of(at + (2 * index + part) * size, 16)
            stage[part, :size, :] = lines[pl.ds(source, size), :].astype(F32)
            for j in range(wide):
                matrix[pl.ds(row, batch), j * LANES : (j + 1) * LANES] = stage[
                    part, pl.ds(j, batch, stride=wide), :
                ].astype(BF)
        return carry

    lax.fori_loop(0, rows // batch // 2, body, 0)


def norm_parts(value):
    centred = value - jnp.mean(value, axis=-1, keepdims=True)
    scale = lax.rsqrt(jnp.mean(centred * centred, axis=-1, keepdims=True) + 1e-06)
    return centred * scale, scale


def norm_back(grad, hat, scale, gain):
    inner = grad * gain
    return scale * (
        inner
        - jnp.mean(inner, axis=-1, keepdims=True)
        - hat * jnp.mean(inner * hat, axis=-1, keepdims=True)
    )


def total(value):
    return jnp.sum(value.astype(F32), axis=0, keepdims=True)


def slot_column(side):
    local = lax.broadcasted_iota(jnp.int32, (SLOTS, 1), 0)
    return (local + side * (SLOTS // 2)) & (SLOTS - 1)


def image_length(bucket, image):
    kind = bucket[image]
    return jnp.where(
        kind == 0, SLOTS * 100 // 256, jnp.where(kind == 1, SLOTS * 196 // 256, SLOTS)
    )


def select_rows(own, far, image, side):
    half = SLOTS // 2
    row = lax.broadcasted_iota(jnp.int32, (PICKS, half), 0)
    row = jnp.where(row < KMAX, (row + side * (KMAX // 2)) & (KMAX - 1), row)
    parts = [
        (row == ref[pl.ds(image, 1), :]).astype(F32) for ref in (own, far)
    ]
    return jnp.concatenate(parts, axis=1).astype(BF)


def three_parts(value):
    high = value.astype(BF)
    rest = value - high.astype(F32)
    mid = rest.astype(BF)
    return high, mid, (rest - mid.astype(F32)).astype(BF)


def head_mask(head):
    lane = lax.broadcasted_iota(jnp.int32, (1, LANES), 1)
    return (lane // HD) == head


def mask_head(value, head):
    return jnp.where(head_mask(head), value, jnp.zeros_like(value))


def prepare_kernel(
    latents, far_latents, restore, far_restore, position, my_latents, choice, my_position,
    near_buffer, far_buffer, sem,
):
    side = lax.axis_index("blk")
    copies = []
    for index, (source, target) in enumerate(((latents, near_buffer), (far_latents, far_buffer))):
        copies.append(
            pltpu.make_async_copy(source.at[pl.ds(side * MINE, MINE)], target, sem.at[index])
        )
        copies[-1].start()
    my_position[...] = position[...]
    for image in range(MINE):
        choice[image] = select_rows(restore, far_restore, side * MINE + image, side)
    for copy in copies:
        copy.wait()
    half = KMAX // 2
    for image in range(MINE):
        at = image * KMAX
        my_latents[at : at + half, :] = near_buffer[image]
        my_latents[at + half : at + KMAX, :] = far_buffer[image]


def prepare_call(*operands):
    outs = (
        pltpu.VMEM((MINE * KMAX, DIN), BF),
        pltpu.VMEM((MINE, PICKS, SLOTS), BF),
        pltpu.VMEM((SLOTS, D), F32),
    )
    return pl.pallas_call(
        prepare_kernel,
        in_specs=[ANY, ANY, VMEM, VMEM, VMEM],
        out_shape=outs,
        out_specs=tuple(VMEM for _ in outs),
        scratch_shapes=[
            pltpu.VMEM((MINE, KMAX // 2, DIN), BF),
            pltpu.VMEM((MINE, KMAX // 2, DIN), BF),
            pltpu.SemaphoreType.DMA((2,)),
        ],
        compiler_params=pltpu.CompilerParams(vmem_limit_bytes=4 * 2**20),
        cost_estimate=pl.CostEstimate(flops=10**6, bytes_accessed=2**20, transcendentals=0),
    )(*operands)


def forward_kernel(bucket, my_latents, choice, position, vectors, *rest, places):
    pieces = len(rest) - 17
    sources = rest[:pieces]
    (
        probs,
        joint,
        normed,
        start,
        middle,
        mixed,
        embed_w,
        joint_w,
        output_w,
        high_lines,
        lines,
        stage,
        query_t,
        value_t,
        mixed_t,
        sem,
        high_sem,
    ) = rest[pieces:]
    step = pl.program_id(0)
    side = lax.axis_index("blk")

    @pl.when(step == 0)
    def _():
        fetch_lines(places, sources, lines, high_lines, sem, high_sem)
        lines_to_matrix(lines, stage, embed_w, EMBED_AT, DIN, 4, 128)
        lines_to_matrix(lines, stage, joint_w, JOINT_AT, D, 12, 64)
        lines_to_matrix(lines, stage, output_w, OUTPUT_AT, D, 4, 128)
        embedded = (dot(my_latents[...], embed_w[...]) + vectors[0:1, :]).astype(BF)
        token = list(three_parts(vectors[1:2, :]))
        for image in range(MINE):
            rows = slice(image * SLOTS, (image + 1) * SLOTS)
            picked = choice[image]
            value = dot(picked[:KMAX], embedded[image * KMAX : (image + 1) * KMAX, :], (0, 0))
            masked = jnp.broadcast_to(picked[KMAX : KMAX + 1], (16, SLOTS))
            table = jnp.concatenate(token + [jnp.zeros((13, D), BF)], axis=0)
            value = value + dot(masked, table, (0, 0)) + position[...]
            start[rows, :] = value
            hat, _ = norm_parts(value)
            normed[rows, :] = (hat * vectors[2:3, :] + vectors[3:4, :]).astype(BF)
        for part, bias in enumerate((4, None, 5)):
            columns = slice(part * D, (part + 1) * D)
            out = dot(normed[...], joint_w[:, columns])
            if bias is not None:
                out = out + vectors[bias : bias + 1, :]
            joint[:, columns] = out.astype(BF)
        query_t[...] = joint[:, :D].T
        value_t[...] = joint[:, 2 * D :].T

    image = step // GROUPS
    group = step % GROUPS
    rows = pl.ds(pl.multiple_of(image * SLOTS, SLOTS), SLOTS)
    lanes = pl.ds(pl.multiple_of(group * LANES, LANES), LANES)
    keys = joint[rows, pl.ds(pl.multiple_of(D + group * LANES, LANES), LANES)]
    queries = query_t[lanes, rows]
    length = image_length(bucket, side * MINE + image)
    hidden_key = jnp.where(slot_column(side) < length, 0.0, -1e30)
    rate = HD**-0.5 * math.log2(math.e)
    for head in range(GROUP):
        scores = dot(mask_head(keys, head), queries) + hidden_key
        top = jnp.max(scores, axis=0, keepdims=True)
        raised = jnp.exp2((scores - top) * rate)
        low = (raised * (1.0 / jnp.sum(raised, axis=0, keepdims=True))).astype(BF)
        probs[step * GROUP + head] = low
        features = pl.ds(pl.multiple_of(group * LANES + head * HD, HD), HD)
        mixed_t[features, rows] = dot(value_t[features, rows], low).astype(BF)

    @pl.when(step == MINE * GROUPS - 1)
    def _():
        mixed[...] = mixed_t[...].T
        middle[...] = start[...] + dot(mixed[...], output_w[...]) + vectors[6:7, :]


def forward_call(bucket, my_latents, choice, position, vectors, sources, places):
    outs = (
        pltpu.VMEM((MINE * HEADS, SLOTS, SLOTS), BF),
        pltpu.VMEM((TOKENS, 3 * D), BF),
        pltpu.VMEM((TOKENS, D), BF),
        pltpu.VMEM((TOKENS, D), F32),
        pltpu.VMEM((TOKENS, D), F32),
        pltpu.VMEM((TOKENS, D), BF),
        pltpu.VMEM((DIN, D), BF),
        pltpu.VMEM((D, 3 * D), BF),
        pltpu.VMEM((D, D), BF),
        pltpu.VMEM((SECOND_BLOCKS * BLOCK, LANES), BF),
    )
    return pl.pallas_call(
        lambda *refs: forward_kernel(*refs, places=places),
        grid=(MINE * GROUPS,),
        in_specs=[SMEM] + [VMEM] * 4 + [VMEM if places else ANY] * len(sources),
        out_shape=outs,
        out_specs=tuple(VMEM for _ in outs),
        scratch_shapes=[
            pltpu.VMEM((FIRST_BLOCKS * BLOCK, LANES), BF),
            pltpu.VMEM((2, 768, LANES), F32),
            pltpu.VMEM((D, TOKENS), BF),
            pltpu.VMEM((D, TOKENS), BF),
            pltpu.VMEM((D, TOKENS), BF),
            pltpu.SemaphoreType.DMA,
            pltpu.SemaphoreType.DMA,
        ],
        compiler_params=pltpu.CompilerParams(vmem_limit_bytes=16 * 2**20),
        cost_estimate=pl.CostEstimate(
            flops=6 * 10**9, bytes_accessed=16 * 2**20, transcendentals=2 * 10**6
        ),
    )(bucket, my_latents, choice, position, vectors, *sources)


def middle_kernel(
    by_hand, bucket, middle, cotangent, far_cotangent, vectors, lines, *rest
):
    (
        own_out,
        far_out,
        hat,
        scale,
        back_out,
        acc_back,
        head_lines,
        far_lines,
        near_lines,
        expand_out,
        stage,
        expand_w,
        reduce_w,
        normed,
        normed_t,
        acc,
        grads,
    ) = rest
    step = pl.program_id(0)
    side = lax.axis_index("blk")
    base = SECOND_FROM * BLOCK

    @pl.when(step == 0)
    def _():
        value, spread = norm_parts(middle[...])
        hat[...] = value
        scale[...] = jnp.broadcast_to(spread, scale.shape)
        normed[...] = (value * vectors[7:8, :] + vectors[8:9, :]).astype(BF)
        normed_t[...] = normed[...].T
        for image in range(MINE):
            valid = slot_column(side) < image_length(bucket, side * MINE + image)
            half = SLOTS // 2
            for part, ref in enumerate((cotangent, far_cotangent)):
                at = image * SLOTS + part * half
                back_out[at : at + half, :] = jnp.where(
                    valid[part * half : (part + 1) * half, :],
                    ref[side * MINE + image].astype(F32),
                    0.0,
                ).astype(BF)
        acc[...] = jnp.zeros_like(acc)
        acc_back[...] = jnp.zeros_like(acc_back)
        lines_to_matrix(lines, stage, expand_w, EXPAND_AT - base, D, 16, 32)
        lines_to_matrix(lines, stage, reduce_w, REDUCE_AT - base, FF, 4, 128)

    columns = pl.ds(pl.multiple_of(step * TILE, TILE), TILE)
    expand = expand_w[:, columns]
    reduce = reduce_w[columns, :]
    bias = vectors[pl.ds(10 + step // 2, 1), pl.ds(pl.multiple_of((step % 2) * TILE, TILE), TILE)]
    hidden = dot(normed[...], expand) + bias
    density = jnp.exp(hidden * hidden * -0.5) * (1.0 / math.sqrt(2.0 * math.pi))
    below = 0.5 + 0.5 * lax.erf(hidden * math.sqrt(0.5))
    active = (hidden * below).astype(BF)
    back_active = dot(back_out[...], reduce, (1, 1))
    back_hidden = (back_active * (below + hidden * density)).astype(BF)
    acc[...] += dot(active, reduce)
    acc_back[...] += dot(back_hidden, expand, (1, 1))
    grad_reduce = dot(active, back_out[...], (0, 0))
    for j in range(4):
        grads[pl.ds(D * 16 + step * (TILE * 4) + j, TILE, stride=4), :] = grad_reduce[
            :, j * LANES : (j + 1) * LANES
        ]
    grad_expand = dot(normed_t[...], back_hidden)
    for j in range(TILE // LANES):
        grads[pl.ds(step * (TILE // LANES) + j, D, stride=16), :] = grad_expand[
            :, j * LANES : (j + 1) * LANES
        ]
    expand_out[pl.ds(step, 1), :] = total(back_hidden)

    @pl.when(step == TILES - 1)
    def _():
        for image in range(MINE):
            near = slice(image * SLOTS, image * SLOTS + SLOTS // 2)
            far = slice(image * SLOTS + SLOTS // 2, (image + 1) * SLOTS)
            own_out[image] = middle[near, :] + acc[near, :] + vectors[9:10, :]
            far_out[image] = (middle[far, :] + acc[far, :] + vectors[9:10, :]).astype(BF)
        cut = HALF - EXPAND_AT
        head_lines[...] = grads[:cut, :].astype(BF)
        put_blocks(
            by_hand,
            far_lines,
            near_lines,
            lambda q: grads[pl.ds(cut + q * BLOCK, BLOCK), :].astype(BF),
        )


def slot_of(index, by_hand):
    if not by_hand:
        return index
    me = place()
    rel = index ^ (me & 15)
    other = (rel >> 1) & 1
    odd = ((me >> 1) & 1) ^ other
    along_y, along_x, along_z = rel & 1, (rel >> 2) & 1, rel >> 3
    first = jnp.where(odd == 0, along_y, along_x)
    second = jnp.where(odd == 0, along_x, along_y)
    slot = (1 - first) * 4 + (1 - second) * 2 + (1 - along_z)
    return slot + jnp.where(other == 1, 0, 8)


def put_blocks(by_hand, far_lines, near_lines, block_of):
    def body(index, carry):
        slot = slot_of(index, by_hand)
        value = block_of(index)

        @pl.when(slot < 8)
        def _():
            far_lines[pl.ds(pl.multiple_of(slot * BLOCK, 16), BLOCK), :] = value

        @pl.when(slot >= 8)
        def _():
            near_lines[pl.ds(pl.multiple_of((slot - 8) * BLOCK, 16), BLOCK), :] = value

        return carry

    lax.fori_loop(0, 16, body, 0)


def middle_call(by_hand, *operands):
    outs = (
        pltpu.VMEM((MINE, SLOTS // 2, D), F32),
        jax.ShapeDtypeStruct((MINE, SLOTS // 2, D), BF),
        pltpu.VMEM((TOKENS, D), F32),
        pltpu.VMEM((TOKENS, LANES), F32),
        pltpu.VMEM((TOKENS, D), BF),
        pltpu.VMEM((TOKENS, D), F32),
        pltpu.VMEM((HALF - EXPAND_AT, LANES), BF),
        pltpu.VMEM((8 * BLOCK, LANES), BF),
        pltpu.VMEM((8 * BLOCK, LANES), BF),
        pltpu.VMEM((TILES, TILE), F32),
    )
    return pl.pallas_call(
        lambda *refs: middle_kernel(by_hand, *refs),
        grid=(TILES,),
        in_specs=[SMEM] + [VMEM] * (len(operands) - 1),
        out_shape=outs,
        out_specs=tuple(VMEM for _ in outs),
        scratch_shapes=[
            pltpu.VMEM((2, 768, LANES), F32),
            pltpu.VMEM((D, FF), BF),
            pltpu.VMEM((FF, D), BF),
            pltpu.VMEM((TOKENS, D), BF),
            pltpu.VMEM((D, TOKENS), BF),
            pltpu.VMEM((TOKENS, D), F32),
            pltpu.VMEM((2 * D * 16, LANES), F32),
        ],
        compiler_params=pltpu.CompilerParams(vmem_limit_bytes=24 * 2**20),
        cost_estimate=pl.CostEstimate(
            flops=8 * 10**9, bytes_accessed=16 * 2**20, transcendentals=2 * 10**6
        ),
    )(*operands)


def branch_kernel(
    hat, scale, back_out, acc_back, mixed, output_w, vectors,
    back_middle, back_mixed, out_lines, rows_out, out_grads,
):
    grad = acc_back[...]
    rows_out[...] = jnp.zeros_like(rows_out)
    rows_out[1:2, :] = total(grad * hat[...])
    rows_out[2:3, :] = total(grad)
    rows_out[3:4, :] = total(back_out[...])
    back = back_out[...].astype(F32) + norm_back(
        grad, hat[...], scale[:, :1], vectors[7:8, :]
    )
    back_middle[...] = back
    branch = back.astype(BF)
    rows_out[0:1, :] = total(branch)
    back_mixed[...] = dot(branch, output_w[...], (1, 1)).astype(BF)
    grad_output = dot(mixed[...], branch, (0, 0))
    for j in range(4):
        out_grads[pl.ds(j, D, stride=4), :] = grad_output[:, j * LANES : (j + 1) * LANES]
    out_lines[...] = out_grads[...].astype(BF)


def branch_call(hat, scale, back_out, acc_back, mixed, output_w, vectors):
    outs = (
        pltpu.VMEM((TOKENS, D), F32),
        pltpu.VMEM((TOKENS, D), BF),
        pltpu.VMEM((EXPAND_AT - OUTPUT_AT, LANES), BF),
        pltpu.VMEM((8, D), F32),
    )
    return pl.pallas_call(
        branch_kernel,
        in_specs=[VMEM] * 7,
        out_shape=outs,
        out_specs=tuple(VMEM for _ in outs),
        scratch_shapes=[pltpu.VMEM((D * 4, LANES), F32)],
        compiler_params=pltpu.CompilerParams(vmem_limit_bytes=16 * 2**20),
        cost_estimate=pl.CostEstimate(
            flops=2 * 10**9, bytes_accessed=4 * 2**20, transcendentals=0
        ),
    )(hat, scale, back_out, acc_back, mixed, output_w, vectors)


def attention_back_kernel(
    probs, joint, back_mixed, joint_back, key_t, back_t, query_back_t
):
    step = pl.program_id(0)

    @pl.when(step == 0)
    def _():
        key_t[...] = joint[:, D : 2 * D].T
        back_t[...] = back_mixed[...].T

    image = step // GROUPS
    group = step % GROUPS
    rows = pl.ds(pl.multiple_of(image * SLOTS, SLOTS), SLOTS)
    lanes = pl.ds(pl.multiple_of(group * LANES, LANES), LANES)
    queries = joint[rows, lanes]
    values = joint[rows, pl.ds(pl.multiple_of(2 * D + group * LANES, LANES), LANES)]
    back = back_mixed[rows, lanes]
    back_lanes = back_t[lanes, rows]
    key_back = jnp.zeros((SLOTS, LANES), F32)
    value_back = jnp.zeros((SLOTS, LANES), F32)
    for head in range(GROUP):
        low = probs[step * GROUP + head]
        wide = low.astype(F32)
        back_probs = dot(mask_head(values, head), back_lanes)
        pull = jnp.sum(wide * back_probs, axis=0, keepdims=True)
        score_back = (wide * (back_probs - pull) * HD**-0.5).astype(BF)
        value_back = value_back + dot(low, mask_head(back, head))
        key_back = key_back + dot(score_back, mask_head(queries, head))
        features = pl.ds(pl.multiple_of(group * LANES + head * HD, HD), HD)
        query_back_t[features, rows] = dot(key_t[features, rows], score_back).astype(BF)
    joint_back[rows, pl.ds(pl.multiple_of(D + group * LANES, LANES), LANES)] = key_back.astype(BF)
    joint_back[rows, pl.ds(pl.multiple_of(2 * D + group * LANES, LANES), LANES)] = (
        value_back.astype(BF)
    )

    @pl.when(step == MINE * GROUPS - 1)
    def _():
        joint_back[:, :D] = query_back_t[...].T


def attention_back_call(probs, joint, back_mixed):
    return pl.pallas_call(
        attention_back_kernel,
        grid=(MINE * GROUPS,),
        in_specs=[VMEM] * 3,
        out_shape=pltpu.VMEM((TOKENS, 3 * D), BF),
        out_specs=VMEM,
        scratch_shapes=[
            pltpu.VMEM((D, TOKENS), BF),
            pltpu.VMEM((D, TOKENS), BF),
            pltpu.VMEM((D, TOKENS), BF),
        ],
        compiler_params=pltpu.CompilerParams(vmem_limit_bytes=16 * 2**20),
        cost_estimate=pl.CostEstimate(
            flops=8 * 10**9, bytes_accessed=4 * 2**20, transcendentals=0
        ),
    )(probs, joint, back_mixed)


def input_back_kernel(
    by_hand,
    joint_back,
    normed,
    start,
    back_middle,
    my_latents,
    choices,
    vectors,
    embed_w,
    joint_w,
    out_lines,
    head_lines,
    rows_in,
    expand_in,
    far_first,
    near_first,
    far_second,
    near_second,
    rows_out,
    own_latent,
    far_latent,
    grads,
    tails,
):
    rows_out[...] = jnp.zeros_like(rows_out)
    rows_out[4:5, :] = total(joint_back[:, :D])
    rows_out[5:6, :] = total(joint_back[:, 2 * D :])
    normed_t = normed[...].T
    for part in range(3):
        grad_joint = dot(normed_t, joint_back[:, part * D : (part + 1) * D])
        for j in range(4):
            grads[pl.ds(JOINT_AT + part * 4 + j, D, stride=12), :] = grad_joint[
                :, j * LANES : (j + 1) * LANES
            ]
    grad = dot(joint_back[...], joint_w[...], (1, 1))
    hat, scale = norm_parts(start[...])
    rows_out[2:3, :] = total(grad * hat)
    rows_out[3:4, :] = total(grad)
    back_start = back_middle[...] + norm_back(grad, hat, scale, vectors[2:3, :])
    low_start = back_start.astype(BF)
    low_rest = (back_start - low_start.astype(F32)).astype(BF)
    picked = []
    token_back = jnp.zeros((1, D), F32)
    for image in range(MINE):
        part = slice(image * SLOTS, (image + 1) * SLOTS)
        choice = choices[image]
        chosen = dot(choice, low_start[part, :])
        picked.append(chosen[:KMAX, :].astype(BF))
        token_back = token_back + chosen[KMAX : KMAX + 1, :]
        token_back = token_back + dot(choice[KMAX:, :], low_rest[part, :])[:1, :]
    rows_out[1:2, :] = token_back
    embedded_back = jnp.concatenate(picked, axis=0)
    rows_out[0:1, :] = total(embedded_back)
    grad_embed = dot(my_latents[...], embedded_back, (0, 0))
    for j in range(4):
        grads[pl.ds(EMBED_AT + j, DIN, stride=4), :] = grad_embed[:, j * LANES : (j + 1) * LANES]
    latent_back = dot(embedded_back, embed_w[...], (1, 1))
    for image in range(MINE):
        at = image * KMAX
        own_latent[image] = latent_back[at : at + KMAX // 2, :]
        far_latent[image] = latent_back[at + KMAX // 2 : at + KMAX, :].astype(BF)
    rows_out[6:10, :] = rows_in[0:4, :]
    for j in range(4):
        rows_out[10 + j : 11 + j, :TILE] = expand_in[2 * j : 2 * j + 1, :]
        rows_out[10 + j : 11 + j, TILE:] = expand_in[2 * j + 1 : 2 * j + 2, :]
    tails[...] = jnp.zeros_like(tails)
    for row in range(ROWS):
        for j in range(D // LANES):
            tails[row * TAIL + j : row * TAIL + j + 1, :] = rows_out[
                row : row + 1, j * LANES : (j + 1) * LANES
            ]

    def store(index, value):
        slot = slot_of(index, by_hand)
        tail = tails[pl.ds(pl.multiple_of(index * TAIL, TAIL), TAIL), :].astype(BF)

        def put(first, second, at):
            first[pl.ds(pl.multiple_of(at * PART, 16), PART), :] = value[:PART]
            row = pl.multiple_of(at * PARTS[1], 16)
            second[pl.ds(row, PART), :] = value[PART:]
            second[pl.ds(row + PART, TAIL), :] = tail

        @pl.when(slot < 8)
        def _():
            put(far_first, far_second, slot)

        @pl.when(slot >= 8)
        def _():
            put(near_first, near_second, slot - 8)

    first = OUTPUT_AT // BLOCK
    last = -(-EXPAND_AT // BLOCK)

    def early(index, carry):
        store(index, grads[pl.ds(pl.multiple_of(index * BLOCK, 16), BLOCK), :].astype(BF))
        return carry

    def late(index, carry):
        at = pl.multiple_of(index * BLOCK - EXPAND_AT, 16)
        store(index, head_lines[pl.ds(at, BLOCK), :])
        return carry

    lax.fori_loop(0, first, early, 0)
    for index in range(first, last):
        low, high = index * BLOCK, (index + 1) * BLOCK
        parts = []
        if low < OUTPUT_AT:
            parts.append(grads[low:OUTPUT_AT, :].astype(BF))
        parts.append(out_lines[max(low - OUTPUT_AT, 0) : min(high, EXPAND_AT) - OUTPUT_AT, :])
        if high > EXPAND_AT:
            parts.append(head_lines[: high - EXPAND_AT, :])
        store(index, jnp.concatenate(parts, axis=0) if len(parts) > 1 else parts[0])
    lax.fori_loop(last, 16, late, 0)


def input_back_call(by_hand, *operands):
    shape = jax.ShapeDtypeStruct
    outs = (
        pltpu.VMEM((8 * PARTS[0], LANES), BF),
        pltpu.VMEM((8 * PARTS[0], LANES), BF),
        pltpu.VMEM((8 * PARTS[1], LANES), BF),
        pltpu.VMEM((8 * PARTS[1], LANES), BF),
        shape((ROWS, D), F32),
        pltpu.VMEM((MINE, KMAX // 2, DIN), F32),
        shape((MINE, KMAX // 2, DIN), BF),
    )
    return pl.pallas_call(
        lambda *refs: input_back_kernel(by_hand, *refs),
        in_specs=[VMEM] * len(operands),
        out_shape=outs,
        out_specs=tuple(VMEM for _ in outs),
        scratch_shapes=[
            pltpu.VMEM((OUTPUT_AT, LANES), F32),
            pltpu.VMEM((ROWS * TAIL, LANES), F32),
        ],
        compiler_params=pltpu.CompilerParams(vmem_limit_bytes=24 * 2**20),
        cost_estimate=pl.CostEstimate(
            flops=4 * 10**9, bytes_accessed=8 * 2**20, transcendentals=0
        ),
    )(*operands)


class Grid:
    def __init__(self, mesh):
        self.axes = ("dp", "blk")
        self.count = mesh.shape["dp"] * mesh.shape["blk"]
        self.by_hand = self.count == 32 and mesh.shape["blk"] == 2

    def send(self, value, bits, other=None, only=None):
        other = bits if other is None else other
        pairs = [(i, i ^ (other if i & 2 else bits)) for i in range(self.count)]
        if only is not None:
            pairs = [(i, j) for i, j in pairs if (i & 16 == 0) == (only == 0)]
        return lax.ppermute(value, self.axes, pairs)

    def gather(self, block):
        if not self.by_hand:
            whole = lax.all_gather(block, self.axes, axis=0, tiled=True)
            return [whole.reshape(LINES, LANES)], None
        held = {0: block}
        near, side, far = {}, {}, {}

        def plane(k):
            near[k] = self.send(held[k], 4, 1)
            side[k] = self.send(held[k], 1, 4)

        def corner(k):
            far[k] = self.send(near[k], 1, 4)

        held[16] = self.send(block, 16)
        plane(0)
        held[8] = self.send(block, 8)
        corner(0)
        plane(8)
        held[24] = self.send(held[16], 8)
        plane(16)
        corner(16)
        far[8] = self.send(far[0], 8)
        plane(24)
        far[24] = self.send(far[16], 8)
        pieces, places = [], []
        for k in (0, 8, 16, 24):
            for value, even, uneven in (
                (held[k], 0, 0),
                (near[k], 4, 1),
                (side[k], 1, 4),
                (far[k], 5, 5),
            ):
                pieces.append(value)
                places.append((k, even, uneven))
                pieces.append(self.send(value, 2))
                places.append((k ^ 2, uneven, even))
        return [in_vmem(piece) for piece in pieces], tuple(places)


def add_call(rows, *terms):
    def kernel(*refs):
        out = refs[-1]
        value = None
        for ref, (_, at) in zip(refs[:-1], terms, strict=True):
            part = ref[at : at + rows, :].astype(F32)
            value = part if value is None else value + part
        out[...] = value.astype(BF)

    return pl.pallas_call(
        kernel,
        in_specs=[VMEM] * len(terms),
        out_shape=pltpu.VMEM((rows, LANES), BF),
        out_specs=VMEM,
        compiler_params=pltpu.CompilerParams(vmem_limit_bytes=4 * 2**20),
        cost_estimate=pl.CostEstimate(flops=10**5, bytes_accessed=2**20, transcendentals=0),
    )(*(in_vmem(array) for array, _ in terms))


def in_vmem(value):
    return pltpu.with_memory_space_constraint(value, pltpu.VMEM)


class Reduction:
    HOPS = ((2, 2), (1, 4), (4, 1), (8, 8))

    def __init__(self, grid, far_lines, near_lines, half):
        self.grid = grid
        self.near = near_lines
        self.half = half
        self.rows = far_lines.shape[0] // 8
        self.head = far_lines
        self.came = []

    def hop(self, *behind):
        step = len(self.came)
        self.came.append(self.grid.send(self.head, *self.HOPS[step]))
        left = 8 >> (step + 1)
        count = max(left, 1) if step < 3 else 1
        begin = 8 - 2 * left if step < 3 else 7
        terms = [(after(self.near, *behind), begin * self.rows)]
        for level, value in enumerate(self.came):
            terms.append((value, (begin - (8 - (8 >> level))) * self.rows))
        self.head = add_call(count * self.rows, *terms)
        return self.head

    def last(self):
        self.across = self.grid.send(self.head, 16, only=1 - self.half)


def finish_kernel(high, high_far, one, one_far, two, two_far, grad, notes):
    lower = (place() & 16) == 0

    def both(near, far):
        return near[...].astype(F32) + far[...].astype(F32)

    low_one, low_two, upper = both(one, one_far), both(two, two_far), both(high, high_far)
    grad[:PART, :] = jnp.where(lower, low_one, upper[:PART])
    grad[PART:, :] = jnp.where(lower, low_two[:PART], upper[PART:])
    row = jnp.where(lower, low_two[PART:], 0.0)
    value = grad[...]
    square = jnp.sum(jnp.sum(value * value, axis=0, keepdims=True), axis=1, keepdims=True)
    square = square + jnp.sum(jnp.sum(row * row, axis=0, keepdims=True), axis=1, keepdims=True)
    line = lax.broadcasted_iota(jnp.int32, (8, LANES), 0)
    note = jnp.where(line < 4, row[:8], square)
    for device in range(notes.shape[0]):
        notes[device] = note


def finish_call(count, *operands):
    outs = (pltpu.VMEM((BLOCK, LANES), F32), pltpu.VMEM((count, 8, LANES), F32))
    return pl.pallas_call(
        finish_kernel,
        in_specs=[VMEM] * len(operands),
        out_shape=outs,
        out_specs=tuple(VMEM for _ in outs),
        compiler_params=pltpu.CompilerParams(vmem_limit_bytes=8 * 2**20),
        cost_estimate=pl.CostEstimate(flops=10**6, bytes_accessed=2**20, transcendentals=0),
    )(*(in_vmem(value) for value in operands))


def update_kernel(
    grad, notes, first, second, weights, vectors, vector_first, vector_second,
    first_out, second_out, weights_out, vectors_first_out, vectors_second_out, vectors_out,
    bias_out, norm_out, sums,
):
    square = jnp.sum(notes[:, 4, :], axis=0, keepdims=True)
    norm = jnp.sqrt(square)
    factor = jnp.minimum(1.0, clip_norm / (norm + 1e-06))
    norm_out[...] = norm
    for row in range(sums.shape[0]):
        for j in range(D // LANES):
            sums[row : row + 1, j * LANES : (j + 1) * LANES] = notes[row, j : j + 1, :]
    first_out[...], second_out[...], weights_out[...] = adam_update(
        grad[...] * factor, first[...], second[...], weights[...], learn_rate, decay_weight
    )
    clipped = sums[...] * jnp.concatenate([factor] * (D // LANES), axis=1)
    bias_out[...] = clipped[9:10, :]
    vectors_first_out[...], vectors_second_out[...], vectors_out[...] = adam_update(
        clipped, vector_first[...], vector_second[...], vectors[...], vector_rate, 0.0
    )


def update_call(*operands):
    shape = jax.ShapeDtypeStruct
    lines, rows = operands[2].shape, operands[5].shape
    outs = (
        [shape(lines, F32)] * 3
        + [shape(rows, F32)] * 3
        + [shape((1, rows[1]), F32), shape((1, LANES), F32)]
    )
    return pl.pallas_call(
        update_kernel,
        in_specs=[VMEM] * len(operands),
        out_shape=outs,
        out_specs=[VMEM for _ in outs],
        scratch_shapes=[pltpu.VMEM(rows, F32)],
        compiler_params=pltpu.CompilerParams(vmem_limit_bytes=12 * 2**20),
        cost_estimate=pl.CostEstimate(flops=10**7, bytes_accessed=2**22, transcendentals=10**6),
    )(*operands)


def after(value, *others):
    if not others:
        return value
    return lax.optimization_barrier((value, *others))[0]


def local(
    grid,
    latents,
    restore,
    bucket,
    cotangent,
    flat_weights,
    flat_first,
    flat_second,
    vectors,
    vector_first,
    vector_second,
):
    side = lax.axis_index("blk").astype(jnp.int32)
    by_hand = grid.by_hand

    def trade(value):
        return lax.ppermute(value, "blk", [(0, 1), (1, 0)])

    pieces, places = grid.gather(flat_weights.reshape(-1, LANES).astype(BF))
    slot = (jnp.arange(SLOTS, dtype=jnp.int32) + side * (SLOTS // 2)) & (SLOTS - 1)
    position = position_rows(slot)
    my_latents, choice, my_position = prepare_call(
        latents, trade(after(latents, pieces[0])), restore, trade(after(restore, pieces[0])), position
    )
    far_cotangent = trade(after(cotangent, *pieces[-2:]))
    (
        probs, joint, normed, start, middle, mixed, embed_w, joint_w, output_w, high_lines,
    ) = forward_call(bucket, my_latents, choice, my_position, vectors, pieces, places)
    (
        own_out, far_out, hat, scale, back_out, acc_back, head_lines, far_high, near_high, expand_b,
    ) = middle_call(by_hand, bucket, middle, cotangent, far_cotangent, vectors, high_lines)
    if by_hand:
        high = Reduction(grid, far_high, near_high, 1)
    back_middle, back_mixed, out_lines, rows_b = branch_call(
        hat, scale, back_out, acc_back, mixed, output_w, vectors
    )
    if by_hand:
        back_mixed = after(back_mixed, high.hop(back_mixed))
    joint_back = attention_back_call(probs, joint, back_mixed)
    if by_hand:
        joint_back = after(joint_back, high.hop(joint_back))
    far_one, near_one, far_two, near_two, rows_c, own_latent, far_latent = input_back_call(
        by_hand, joint_back, normed, start, back_middle, my_latents, choice,
        vectors, embed_w, joint_w, out_lines, head_lines, rows_b, expand_b,
    )
    if by_hand:
        one = Reduction(grid, far_one, near_one, 0)
        two = Reduction(grid, far_two, near_two, 0)
        mark = high.hop(far_one)
        mark = one.hop(mark)
        mark = two.hop(mark)
        mark = high.hop(mark)
        high.last()
        for _ in range(3):
            mark = one.hop(mark)
            mark = two.hop(mark)
        one.last()
        two.last()
        far_out = after(far_out, mark)
        far_latent = after(far_latent, mark)

    def join(own, far):
        other = trade(far).astype(F32)
        return jnp.where(
            side == 0,
            jnp.concatenate([own, other], axis=0),
            jnp.concatenate([other, own], axis=0),
        )

    block_out = join(own_out, far_out)
    latent_out = join(own_latent, far_latent)

    if by_hand:
        grad, notes = finish_call(
            grid.count, high.head, high.across, one.head, one.across, two.head, two.across
        )
        notes = lax.all_to_all(notes, grid.axes, 0, 0, tiled=True)
        lines = [value.reshape(-1, LANES) for value in (flat_first, flat_second, flat_weights)]
        outs = update_call(grad, notes, *lines, vectors, vector_first, vector_second)
        return (
            block_out,
            latent_out,
            *(value.reshape(-1) for value in outs[:3]),
            *outs[3:6],
            outs[6].reshape(-1),
            outs[7][0, 0],
        )

    low = [
        jnp.concatenate([far, near], axis=0).reshape(16, -1, LANES)[:, :PART]
        for far, near in ((far_one, near_one), (far_two, near_two))
    ]
    flat = jnp.concatenate(
        [jnp.concatenate(low, axis=1).reshape(-1), far_high.reshape(-1), near_high.reshape(-1)]
    )
    shard_grad = lax.psum_scatter(flat, grid.axes, scatter_dimension=0, tiled=True)
    shard_grad = shard_grad.astype(F32).reshape(-1, LANES)
    vector_sum = lax.psum(rows_c[: vectors.shape[0]], grid.axes)
    square_sum = lax.psum(jnp.sum(shard_grad * shard_grad), grid.axes)
    grad_norm = jnp.sqrt(square_sum + jnp.sum(vector_sum * vector_sum))
    factor = jnp.minimum(1.0, clip_norm / (grad_norm + 1e-06))
    new_first, new_second, new_weights = adam_update(
        shard_grad.reshape(-1) * factor,
        flat_first,
        flat_second,
        flat_weights,
        learn_rate,
        decay_weight,
    )
    vector_first_new, vector_second_new, vectors_new = adam_update(
        vector_sum * factor, vector_first, vector_second, vectors, vector_rate, 0.0
    )
    reduce_bias_grad = vector_sum[9] * factor
    return (
        block_out,
        latent_out,
        new_first,
        new_second,
        new_weights,
        vector_first_new,
        vector_second_new,
        vectors_new,
        reduce_bias_grad,
        grad_norm,
    )


def solution(mesh):
    grid = Grid(mesh)
    return jax.shard_map(
        lambda *args: local(grid, *args),
        mesh=mesh,
        in_specs=(
            P("dp", "blk", None),
            P("dp", "blk"),
            P("dp"),
            P("dp", "blk", None),
            P(("dp", "blk")),
            P(("dp", "blk")),
            P(("dp", "blk")),
            P(),
            P(),
            P(),
        ),
        out_specs=(
            P("dp", "blk", None),
            P("dp", "blk", None),
            P(("dp", "blk")),
            P(("dp", "blk")),
            P(("dp", "blk")),
            P(),
            P(),
            P(),
            P(),
            P(),
        ),
        check_vma=False,
    )
```

time: 228 us -> 174 us (0.76)
  starting transfers between devices: 73.8 us -> 49.8 us
  other arithmetic: 17.2 us -> 5.06 us
  Pallas kernels: 62.2 us -> 52.5 us
  between operations: 7.19 us -> 1.21 us
    ppermute x55 -> x46, starting transfers between devices: 66.5 us -> 41.5 us  [send(): return lax.ppermute(value, self.axes, pairs)]
    pallas_call x3 -> x20, Pallas kernels: 62.2 us -> 52.5 us  [the longest x1 17.3 us: forward_call(): pl.pallas_call(lambda *refs: forward_kernel(*refs, places=places), grid=(...]
    all_to_all x0 -> x1, waiting for transfers between devices: none -> 5.67 us  [local(): notes = lax.all_to_all(notes, grid.axes, 0, 0, tiled=True)]
    ppermute x55 -> x46, waiting for transfers between devices: 55.3 us -> 50.6 us  [send(): return lax.ppermute(value, self.axes, pairs)]
    concatenate x4 -> x0, other arithmetic: 2.81 us -> none  [the longest x2 1.5 us: trade(): jnp.concatenate([mine(value), lax.ppermute(sent, 'blk', swap)], axis=1)]
    all_to_all x0 -> x1, starting transfers between devices: none -> 2.78 us  [local(): notes = lax.all_to_all(notes, grid.axes, 0, 0, tiled=True)]
  transfers between devices with their start and end apart: 60 -> 52, of which waited for: 29 -> 21; matrix products, arithmetic and copies ran while one was open for 7% -> 2% of each run, Pallas kernels for 0% -> 18%
where the time goes in v2:
time: 174 us; the launch traced here: 173 us
  waiting for transfers between devices  60.8 us (35%)
  Pallas kernels  52.5 us (30%)
  starting transfers between devices  49.8 us (29%)
  other arithmetic  5.06 us (3%)
  local copies, waits for them, and re-layouts  4.04 us (2%)
    ppermute x46, waiting for transfers between devices, send(): return lax.ppermute(value, self.axes, pairs)  50.6 us
    ppermute x46, starting transfers between devices, send(): return lax.ppermute(value, self.axes, pairs)  41.5 us
    pallas_call x1, Pallas kernels, forward_call(): pl.pallas_call(lambda *refs: forward_kernel(*refs, places=places), grid=(...  17.3 us
    pallas_call x1, Pallas kernels, middle_call(): pl.pallas_call(lambda *refs: middle_kernel(by_hand, *refs), grid=(TILES,)...  14.5 us
    pallas_call x1, Pallas kernels, attention_back_call(): pl.pallas_call(attention_back_kernel, grid=(MINE * GROUPS,), in_specs=[VM...  10.2 us
    all_to_all x1, waiting for transfers between devices, local(): notes = lax.all_to_all(notes, grid.axes, 0, 0, tiled=True)  5.67 us
    ppermute x5, starting transfers between devices, trade(): return lax.ppermute(value, 'blk', [(0, 1), (1, 0)])  5.54 us
    pallas_call x1, Pallas kernels, input_back_call(): pl.pallas_call(lambda *refs: input_back_kernel(by_hand, *refs), in_specs=...  4.67 us
  transfers between devices with their start and end apart: 52, of which 21 were waited for; matrix products, arithmetic and copies ran while one was open for 2% of the time, Pallas kernels for 18%

profile of v2, /device:TPU:0, one launch (start us, length us, event | category | flops | bytes accessed | tf_op | source)
XLA Modules:
  0.0 173.4 jit_solution(17216724988226802484)
XLA Ops:
  1.8 4.1 %collective-permute-start.17 = (bf16[864,128]{1,0:T(8,128)(2,1)S(1)}, bf16[864,128]{1,0:T(8,128)(2,1)S(1)}, u32[]{:S(2)}, u32[]{:S(2)}) collective-permute-start(bf16[864,128]{1,0:T(8,128)(2,1)S(1)} %bitcast_convert_fusion.refs_5_), channel_id=1, source_target_pairs={{0,16},{1,17},{2,18},{3,19},{4,20},{5,21},{6,22},{7,23},{8,24},{9,... | collective-permute-start | bytes 663560 | tf_op jit(solution)/shard_map/ppermute | solution.py:750
  7.9 1.6 collective-permute-start.9
  14.0 2.2 %collective-permute-done.17.refs_21_ = bf16[864,128]{1,0:T(8,128)(2,1)S(1)} collective-permute-done((bf16[864,128]{1,0:T(8,128)(2,1)S(1)}, bf16[864,128]{1,0:T(8,128)(2,1)S(1)}, u32[]{:S(2)}, u32[]{:S(2)}) %collective-permute-start.17) | collective-permute-done | bytes 221216 | tf_op jit(solution)/shard_map/ppermute | solution.py:750
  17.8 1.6 collective-permute-start.21
  24.1 1.7 collective-permute-done.21.refs_25_
  37.5 3.5 %collective-permute-done.29.refs_33_ = bf16[864,128]{1,0:T(8,128)(2,1)} collective-permute-done((bf16[864,128]{1,0:T(8,128)(2,1)S(1)}, bf16[864,128]{1,0:T(8,128)(2,1)}, u32[]{:S(2)}, u32[]{:S(2)}) %collective-permute-start.29) | collective-permute-done | bytes 221216 | tf_op jit(solution)/shard_map/ppermute | solution.py:750
  42.1 1.9 %collective-permute-done.31.refs_35_ = bf16[864,128]{1,0:T(8,128)(2,1)} collective-permute-done((bf16[864,128]{1,0:T(8,128)(2,1)}, bf16[864,128]{1,0:T(8,128)(2,1)}, u32[]{:S(2)}, u32[]{:S(2)}) %collective-permute-start.31) | collective-permute-done | bytes 221216 | tf_op jit(solution)/shard_map/ppermute | solution.py:750
  45.1 4.4 %collective-permute-done.15.refs_19_ = bf16[864,128]{1,0:T(8,128)(2,1)S(1)} collective-permute-done((bf16[864,128]{1,0:T(8,128)(2,1)}, bf16[864,128]{1,0:T(8,128)(2,1)S(1)}, u32[]{:S(2)}, u32[]{:S(2)}) %collective-permute-start.15) | collective-permute-done | bytes 221216 | tf_op jit(solution)/shard_map/ppermute | solution.py:750
  55.0 17.3 %shard_map.178 = (bf16[32,256,256]{2,1,0:T(8,128)(2,1)S(1)}, bf16[512,1536]{1,0:T(8,128)(2,1)S(1)}, bf16[512,512]{1,0:T(8,128)(2,1)S(1)}, f32[512,512]{1,0:T(8,1...) custom-call(s32[4]{0:T(128)S(1)} %copy-done.23, ...), custom_call_target="tpu_custom_call" | custom-call | flops 6000000000 | bytes 16777216 | tf_op jit(solution)/shard_map/pallas_call | solution.py:317
  72.3 14.5 %shard_map.179 = (f32[2,128,512]{2,1,0:T(8,128)S(1)}, bf16[2,128,512]{2,1,0:T(8,128)(2,1)S(1)}, f32[512,512]{1,0:T(8,128)S(1)}, f32[512,128]{1,0:T(8,128)S(1)}, ...) custom-call(s32[4]{0:T(128)S(1)} %copy-done.23, ...), custom_call_target="tpu_custom_call" | custom-call | flops 8000000000 | bytes 16777216 | tf_op jit(solution)/shard_map/pallas_call | solution.py:473
  88.4 2.2 %collective-permute-done.34.refs_1_ = bf16[6912,128]{1,0:T(8,128)(2,1)S(1)} collective-permute-done((bf16[6912,128]{1,0:T(8,128)(2,1)S(1)}, bf16[6912,128]{1,0:T(8,128)(2,1)S(1)}, u32[]{:S(2)}, u32[]{:S(2)}) %collective-permute-start.34) | collective-permute-done | bytes 1769504 | tf_op jit(solution)/shard_map/ppermute | solution.py:750
  91.7 10.2 %shard_map.182.refs_0_ = bf16[512,1536]{1,0:T(8,128)(2,1)S(1)} custom-call(bf16[32,256,256]{2,1,0:T(8,128)(2,1)S(1)} %get-tuple-element.82.probs, bf16[512,1536]{1,0:T(8,128)(2,1)S(1)} %get-tuple-element.83.joint, bf16[512,512]{1,0:T(8,128)(2,1)S(1)} %get-tuple-element.94.back_mixed), custom_call_target="tpu_custom_call" | custom-call | flops 8000000000 | bytes 4194304 | tf_op jit(solution)/shard_map/pallas_call | solution.py:578
  101.8 2.1 %collective-permute-done.35.refs_2_ = bf16[3456,128]{1,0:T(8,128)(2,1)S(1)} collective-permute-done((bf16[3456,128]{1,0:T(8,128)(2,1)S(1)}, bf16[3456,128]{1,0:T(8,128)(2,1)S(1)}, u32[]{:S(2)}, u32[]{:S(2)}) %collective-permute-start.35) | collective-permute-done | bytes 884768 | tf_op jit(solution)/shard_map/ppermute | solution.py:750
  104.1 4.7 %shard_map.184 = (bf16[3456,128]{1,0:T(8,128)(2,1)S(1)}, bf16[3456,128]{1,0:T(8,128)(2,1)S(1)}, bf16[3584,128]{1,0:T(8,128)(2,1)S(1)}, bf16[3584,128]{1,0:T(8,12...) custom-call(bf16[512,1536]{1,0:T(8,128)(2,1)S(1)} %shard_map.182.refs_0_, ...), custom_call_target="tpu_custom_call" | custom-call | flops 4000000000 | bytes 8388608 | tf_op jit(solution)/shard_map/pallas_call | solution.py:723
  110.3 7.3 %collective-permute-done.36.refs_3_ = bf16[1728,128]{1,0:T(8,128)(2,1)S(1)} collective-permute-done((bf16[1728,128]{1,0:T(8,128)(2,1)S(1)}, bf16[1728,128]{1,0:T(8,128)(2,1)S(1)}, u32[]{:S(2)}, u32[]{:S(2)}) %collective-permute-start.36) | collective-permute-done | bytes 442400 | tf_op jit(solution)/shard_map/ppermute | solution.py:750
  121.3 4.7 %collective-permute-done.39.refs_4_ = bf16[864,128]{1,0:T(8,128)(2,1)S(1)} collective-permute-done((bf16[864,128]{1,0:T(8,128)(2,1)S(1)}, bf16[864,128]{1,0:T(8,128)(2,1)S(1)}, u32[]{:S(2)}, u32[]{:S(2)}) %collective-permute-start.39) | collective-permute-done | bytes 221216 | tf_op jit(solution)/shard_map/ppermute | solution.py:750
  126.1 5.1 %collective-permute-done.40.refs_2_ = bf16[1728,128]{1,0:T(8,128)(2,1)S(1)} collective-permute-done((bf16[1728,128]{1,0:T(8,128)(2,1)S(1)}, bf16[1728,128]{1,0:T(8,128)(2,1)S(1)}, u32[]{:S(2)}, u32[]{:S(2)}) %collective-permute-start.40) | collective-permute-done | bytes 442400 | tf_op jit(solution)/shard_map/ppermute | solution.py:750
  133.5 6.4 %collective-permute-done.42.refs_3_ = bf16[864,128]{1,0:T(8,128)(2,1)S(1)} collective-permute-done((bf16[864,128]{1,0:T(8,128)(2,1)S(1)}, bf16[864,128]{1,0:T(8,128)(2,1)S(1)}, u32[]{:S(2)}, u32[]{:S(2)}) %collective-permute-start.42) | collective-permute-done | bytes 221216 | tf_op jit(solution)/shard_map/ppermute | solution.py:750
  142.1 5.2 %collective-permute-start.48 = (bf16[864,128]{1,0:T(8,128)(2,1)S(1)}, bf16[864,128]{1,0:T(8,128)(2,1)S(1)}, u32[]{:S(2)}, u32[]{:S(2)}) collective-permute-start(bf16[864,128]{1,0:T(8,128)(2,1)S(1)} %shard_map.188.high), channel_id=1, source_target_pairs={{0,16},{1,17},{2,18},{3,19},{4,20},{5,21},{6,22},{7,23},{8,24},{9,... | collective-permute-start | bytes 663560 | tf_op jit(solution)/shard_map/ppermute | solution.py:750
  150.6 1.6 collective-permute-start.47
  152.2 3.1 %collective-permute-done.47 = bf16[2,32,768]{2,1,0:T(8,128)(2,1)S(1)} collective-permute-done((bf16[2,32,768]{2,1,0:T(8,128)(2,1)S(1)}, bf16[2,32,768]{2,1,0:T(8,128)(2,1)S(1)}, u32[]{:S(2)}, u32[]{:S(2)}) %collective-permute-start.47) | collective-permute-done | bytes 98336 | tf_op jit(solution)/shard_map/ppermute | solution.py:937
  155.3 4.0 %collective-permute-done.49.one_far = bf16[432,128]{1,0:T(8,128)(2,1)S(1)} collective-permute-done((bf16[432,128]{1,0:T(8,128)(2,1)S(1)}, bf16[432,128]{1,0:T(8,128)(2,1)S(1)}, u32[]{:S(2)}, u32[]{:S(2)}) %collective-permute-start.49) | collective-permute-done | bytes 110624 | tf_op jit(solution)/shard_map/ppermute | solution.py:750
  160.4 2.8 %all-to-all-start = ((f32[32,8,128]{2,1,0:T(8,128)}), f32[32,8,128]{2,1,0:T(8,128)S(1)}, u32[]{:S(2)}, u32[]{:S(2)}) async-start(f32[32,8,128]{2,1,0:T(8,128)} %get-tuple-element.125), calls=%async_computation | async-start | bytes 262144 | tf_op jit(solution)/shard_map/all_to_all | solution.py:997
  166.2 5.7 %all-to-all-done.notes = f32[32,8,128]{2,1,0:T(8,128)S(1)} async-done(((f32[32,8,128]{2,1,0:T(8,128)}), f32[32,8,128]{2,1,0:T(8,128)S(1)}, u32[]{:S(2)}, u32[]{:S(2)}) %all-to-all-start) | async-done | bytes 131104 | tf_op jit(solution)/shard_map/all_to_all | solution.py:997
  (157 shorter events, 54.5 us)
Async XLA Ops:
  1.8 14.4 %collective-permute-start.17 = (bf16[864,128]{1,0:T(8,128)(2,1)S(1)}, bf16[864,128]{1,0:T(8,128)(2,1)S(1)}, u32[]{:S(2)}, u32[]{:S(2)}) collective-permute-start(bf16[864,128]{1,0:T(8,128)(2,1)S(1)} %bitcast_convert_fusion.refs_5_), channel_id=1, source_target_pairs={{0,16},{1,17},{2,18},{3,19},{4,20},{5,21},{6,22},{7,23},{8,24},{9,... | collective-permute-start | bytes 663560 | tf_op jit(solution)/shard_map/ppermute | solution.py:750
  5.9 8.1 %collective-permute-start = (bf16[4,32,768]{2,1,0:T(8,128)(2,1)}, bf16[4,32,768]{2,1,0:T(8,128)(2,1)S(1)}, u32[]{:S(2)}, u32[]{:S(2)}) collective-permute-start(bf16[4,32,768]{2,1,0:T(8,128)(2,1)} %latents.1), channel_id=1, source_target_pairs={{0,1},{1,0},{2,3},{3,2},{4,5},{5,4},{6,7},{7,6},{8,9},{9,8},{10,11... | collective-permute-start | bytes 589832 | tf_op jit(solution)/shard_map/ppermute | solution.py:937
  7.9 9.9 %collective-permute-start.9 = (bf16[864,128]{1,0:T(8,128)(2,1)S(1)}, bf16[864,128]{1,0:T(8,128)(2,1)S(1)}, u32[]{:S(2)}, u32[]{:S(2)}) collective-permute-start(bf16[864,128]{1,0:T(8,128)(2,1)S(1)} %bitcast_convert_fusion.refs_5_), channel_id=1, source_target_pairs={{0,8},{1,9},{2,10},{3,11},{4,12},{5,13},{6,14},{7,15},{8,0},{9,1},... | collective-permute-start | bytes 663560 | tf_op jit(solution)/shard_map/ppermute | solution.py:750
  9.5 10.0 %collective-permute-start.5 = (bf16[864,128]{1,0:T(8,128)(2,1)S(1)}, bf16[864,128]{1,0:T(8,128)(2,1)S(1)}, u32[]{:S(2)}, u32[]{:S(2)}) collective-permute-start(bf16[864,128]{1,0:T(8,128)(2,1)S(1)} %bitcast_convert_fusion.refs_5_), channel_id=1, source_target_pairs={{0,1},{1,0},{2,6},{3,7},{4,5},{5,4},{6,2},{7,3},{8,9},{9,8},{10,14... | collective-permute-start | bytes 663560 | tf_op jit(solution)/shard_map/ppermute | solution.py:750
  12.5 8.5 %collective-permute-start.3 = (bf16[864,128]{1,0:T(8,128)(2,1)S(1)}, bf16[864,128]{1,0:T(8,128)(2,1)S(1)}, u32[]{:S(2)}, u32[]{:S(2)}) collective-permute-start(bf16[864,128]{1,0:T(8,128)(2,1)S(1)} %bitcast_convert_fusion.refs_5_), channel_id=1, source_target_pairs={{0,4},{1,5},{2,3},{3,2},{4,0},{5,1},{6,7},{7,6},{8,12},{9,13},{10,... | collective-permute-start | bytes 663560 | tf_op jit(solution)/shard_map/ppermute | solution.py:750
  17.8 8.0 %collective-permute-start.21 = (bf16[864,128]{1,0:T(8,128)(2,1)S(1)}, bf16[864,128]{1,0:T(8,128)(2,1)S(1)}, u32[]{:S(2)}, u32[]{:S(2)}) collective-permute-start(bf16[864,128]{1,0:T(8,128)(2,1)S(1)} %collective-permute-done.17.refs_21_), channel_id=1, source_target_pairs={{0,1},{1,0},{2,6},{3,7},{4,5},{5,4},{6,2},{7,3},{8,9},{9,8},{10,14... | collective-permute-start | bytes 663560 | tf_op jit(solution)/shard_map/ppermute | solution.py:750
  21.0 8.9 %collective-permute-start.13 = (bf16[864,128]{1,0:T(8,128)(2,1)S(1)}, bf16[864,128]{1,0:T(8,128)(2,1)S(1)}, u32[]{:S(2)}, u32[]{:S(2)}) collective-permute-start(bf16[864,128]{1,0:T(8,128)(2,1)S(1)} %collective-permute-done.9.refs_13_), channel_id=1, source_target_pairs={{0,1},{1,0},{2,6},{3,7},{4,5},{5,4},{6,2},{7,3},{8,9},{9,8},{10,14... | collective-permute-start | bytes 663560 | tf_op jit(solution)/shard_map/ppermute | solution.py:750
  26.8 8.3 %collective-permute-start.7 = (bf16[864,128]{1,0:T(8,128)(2,1)S(1)}, bf16[864,128]{1,0:T(8,128)(2,1)S(1)}, u32[]{:S(2)}, u32[]{:S(2)}) collective-permute-start(bf16[864,128]{1,0:T(8,128)(2,1)S(1)} %collective-permute-done.3.refs_7_), channel_id=1, source_target_pairs={{0,1},{1,0},{2,6},{3,7},{4,5},{5,4},{6,2},{7,3},{8,9},{9,8},{10,14... | collective-permute-start | bytes 663560 | tf_op jit(solution)/shard_map/ppermute | solution.py:750
  32.2 8.8 %collective-permute-start.29 = (bf16[864,128]{1,0:T(8,128)(2,1)S(1)}, bf16[864,128]{1,0:T(8,128)(2,1)}, u32[]{:S(2)}, u32[]{:S(2)}) collective-permute-start(bf16[864,128]{1,0:T(8,128)(2,1)S(1)} %collective-permute-done.25.refs_29_), channel_id=1, source_target_pairs={{0,1},{1,0},{2,6},{3,7},{4,5},{5,4},{6,2},{7,3},{8,9},{9,8},{10,14... | collective-permute-start | bytes 663560 | tf_op jit(solution)/shard_map/ppermute | solution.py:750
  44.6 8.5 %collective-permute-start.24 = (bf16[864,128]{1,0:T(8,128)(2,1)}, bf16[864,128]{1,0:T(8,128)(2,1)S(1)}, u32[]{:S(2)}, u32[]{:S(2)}) collective-permute-start(bf16[864,128]{1,0:T(8,128)(2,1)} %collective-permute-done.23.refs_27_), channel_id=1, source_target_pairs={{0,2},{1,3},{2,0},{3,1},{4,6},{5,7},{6,4},{7,5},{8,10},{9,11},{10,... | collective-permute-start | bytes 663560 | tf_op jit(solution)/shard_map/ppermute | solution.py:750
  44.7 8.4 %collective-permute-start.30 = (bf16[864,128]{1,0:T(8,128)(2,1)}, bf16[864,128]{1,0:T(8,128)(2,1)S(1)}, u32[]{:S(2)}, u32[]{:S(2)}) collective-permute-start(bf16[864,128]{1,0:T(8,128)(2,1)} %collective-permute-done.29.refs_33_), channel_id=1, source_target_pairs={{0,2},{1,3},{2,0},{3,1},{4,6},{5,7},{6,4},{7,5},{8,10},{9,11},{10,... | collective-permute-start | bytes 663560 | tf_op jit(solution)/shard_map/ppermute | solution.py:750
  51.7 20.7 %collective-permute-start.33 = (bf16[4,128,512]{2,1,0:T(8,128)(2,1)S(1)}, bf16[4,128,512]{2,1,0:T(8,128)(2,1)S(1)}, u32[]{:S(2)}, u32[]{:S(2)}) collective-permute-start(bf16[4,128,512]{2,1,0:T(8,128)(2,1)S(1)} %copy-done.8), channel_id=1, source_target_pairs={{0,1},{1,0},{2,3},{3,2},{4,5},{5,4},{6,7},{7,6},{8,9},{9,8},{10,11... | collective-permute-start | bytes 1572872 | tf_op jit(solution)/shard_map/ppermute | solution.py:937
  90.8 13.1 %collective-permute-start.35 = (bf16[3456,128]{1,0:T(8,128)(2,1)S(1)}, bf16[3456,128]{1,0:T(8,128)(2,1)S(1)}, u32[]{:S(2)}, u32[]{:S(2)}) collective-permute-start(bf16[3456,128]{1,0:T(8,128)(2,1)S(1)} %shard_map.181), channel_id=1, source_target_pairs={{0,1},{1,0},{2,6},{3,7},{4,5},{5,4},{6,2},{7,3},{8,9},{9,8},{10,14... | collective-permute-start | bytes 2654216 | tf_op jit(solution)/shard_map/ppermute | solution.py:750
  108.8 9.1 %collective-permute-start.38 = (bf16[3584,128]{1,0:T(8,128)(2,1)S(1)}, bf16[3584,128]{1,0:T(8,128)(2,1)S(1)}, u32[]{:S(2)}, u32[]{:S(2)}) collective-permute-start(bf16[3584,128]{1,0:T(8,128)(2,1)S(1)} %get-tuple-element.112), channel_id=1, source_target_pairs={{0,2},{1,3},{2,0},{3,1},{4,6},{5,7},{6,4},{7,5},{8,10},{9,11},{10,... | collective-permute-start | bytes 2752520 | tf_op jit(solution)/shard_map/ppermute | solution.py:750
  108.8 8.9 %collective-permute-start.37 = (bf16[3456,128]{1,0:T(8,128)(2,1)S(1)}, bf16[3456,128]{1,0:T(8,128)(2,1)S(1)}, u32[]{:S(2)}, u32[]{:S(2)}) collective-permute-start(bf16[3456,128]{1,0:T(8,128)(2,1)S(1)} %get-tuple-element.108), channel_id=1, source_target_pairs={{0,2},{1,3},{2,0},{3,1},{4,6},{5,7},{6,4},{7,5},{8,10},{9,11},{10,... | collective-permute-start | bytes 2654216 | tf_op jit(solution)/shard_map/ppermute | solution.py:750
  109.3 8.3 %collective-permute-start.36 = (bf16[1728,128]{1,0:T(8,128)(2,1)S(1)}, bf16[1728,128]{1,0:T(8,128)(2,1)S(1)}, u32[]{:S(2)}, u32[]{:S(2)}) collective-permute-start(bf16[1728,128]{1,0:T(8,128)(2,1)S(1)} %shard_map.183), channel_id=1, source_target_pairs={{0,4},{1,5},{2,3},{3,2},{4,0},{5,1},{6,7},{7,6},{8,12},{9,13},{10,... | collective-permute-start | bytes 1327112 | tf_op jit(solution)/shard_map/ppermute | solution.py:750
  118.0 13.4 %collective-permute-start.41 = (bf16[1792,128]{1,0:T(8,128)(2,1)S(1)}, bf16[1792,128]{1,0:T(8,128)(2,1)S(1)}, u32[]{:S(2)}, u32[]{:S(2)}) collective-permute-start(bf16[1792,128]{1,0:T(8,128)(2,1)S(1)} %shard_map.187), channel_id=1, source_target_pairs={{0,1},{1,0},{2,6},{3,7},{4,5},{5,4},{6,2},{7,3},{8,9},{9,8},{10,14... | collective-permute-start | bytes 1376264 | tf_op jit(solution)/shard_map/ppermute | solution.py:750
  118.8 12.5 %collective-permute-start.40 = (bf16[1728,128]{1,0:T(8,128)(2,1)S(1)}, bf16[1728,128]{1,0:T(8,128)(2,1)S(1)}, u32[]{:S(2)}, u32[]{:S(2)}) collective-permute-start(bf16[1728,128]{1,0:T(8,128)(2,1)S(1)} %shard_map.186), channel_id=1, source_target_pairs={{0,1},{1,0},{2,6},{3,7},{4,5},{5,4},{6,2},{7,3},{8,9},{9,8},{10,14... | collective-permute-start | bytes 1327112 | tf_op jit(solution)/shard_map/ppermute | solution.py:750
  131.4 8.5 %collective-permute-start.43 = (bf16[896,128]{1,0:T(8,128)(2,1)S(1)}, bf16[896,128]{1,0:T(8,128)(2,1)S(1)}, u32[]{:S(2)}, u32[]{:S(2)}) collective-permute-start(bf16[896,128]{1,0:T(8,128)(2,1)S(1)} %shard_map.190), channel_id=1, source_target_pairs={{0,4},{1,5},{2,3},{3,2},{4,0},{5,1},{6,7},{7,6},{8,12},{9,13},{10,... | collective-permute-start | bytes 688136 | tf_op jit(solution)/shard_map/ppermute | solution.py:750
  142.1 13.2 %collective-permute-start.48 = (bf16[864,128]{1,0:T(8,128)(2,1)S(1)}, bf16[864,128]{1,0:T(8,128)(2,1)S(1)}, u32[]{:S(2)}, u32[]{:S(2)}) collective-permute-start(bf16[864,128]{1,0:T(8,128)(2,1)S(1)} %shard_map.188.high), channel_id=1, source_target_pairs={{0,16},{1,17},{2,18},{3,19},{4,20},{5,21},{6,22},{7,23},{8,24},{9,... | collective-permute-start | bytes 663560 | tf_op jit(solution)/shard_map/ppermute | solution.py:750
  147.5 16.6 %collective-permute-start.46 = (bf16[2,128,512]{2,1,0:T(8,128)(2,1)S(1)}, bf16[2,128,512]{2,1,0:T(8,128)(2,1)}, u32[]{:S(2)}, u32[]{:S(2)}) collective-permute-start(bf16[2,128,512]{2,1,0:T(8,128)(2,1)S(1)} %get-tuple-element.120), channel_id=1, source_target_pairs={{0,1},{1,0},{2,3},{3,2},{4,5},{5,4},{6,7},{7,6},{8,9},{9,8},{10,11... | collective-permute-start | bytes 786440 | tf_op jit(solution)/shard_map/ppermute | solution.py:937
  148.0 11.4 %collective-permute-start.50 = (bf16[448,128]{1,0:T(8,128)(2,1)S(1)}, bf16[448,128]{1,0:T(8,128)(2,1)S(1)}, u32[]{:S(2)}, u32[]{:S(2)}) collective-permute-start(bf16[448,128]{1,0:T(8,128)(2,1)S(1)} %shard_map.194.two), channel_id=1, source_target_pairs={{16,0},{17,1},{18,2},{19,3},{20,4},{21,5},{22,6},{23,7},{24,8},{25... | collective-permute-start | bytes 344072 | tf_op jit(solution)/shard_map/ppermute | solution.py:750
  149.3 10.1 %collective-permute-start.49 = (bf16[432,128]{1,0:T(8,128)(2,1)S(1)}, bf16[432,128]{1,0:T(8,128)(2,1)S(1)}, u32[]{:S(2)}, u32[]{:S(2)}) collective-permute-start(bf16[432,128]{1,0:T(8,128)(2,1)S(1)} %shard_map.193.one), channel_id=1, source_target_pairs={{16,0},{17,1},{18,2},{19,3},{20,4},{21,5},{22,6},{23,7},{24,8},{25... | collective-permute-start | bytes 331784 | tf_op jit(solution)/shard_map/ppermute | solution.py:750
  160.4 11.4 %all-to-all-start = ((f32[32,8,128]{2,1,0:T(8,128)}), f32[32,8,128]{2,1,0:T(8,128)S(1)}, u32[]{:S(2)}, u32[]{:S(2)}) async-start(f32[32,8,128]{2,1,0:T(8,128)} %get-tuple-element.125), calls=%async_computation | async-start | bytes 262144 | tf_op jit(solution)/shard_map/all_to_all | solution.py:997
  (52 other events, 602.8 us)

commit v3 on v2

--- a/solution.py
+++ b/solution.py
@@ -40,10 +40,7 @@
 TAIL = 16
 ROWS = 16
 PART = BLOCK // 2
-PARTS = (PART, PART + TAIL)
-FIRST_BLOCKS = -(-EXPAND_AT // BLOCK)
-SECOND_FROM = EXPAND_AT // BLOCK
-SECOND_BLOCKS = 32 - SECOND_FROM
+PARTS = (PART + TAIL, PART)
 TILE = 256
 TILES = FF // TILE
 GROUP = 4
@@ -51,6 +48,7 @@
 MINE = 2
 TOKENS = MINE * SLOTS
 PICKS = KMAX + 16
+PACK = SLOTS // 2 + KMAX // 2 + KMAX // 4
 VMEM = pl.BlockSpec(memory_space=pltpu.VMEM)
 SMEM = pl.BlockSpec(memory_space=pltpu.SMEM)
 ANY = pl.BlockSpec(memory_space=pl.ANY)
@@ -81,30 +79,25 @@
     return lax.axis_index("dp") * lax.axis_size("blk") + lax.axis_index("blk")
 
 
-def fetch_lines(places, pieces, low_lines, high_lines, low_sem, high_sem):
-    if places is None:
-        for lines, low, sem in ((low_lines, 0, low_sem), (high_lines, SECOND_FROM, high_sem)):
-            rows = pl.ds(low * BLOCK, lines.shape[0])
-            pltpu.make_async_copy(pieces[0].at[rows], lines, sem).start()
-            wait_lines(lines, sem)
-        return
-    me = place()
-    odd = (me >> 1) & 1
-    for (bits, even, uneven), piece in zip(places, pieces, strict=True):
-        block = me ^ bits ^ jnp.where(odd == 0, even, uneven)
-
-        @pl.when(block < FIRST_BLOCKS)
-        def _(piece=piece, block=block):
-            low_lines[pl.ds(pl.multiple_of(block * BLOCK, 16), BLOCK), :] = piece[...]
-
-        @pl.when(block >= SECOND_FROM)
-        def _(piece=piece, block=block):
-            at = pl.multiple_of((block - SECOND_FROM) * BLOCK, 16)
-            high_lines[pl.ds(at, BLOCK), :] = piece[...]
-
-
-def wait_lines(lines, sem):
-    pltpu.make_async_copy(lines, lines, sem).wait()
+def collect_call(lines, pieces, places):
+    def kernel(*refs):
+        out = refs[-1]
+        me = place()
+        odd = (me >> 1) & 1
+        for (bits, even, uneven), piece in zip(places, refs[-1 - len(pieces) : -1], strict=True):
+            block = me ^ bits ^ jnp.where(odd == 0, even, uneven)
+            out[pl.ds(pl.multiple_of(block * BLOCK, 16), BLOCK), :] = piece[...]
+
+    given = ([] if lines is None else [lines]) + list(pieces)
+    return pl.pallas_call(
+        kernel,
+        in_specs=[VMEM] * len(given),
+        out_shape=pltpu.VMEM((LINES, LANES), BF),
+        out_specs=VMEM,
+        input_output_aliases={} if lines is None else {0: 0},
+        compiler_params=pltpu.CompilerParams(vmem_limit_bytes=2 * 2**20),
+        cost_estimate=pl.CostEstimate(flops=0, bytes_accessed=2**20, transcendentals=0),
+    )(*(in_vmem(value) for value in given))
 
 
 def lines_to_matrix(lines, stage, matrix, at, rows, wide, batch):
@@ -155,12 +148,12 @@
     )
 
 
-def select_rows(own, far, image, side):
+def select_rows(own, far, side):
     half = SLOTS // 2
     row = lax.broadcasted_iota(jnp.int32, (PICKS, half), 0)
     row = jnp.where(row < KMAX, (row + side * (KMAX // 2)) & (KMAX - 1), row)
     parts = [
-        (row == ref[pl.ds(image, 1), :]).astype(F32) for ref in (own, far)
+        (row == names).astype(F32) for names in (own, far)
     ]
     return jnp.concatenate(parts, axis=1).astype(BF)
 
@@ -181,27 +174,55 @@
     return jnp.where(head_mask(head), value, jnp.zeros_like(value))
 
 
+def pick_kernel(latents, cotangent, restore, far_latents, far_cotangent, far_restore, sem):
+    first = (1 - lax.axis_index("blk")) * MINE
+    copies = [
+        pltpu.make_async_copy(source.at[pl.ds(first, MINE)], target, sem.at[index])
+        for index, (source, target) in enumerate(
+            ((latents, far_latents), (cotangent, far_cotangent))
+        )
+    ]
+    for copy in copies:
+        copy.start()
+    for image in range(MINE):
+        far_restore[image : image + 1, :] = restore[pl.ds(first + image, 1), :]
+    for copy in copies:
+        copy.wait()
+
+
+def pick_call(latents, cotangent, restore):
+    outs = tuple(
+        pltpu.VMEM((MINE, *value.shape[1:]), value.dtype) for value in (latents, cotangent, restore)
+    )
+    return pl.pallas_call(
+        pick_kernel,
+        in_specs=[ANY, ANY, VMEM],
+        out_shape=outs,
+        out_specs=tuple(VMEM for _ in outs),
+        scratch_shapes=[pltpu.SemaphoreType.DMA((2,))],
+        compiler_params=pltpu.CompilerParams(vmem_limit_bytes=2 * 2**20),
+        cost_estimate=pl.CostEstimate(flops=0, bytes_accessed=2**19, transcendentals=0),
+    )(in_hbm(latents), in_hbm(cotangent), restore)
+
+
 def prepare_kernel(
     latents, far_latents, restore, far_restore, position, my_latents, choice, my_position,
-    near_buffer, far_buffer, sem,
+    near_buffer, sem,
 ):
     side = lax.axis_index("blk")
-    copies = []
-    for index, (source, target) in enumerate(((latents, near_buffer), (far_latents, far_buffer))):
-        copies.append(
-            pltpu.make_async_copy(source.at[pl.ds(side * MINE, MINE)], target, sem.at[index])
-        )
-        copies[-1].start()
+    copy = pltpu.make_async_copy(latents.at[pl.ds(side * MINE, MINE)], near_buffer, sem)
+    copy.start()
     my_position[...] = position[...]
     for image in range(MINE):
-        choice[image] = select_rows(restore, far_restore, side * MINE + image, side)
-    for copy in copies:
-        copy.wait()
+        choice[image] = select_rows(
+            restore[pl.ds(side * MINE + image, 1), :], far_restore[image : image + 1, :], side
+        )
+    copy.wait()
     half = KMAX // 2
     for image in range(MINE):
         at = image * KMAX
         my_latents[at : at + half, :] = near_buffer[image]
-        my_latents[at + half : at + KMAX, :] = far_buffer[image]
+        my_latents[at + half : at + KMAX, :] = far_latents[image]
 
 
 def prepare_call(*operands):
@@ -212,24 +233,22 @@
     )
     return pl.pallas_call(
         prepare_kernel,
-        in_specs=[ANY, ANY, VMEM, VMEM, VMEM],
+        in_specs=[ANY, VMEM, VMEM, VMEM, VMEM],
         out_shape=outs,
         out_specs=tuple(VMEM for _ in outs),
         scratch_shapes=[
             pltpu.VMEM((MINE, KMAX // 2, DIN), BF),
-            pltpu.VMEM((MINE, KMAX // 2, DIN), BF),
-            pltpu.SemaphoreType.DMA((2,)),
+            pltpu.SemaphoreType.DMA,
         ],
         compiler_params=pltpu.CompilerParams(vmem_limit_bytes=4 * 2**20),
         cost_estimate=pl.CostEstimate(flops=10**6, bytes_accessed=2**20, transcendentals=0),
-    )(*operands)
-
-
-def forward_kernel(bucket, my_latents, choice, position, vectors, *rest, places):
-    pieces = len(rest) - 17
-    sources = rest[:pieces]
+    )(in_hbm(operands[0]), *operands[1:])
+
+
+def forward_kernel(bucket, my_latents, choice, position, vectors, lines, *rest):
     (
         probs,
+        shares,
         joint,
         normed,
         start,
@@ -238,72 +257,83 @@
         embed_w,
         joint_w,
         output_w,
-        high_lines,
-        lines,
         stage,
         query_t,
         value_t,
         mixed_t,
-        sem,
-        high_sem,
-    ) = rest[pieces:]
-    step = pl.program_id(0)
+        scores_even,
+        scores_odd,
+    ) = rest
     side = lax.axis_index("blk")
-
-    @pl.when(step == 0)
-    def _():
-        fetch_lines(places, sources, lines, high_lines, sem, high_sem)
-        lines_to_matrix(lines, stage, embed_w, EMBED_AT, DIN, 4, 128)
-        lines_to_matrix(lines, stage, joint_w, JOINT_AT, D, 12, 64)
-        lines_to_matrix(lines, stage, output_w, OUTPUT_AT, D, 4, 128)
-        embedded = (dot(my_latents[...], embed_w[...]) + vectors[0:1, :]).astype(BF)
-        token = list(three_parts(vectors[1:2, :]))
-        for image in range(MINE):
-            rows = slice(image * SLOTS, (image + 1) * SLOTS)
-            picked = choice[image]
-            value = dot(picked[:KMAX], embedded[image * KMAX : (image + 1) * KMAX, :], (0, 0))
-            masked = jnp.broadcast_to(picked[KMAX : KMAX + 1], (16, SLOTS))
-            table = jnp.concatenate(token + [jnp.zeros((13, D), BF)], axis=0)
-            value = value + dot(masked, table, (0, 0)) + position[...]
-            start[rows, :] = value
-            hat, _ = norm_parts(value)
-            normed[rows, :] = (hat * vectors[2:3, :] + vectors[3:4, :]).astype(BF)
-        for part, bias in enumerate((4, None, 5)):
-            columns = slice(part * D, (part + 1) * D)
-            out = dot(normed[...], joint_w[:, columns])
-            if bias is not None:
-                out = out + vectors[bias : bias + 1, :]
-            joint[:, columns] = out.astype(BF)
-        query_t[...] = joint[:, :D].T
-        value_t[...] = joint[:, 2 * D :].T
-
-    image = step // GROUPS
-    group = step % GROUPS
-    rows = pl.ds(pl.multiple_of(image * SLOTS, SLOTS), SLOTS)
-    lanes = pl.ds(pl.multiple_of(group * LANES, LANES), LANES)
-    keys = joint[rows, pl.ds(pl.multiple_of(D + group * LANES, LANES), LANES)]
-    queries = query_t[lanes, rows]
-    length = image_length(bucket, side * MINE + image)
-    hidden_key = jnp.where(slot_column(side) < length, 0.0, -1e30)
+    lines_to_matrix(lines, stage, embed_w, EMBED_AT, DIN, 4, 128)
+    lines_to_matrix(lines, stage, joint_w, JOINT_AT, D, 12, 64)
+    lines_to_matrix(lines, stage, output_w, OUTPUT_AT, D, 4, 128)
+    embedded = (dot(my_latents[...], embed_w[...]) + vectors[0:1, :]).astype(BF)
+    token = list(three_parts(vectors[1:2, :]))
+    for image in range(MINE):
+        rows = slice(image * SLOTS, (image + 1) * SLOTS)
+        picked = choice[image]
+        value = dot(picked[:KMAX], embedded[image * KMAX : (image + 1) * KMAX, :], (0, 0))
+        masked = jnp.broadcast_to(picked[KMAX : KMAX + 1], (16, SLOTS))
+        table = jnp.concatenate(token + [jnp.zeros((13, D), BF)], axis=0)
+        value = value + dot(masked, table, (0, 0)) + position[...]
+        start[rows, :] = value
+        hat, _ = norm_parts(value)
+        normed[rows, :] = (hat * vectors[2:3, :] + vectors[3:4, :]).astype(BF)
+    for part, bias in enumerate((4, None, 5)):
+        columns = slice(part * D, (part + 1) * D)
+        out = dot(normed[...], joint_w[:, columns])
+        if bias is not None:
+            out = out + vectors[bias : bias + 1, :]
+        joint[:, columns] = out.astype(BF)
+    query_t[...] = joint[:, :D].T
+    value_t[...] = joint[:, 2 * D :].T
+
     rate = HD**-0.5 * math.log2(math.e)
-    for head in range(GROUP):
-        scores = dot(mask_head(keys, head), queries) + hidden_key
-        top = jnp.max(scores, axis=0, keepdims=True)
-        raised = jnp.exp2((scores - top) * rate)
-        low = (raised * (1.0 / jnp.sum(raised, axis=0, keepdims=True))).astype(BF)
-        probs[step * GROUP + head] = low
-        features = pl.ds(pl.multiple_of(group * LANES + head * HD, HD), HD)
-        mixed_t[features, rows] = dot(value_t[features, rows], low).astype(BF)
-
-    @pl.when(step == MINE * GROUPS - 1)
-    def _():
-        mixed[...] = mixed_t[...].T
-        middle[...] = start[...] + dot(mixed[...], output_w[...]) + vectors[6:7, :]
-
-
-def forward_call(bucket, my_latents, choice, position, vectors, sources, places):
+
+    def score(unit, target):
+        image, group = unit // GROUPS, unit % GROUPS
+        rows = pl.ds(pl.multiple_of(image * SLOTS, SLOTS), SLOTS)
+        keys = joint[rows, pl.ds(pl.multiple_of(D + group * LANES, LANES), LANES)]
+        queries = query_t[pl.ds(pl.multiple_of(group * LANES, LANES), LANES), rows]
+        for head in range(GROUP):
+            target[head] = dot(mask_head(keys, head), queries)
+
+    def mix(unit, source):
+        image, group = unit // GROUPS, unit % GROUPS
+        rows = pl.ds(pl.multiple_of(image * SLOTS, SLOTS), SLOTS)
+        length = image_length(bucket, side * MINE + image)
+        hidden_key = jnp.where(slot_column(side) < length, 0.0, -1e30)
+        for head in range(GROUP):
+            scores = source[head] + hidden_key
+            top = jnp.max(scores, axis=0, keepdims=True)
+            raised = jnp.exp2((scores - top) * rate)
+            share = 1.0 / jnp.sum(raised, axis=0, keepdims=True)
+            low = raised.astype(BF)
+            probs[unit * GROUP + head] = low
+            shares[pl.ds(unit * GROUP + head, 1), :] = share
+            features = pl.ds(pl.multiple_of(group * LANES + head * HD, HD), HD)
+            mixed_t[features, rows] = (dot(value_t[features, rows], low) * share).astype(BF)
+
+    score(0, scores_even)
+
+    def pair(index, carry):
+        unit = 2 * index
+        score(unit + 1, scores_odd)
+        mix(unit, scores_even)
+        score(jnp.minimum(unit + 2, MINE * GROUPS - 1), scores_even)
+        mix(unit + 1, scores_odd)
+        return carry
+
+    lax.fori_loop(0, MINE * GROUPS // 2, pair, 0)
+    mixed[...] = mixed_t[...].T
+    middle[...] = start[...] + dot(mixed[...], output_w[...]) + vectors[6:7, :]
+
+
+def forward_call(*operands):
     outs = (
         pltpu.VMEM((MINE * HEADS, SLOTS, SLOTS), BF),
+        pltpu.VMEM((MINE * HEADS, SLOTS), F32),
         pltpu.VMEM((TOKENS, 3 * D), BF),
         pltpu.VMEM((TOKENS, D), BF),
         pltpu.VMEM((TOKENS, D), F32),
@@ -312,28 +342,25 @@
         pltpu.VMEM((DIN, D), BF),
         pltpu.VMEM((D, 3 * D), BF),
         pltpu.VMEM((D, D), BF),
-        pltpu.VMEM((SECOND_BLOCKS * BLOCK, LANES), BF),
-    )
-    return pl.pallas_call(
-        lambda *refs: forward_kernel(*refs, places=places),
-        grid=(MINE * GROUPS,),
-        in_specs=[SMEM] + [VMEM] * 4 + [VMEM if places else ANY] * len(sources),
+    )
+    return pl.pallas_call(
+        forward_kernel,
+        in_specs=[SMEM] + [VMEM] * (len(operands) - 1),
         out_shape=outs,
         out_specs=tuple(VMEM for _ in outs),
         scratch_shapes=[
-            pltpu.VMEM((FIRST_BLOCKS * BLOCK, LANES), BF),
             pltpu.VMEM((2, 768, LANES), F32),
             pltpu.VMEM((D, TOKENS), BF),
             pltpu.VMEM((D, TOKENS), BF),
             pltpu.VMEM((D, TOKENS), BF),
-            pltpu.SemaphoreType.DMA,
-            pltpu.SemaphoreType.DMA,
+            pltpu.VMEM((GROUP, SLOTS, SLOTS), F32),
+            pltpu.VMEM((GROUP, SLOTS, SLOTS), F32),
         ],
-        compiler_params=pltpu.CompilerParams(vmem_limit_bytes=16 * 2**20),
+        compiler_params=pltpu.CompilerParams(vmem_limit_bytes=10 * 2**20),
         cost_estimate=pl.CostEstimate(
             flops=6 * 10**9, bytes_accessed=16 * 2**20, transcendentals=2 * 10**6
         ),
-    )(bucket, my_latents, choice, position, vectors, *sources)
+    )(*operands)
 
 
 def middle_kernel(
@@ -360,7 +387,6 @@
     ) = rest
     step = pl.program_id(0)
     side = lax.axis_index("blk")
-    base = SECOND_FROM * BLOCK
 
     @pl.when(step == 0)
     def _():
@@ -372,17 +398,19 @@
         for image in range(MINE):
             valid = slot_column(side) < image_length(bucket, side * MINE + image)
             half = SLOTS // 2
-            for part, ref in enumerate((cotangent, far_cotangent)):
-                at = image * SLOTS + part * half
-                back_out[at : at + half, :] = jnp.where(
+            for part, (ref, at) in enumerate(
+                ((cotangent, side * MINE + image), (far_cotangent, image))
+            ):
+                first = image * SLOTS + part * half
+                back_out[first : first + half, :] = jnp.where(
                     valid[part * half : (part + 1) * half, :],
-                    ref[side * MINE + image].astype(F32),
+                    ref[at].astype(F32),
                     0.0,
                 ).astype(BF)
         acc[...] = jnp.zeros_like(acc)
         acc_back[...] = jnp.zeros_like(acc_back)
-        lines_to_matrix(lines, stage, expand_w, EXPAND_AT - base, D, 16, 32)
-        lines_to_matrix(lines, stage, reduce_w, REDUCE_AT - base, FF, 4, 128)
+        lines_to_matrix(lines, stage, expand_w, EXPAND_AT, D, 16, 32)
+        lines_to_matrix(lines, stage, reduce_w, REDUCE_AT, FF, 4, 128)
 
     columns = pl.ds(pl.multiple_of(step * TILE, TILE), TILE)
     expand = expand_w[:, columns]
@@ -460,7 +488,7 @@
 def middle_call(by_hand, *operands):
     outs = (
         pltpu.VMEM((MINE, SLOTS // 2, D), F32),
-        jax.ShapeDtypeStruct((MINE, SLOTS // 2, D), BF),
+        pltpu.VMEM((MINE, SLOTS // 2, D), BF),
         pltpu.VMEM((TOKENS, D), F32),
         pltpu.VMEM((TOKENS, LANES), F32),
         pltpu.VMEM((TOKENS, D), BF),
@@ -485,7 +513,7 @@
             pltpu.VMEM((TOKENS, D), F32),
             pltpu.VMEM((2 * D * 16, LANES), F32),
         ],
-        compiler_params=pltpu.CompilerParams(vmem_limit_bytes=24 * 2**20),
+        compiler_params=pltpu.CompilerParams(vmem_limit_bytes=20 * 2**20),
         cost_estimate=pl.CostEstimate(
             flops=8 * 10**9, bytes_accessed=16 * 2**20, transcendentals=2 * 10**6
         ),
@@ -535,106 +563,142 @@
 
 
 def attention_back_kernel(
-    probs, joint, back_mixed, joint_back, key_t, back_t, query_back_t
+    probs, shares, joint, back_mixed, normed, start, back_middle, vectors, joint_w,
+    joint_lines, back_start, rows_out,
+    joint_back, key_t, back_t, shared_t, shared, query_back_t, even, odd, grads,
 ):
-    step = pl.program_id(0)
-
-    @pl.when(step == 0)
-    def _():
-        key_t[...] = joint[:, D : 2 * D].T
-        back_t[...] = back_mixed[...].T
-
-    image = step // GROUPS
-    group = step % GROUPS
-    rows = pl.ds(pl.multiple_of(image * SLOTS, SLOTS), SLOTS)
-    lanes = pl.ds(pl.multiple_of(group * LANES, LANES), LANES)
-    queries = joint[rows, lanes]
-    values = joint[rows, pl.ds(pl.multiple_of(2 * D + group * LANES, LANES), LANES)]
-    back = back_mixed[rows, lanes]
-    back_lanes = back_t[lanes, rows]
-    key_back = jnp.zeros((SLOTS, LANES), F32)
-    value_back = jnp.zeros((SLOTS, LANES), F32)
-    for head in range(GROUP):
-        low = probs[step * GROUP + head]
-        wide = low.astype(F32)
-        back_probs = dot(mask_head(values, head), back_lanes)
-        pull = jnp.sum(wide * back_probs, axis=0, keepdims=True)
-        score_back = (wide * (back_probs - pull) * HD**-0.5).astype(BF)
-        value_back = value_back + dot(low, mask_head(back, head))
-        key_back = key_back + dot(score_back, mask_head(queries, head))
-        features = pl.ds(pl.multiple_of(group * LANES + head * HD, HD), HD)
-        query_back_t[features, rows] = dot(key_t[features, rows], score_back).astype(BF)
-    joint_back[rows, pl.ds(pl.multiple_of(D + group * LANES, LANES), LANES)] = key_back.astype(BF)
-    joint_back[rows, pl.ds(pl.multiple_of(2 * D + group * LANES, LANES), LANES)] = (
-        value_back.astype(BF)
-    )
-
-    @pl.when(step == MINE * GROUPS - 1)
-    def _():
-        joint_back[:, :D] = query_back_t[...].T
-
-
-def attention_back_call(probs, joint, back_mixed):
+    key_t[...] = joint[:, D : 2 * D].T
+    back_t[...] = back_mixed[...].T
+    for image in range(MINE):
+        columns = slice(image * SLOTS, (image + 1) * SLOTS)
+        for head in range(HEADS):
+            features = slice(head * HD, (head + 1) * HD)
+            at = image * HEADS + head
+            shared_t[features, columns] = (
+                back_t[features, columns].astype(F32) * shares[at : at + 1, :]
+            ).astype(BF)
+    shared[...] = shared_t[...].T
+
+    def pull_back(unit, target):
+        image, group = unit // GROUPS, unit % GROUPS
+        rows = pl.ds(pl.multiple_of(image * SLOTS, SLOTS), SLOTS)
+        values = joint[rows, pl.ds(pl.multiple_of(2 * D + group * LANES, LANES), LANES)]
+        back_lanes = back_t[pl.ds(pl.multiple_of(group * LANES, LANES), LANES), rows]
+        for head in range(GROUP):
+            target[head] = dot(mask_head(values, head), back_lanes)
+
+    def spread(unit, source):
+        image, group = unit // GROUPS, unit % GROUPS
+        rows = pl.ds(pl.multiple_of(image * SLOTS, SLOTS), SLOTS)
+        lanes = pl.ds(pl.multiple_of(group * LANES, LANES), LANES)
+        queries = joint[rows, lanes]
+        back = shared[rows, lanes]
+        key_back = jnp.zeros((SLOTS, LANES), F32)
+        value_back = jnp.zeros((SLOTS, LANES), F32)
+        for head in range(GROUP):
+            low = probs[unit * GROUP + head]
+            share = shares[pl.ds(unit * GROUP + head, 1), :]
+            wide = low.astype(F32)
+            back_probs = source[head]
+            pull = jnp.sum(wide * back_probs, axis=0, keepdims=True) * share
+            score_back = (wide * ((back_probs - pull) * (share * HD**-0.5))).astype(BF)
+            value_back = value_back + dot(low, mask_head(back, head))
+            key_back = key_back + dot(score_back, mask_head(queries, head))
+            features = pl.ds(pl.multiple_of(group * LANES + head * HD, HD), HD)
+            query_back_t[features, rows] = dot(key_t[features, rows], score_back).astype(BF)
+        joint_back[rows, pl.ds(pl.multiple_of(D + group * LANES, LANES), LANES)] = (
+            key_back.astype(BF)
+        )
+        joint_back[rows, pl.ds(pl.multiple_of(2 * D + group * LANES, LANES), LANES)] = (
+            value_back.astype(BF)
+        )
+
+    pull_back(0, even)
+
+    def pair(index, carry):
+        unit = 2 * index
+        pull_back(unit + 1, odd)
+        spread(unit, even)
+        pull_back(jnp.minimum(unit + 2, MINE * GROUPS - 1), even)
+        spread(unit + 1, odd)
+        return carry
+
+    lax.fori_loop(0, MINE * GROUPS // 2, pair, 0)
+    joint_back[:, :D] = query_back_t[...].T
+    rows_out[...] = jnp.zeros_like(rows_out)
+    rows_out[2:3, :] = total(joint_back[:, :D])
+    rows_out[3:4, :] = total(joint_back[:, 2 * D :])
+    normed_t = normed[...].T
+    for part in range(3):
+        grad_joint = dot(normed_t, joint_back[:, part * D : (part + 1) * D])
+        for j in range(4):
+            grads[pl.ds(part * 4 + j, D, stride=12), :] = grad_joint[
+                :, j * LANES : (j + 1) * LANES
+            ]
+    grad = dot(joint_back[...], joint_w[...], (1, 1))
+    hat, scale = norm_parts(start[...])
+    rows_out[0:1, :] = total(grad * hat)
+    rows_out[1:2, :] = total(grad)
+    back_start[...] = back_middle[...] + norm_back(grad, hat, scale, vectors[2:3, :])
+    joint_lines[...] = grads[...].astype(BF)
+
+
+def attention_back_call(*operands):
+    outs = (
+        pltpu.VMEM((OUTPUT_AT - JOINT_AT, LANES), BF),
+        pltpu.VMEM((TOKENS, D), F32),
+        pltpu.VMEM((8, D), F32),
+    )
     return pl.pallas_call(
         attention_back_kernel,
-        grid=(MINE * GROUPS,),
-        in_specs=[VMEM] * 3,
-        out_shape=pltpu.VMEM((TOKENS, 3 * D), BF),
-        out_specs=VMEM,
+        in_specs=[VMEM] * len(operands),
+        out_shape=outs,
+        out_specs=tuple(VMEM for _ in outs),
         scratch_shapes=[
+            pltpu.VMEM((TOKENS, 3 * D), BF),
             pltpu.VMEM((D, TOKENS), BF),
             pltpu.VMEM((D, TOKENS), BF),
             pltpu.VMEM((D, TOKENS), BF),
+            pltpu.VMEM((TOKENS, D), BF),
+            pltpu.VMEM((D, TOKENS), BF),
+            pltpu.VMEM((GROUP, SLOTS, SLOTS), F32),
+            pltpu.VMEM((GROUP, SLOTS, SLOTS), F32),
+            pltpu.VMEM((OUTPUT_AT - JOINT_AT, LANES), F32),
         ],
         compiler_params=pltpu.CompilerParams(vmem_limit_bytes=16 * 2**20),
         cost_estimate=pl.CostEstimate(
             flops=8 * 10**9, bytes_accessed=4 * 2**20, transcendentals=0
         ),
-    )(probs, joint, back_mixed)
+    )(*operands)
 
 
 def input_back_kernel(
     by_hand,
-    joint_back,
-    normed,
-    start,
-    back_middle,
+    back_start,
     my_latents,
     choices,
-    vectors,
     embed_w,
-    joint_w,
+    joint_lines,
+    rows_joint,
     out_lines,
     head_lines,
     rows_in,
     expand_in,
+    far_out,
     far_first,
     near_first,
     far_second,
     near_second,
     rows_out,
     own_latent,
-    far_latent,
+    pack,
     grads,
     tails,
 ):
     rows_out[...] = jnp.zeros_like(rows_out)
-    rows_out[4:5, :] = total(joint_back[:, :D])
-    rows_out[5:6, :] = total(joint_back[:, 2 * D :])
-    normed_t = normed[...].T
-    for part in range(3):
-        grad_joint = dot(normed_t, joint_back[:, part * D : (part + 1) * D])
-        for j in range(4):
-            grads[pl.ds(JOINT_AT + part * 4 + j, D, stride=12), :] = grad_joint[
-                :, j * LANES : (j + 1) * LANES
-            ]
-    grad = dot(joint_back[...], joint_w[...], (1, 1))
-    hat, scale = norm_parts(start[...])
-    rows_out[2:3, :] = total(grad * hat)
-    rows_out[3:4, :] = total(grad)
-    back_start = back_middle[...] + norm_back(grad, hat, scale, vectors[2:3, :])
-    low_start = back_start.astype(BF)
-    low_rest = (back_start - low_start.astype(F32)).astype(BF)
+    rows_out[2:6, :] = rows_joint[0:4, :]
+    low_start = back_start[...].astype(BF)
+    low_rest = (back_start[...] - low_start.astype(F32)).astype(BF)
     picked = []
     token_back = jnp.zeros((1, D), F32)
     for image in range(MINE):
@@ -654,7 +718,11 @@
     for image in range(MINE):
         at = image * KMAX
         own_latent[image] = latent_back[at : at + KMAX // 2, :]
-        far_latent[image] = latent_back[at + KMAX // 2 : at + KMAX, :].astype(BF)
+        far = latent_back[at + KMAX // 2 : at + KMAX, :].astype(BF)
+        pack[image, : SLOTS // 2, :] = far_out[image]
+        pack[image, SLOTS // 2 : SLOTS // 2 + KMAX // 2, :] = far[:, :D]
+        pack[image, SLOTS // 2 + KMAX // 2 :, : DIN - D] = far[: KMAX // 4, D:]
+        pack[image, SLOTS // 2 + KMAX // 2 :, DIN - D :] = far[KMAX // 4 :, D:]
     rows_out[6:10, :] = rows_in[0:4, :]
     for j in range(4):
         rows_out[10 + j : 11 + j, :TILE] = expand_in[2 * j : 2 * j + 1, :]
@@ -671,10 +739,10 @@
         tail = tails[pl.ds(pl.multiple_of(index * TAIL, TAIL), TAIL), :].astype(BF)
 
         def put(first, second, at):
-            first[pl.ds(pl.multiple_of(at * PART, 16), PART), :] = value[:PART]
-            row = pl.multiple_of(at * PARTS[1], 16)
-            second[pl.ds(row, PART), :] = value[PART:]
-            second[pl.ds(row + PART, TAIL), :] = tail
+            row = pl.multiple_of(at * PARTS[0], 16)
+            first[pl.ds(row, PART), :] = value[:PART]
+            first[pl.ds(row + PART, TAIL), :] = tail
+            second[pl.ds(pl.multiple_of(at * PART, 16), PART), :] = value[PART:]
 
         @pl.when(slot < 8)
         def _():
@@ -684,29 +752,20 @@
         def _():
             put(near_first, near_second, slot - 8)
 
-    first = OUTPUT_AT // BLOCK
-    last = -(-EXPAND_AT // BLOCK)
-
-    def early(index, carry):
-        store(index, grads[pl.ds(pl.multiple_of(index * BLOCK, 16), BLOCK), :].astype(BF))
-        return carry
-
-    def late(index, carry):
-        at = pl.multiple_of(index * BLOCK - EXPAND_AT, 16)
-        store(index, head_lines[pl.ds(at, BLOCK), :])
-        return carry
-
-    lax.fori_loop(0, first, early, 0)
-    for index in range(first, last):
+    ranges = (
+        (EMBED_AT, JOINT_AT, lambda low, high: grads[low:high, :].astype(BF)),
+        (JOINT_AT, OUTPUT_AT, lambda low, high: joint_lines[low:high, :]),
+        (OUTPUT_AT, EXPAND_AT, lambda low, high: out_lines[low:high, :]),
+        (EXPAND_AT, HALF, lambda low, high: head_lines[low:high, :]),
+    )
+    for index in range(16):
         low, high = index * BLOCK, (index + 1) * BLOCK
-        parts = []
-        if low < OUTPUT_AT:
-            parts.append(grads[low:OUTPUT_AT, :].astype(BF))
-        parts.append(out_lines[max(low - OUTPUT_AT, 0) : min(high, EXPAND_AT) - OUTPUT_AT, :])
-        if high > EXPAND_AT:
-            parts.append(head_lines[: high - EXPAND_AT, :])
+        parts = [
+            take(max(low, begin) - begin, min(high, end) - begin)
+            for begin, end, take in ranges
+            if max(low, begin) < min(high, end)
+        ]
         store(index, jnp.concatenate(parts, axis=0) if len(parts) > 1 else parts[0])
-    lax.fori_loop(last, 16, late, 0)
 
 
 def input_back_call(by_hand, *operands):
@@ -718,7 +777,7 @@
         pltpu.VMEM((8 * PARTS[1], LANES), BF),
         shape((ROWS, D), F32),
         pltpu.VMEM((MINE, KMAX // 2, DIN), F32),
-        shape((MINE, KMAX // 2, DIN), BF),
+        pltpu.VMEM((MINE, PACK, D), BF),
     )
     return pl.pallas_call(
         lambda *refs: input_back_kernel(by_hand, *refs),
@@ -726,7 +785,7 @@
         out_shape=outs,
         out_specs=tuple(VMEM for _ in outs),
         scratch_shapes=[
-            pltpu.VMEM((OUTPUT_AT, LANES), F32),
+            pltpu.VMEM((JOINT_AT, LANES), F32),
             pltpu.VMEM((ROWS * TAIL, LANES), F32),
         ],
         compiler_params=pltpu.CompilerParams(vmem_limit_bytes=24 * 2**20),
@@ -740,53 +799,56 @@
     def __init__(self, mesh):
         self.axes = ("dp", "blk")
         self.count = mesh.shape["dp"] * mesh.shape["blk"]
+        self.early = self.late = ()
         self.by_hand = self.count == 32 and mesh.shape["blk"] == 2
 
-    def send(self, value, bits, other=None, only=None):
+    def send(self, value, bits, other=None):
         other = bits if other is None else other
         pairs = [(i, i ^ (other if i & 2 else bits)) for i in range(self.count)]
-        if only is not None:
-            pairs = [(i, j) for i, j in pairs if (i & 16 == 0) == (only == 0)]
         return lax.ppermute(value, self.axes, pairs)
 
     def gather(self, block):
         if not self.by_hand:
             whole = lax.all_gather(block, self.axes, axis=0, tiled=True)
-            return [whole.reshape(LINES, LANES)], None
-        held = {0: block}
-        near, side, far = {}, {}, {}
-
-        def plane(k):
-            near[k] = self.send(held[k], 4, 1)
-            side[k] = self.send(held[k], 1, 4)
-
-        def corner(k):
-            far[k] = self.send(near[k], 1, 4)
-
-        held[16] = self.send(block, 16)
-        plane(0)
-        held[8] = self.send(block, 8)
-        corner(0)
-        plane(8)
-        held[24] = self.send(held[16], 8)
-        plane(16)
-        corner(16)
-        far[8] = self.send(far[0], 8)
-        plane(24)
-        far[24] = self.send(far[16], 8)
-        pieces, places = [], []
-        for k in (0, 8, 16, 24):
-            for value, even, uneven in (
-                (held[k], 0, 0),
-                (near[k], 4, 1),
-                (side[k], 1, 4),
-                (far[k], 5, 5),
-            ):
-                pieces.append(value)
-                places.append((k, even, uneven))
-                pieces.append(self.send(value, 2))
-                places.append((k ^ 2, uneven, even))
-        return [in_vmem(piece) for piece in pieces], tuple(places)
+            return whole.reshape(LINES, LANES)
+        got = {"held0": block}
+
+        def send(name, value, bits, other=None, behind=()):
+            got[name] = self.send(after(got[value], *(got[b] for b in behind)), bits, other)
+
+        def put(lines, *names):
+            pieces, places = [], []
+            for name in names:
+                even, uneven = {"held": (0, 0), "near": (4, 1), "side": (1, 4), "far": (5, 5)}[
+                    name.rstrip("0123456789")
+                ]
+                bits = int(name.lstrip("abcdefghijklmnopqrstuvwxyz"))
+                pieces += [got[name], self.send(got[name], 2)]
+                places += [(bits, even, uneven), (bits ^ 2, uneven, even)]
+            return collect_call(lines, pieces, places)
+
+        send("held16", "held0", 16)
+        send("near0", "held0", 4, 1)
+        send("held8", "held0", 8)
+        send("side0", "held0", 1, 4)
+        send("far0", "near0", 1, 4)
+        send("near16", "held16", 4, 1)
+        send("side16", "held16", 1, 4)
+        send("held24", "held16", 8)
+        send("near8", "held8", 4, 1)
+        send("side8", "held8", 1, 4)
+        send("far8", "far0", 8)
+        send("far16", "near16", 1, 4)
+        send("near24", "held24", 4, 1, behind=("near8",))
+        send("side24", "held24", 1, 4, behind=("side8",))
+        send("far24", "far16", 8, behind=("far8",))
+        lines = put(
+            None, "held0", "near0", "side0", "far0", "held8", "near8", "side8", "far8", "held16",
+            "near16", "side16", "far16", "held24", "near24", "side24", "far24",
+        )
+        self.late = (got["side24"], got["far24"])
+        self.early = (got["near24"],)
+        return lines
 
 
 def add_call(rows, *terms):
@@ -806,6 +868,10 @@
         compiler_params=pltpu.CompilerParams(vmem_limit_bytes=4 * 2**20),
         cost_estimate=pl.CostEstimate(flops=10**5, bytes_accessed=2**20, transcendentals=0),
     )(*(in_vmem(array) for array, _ in terms))
+
+
+def in_hbm(value):
+    return pltpu.with_memory_space_constraint(value, pltpu.HBM)
 
 
 def in_vmem(value):
@@ -835,20 +901,36 @@
         self.head = add_call(count * self.rows, *terms)
         return self.head
 
-    def last(self):
-        self.across = self.grid.send(self.head, 16, only=1 - self.half)
-
-
-def finish_kernel(high, high_far, one, one_far, two, two_far, grad, notes):
+
+def cross_call(low, high, at):
+    rows = low.shape[0]
+    lines = min(rows, PART)
+
+    def kernel(low, high, out):
+        lower = (place() & 16) == 0
+        out[:lines, :] = jnp.where(lower, high[at : at + lines, :], low[:lines, :])
+        if lines < rows:
+            out[lines:, :] = low[lines:, :]
+
+    return pl.pallas_call(
+        kernel,
+        in_specs=[VMEM] * 2,
+        out_shape=pltpu.VMEM((rows, LANES), BF),
+        out_specs=VMEM,
+        compiler_params=pltpu.CompilerParams(vmem_limit_bytes=2**20),
+        cost_estimate=pl.CostEstimate(flops=0, bytes_accessed=2**17, transcendentals=0),
+    )(in_vmem(low), in_vmem(high))
+
+
+def finish_kernel(high, one, one_far, two, two_far, grad, notes):
     lower = (place() & 16) == 0
 
-    def both(near, far):
-        return near[...].astype(F32) + far[...].astype(F32)
-
-    low_one, low_two, upper = both(one, one_far), both(two, two_far), both(high, high_far)
-    grad[:PART, :] = jnp.where(lower, low_one, upper[:PART])
-    grad[PART:, :] = jnp.where(lower, low_two[:PART], upper[PART:])
-    row = jnp.where(lower, low_two[PART:], 0.0)
+    for begin, near, far in ((0, one, one_far), (PART, two, two_far)):
+        upper = high[begin : begin + PART, :].astype(F32)
+        mine = jnp.where(lower, near[:PART, :].astype(F32), upper)
+        grad[begin : begin + PART, :] = mine + far[:PART, :].astype(F32)
+    tail = one[PART:, :].astype(F32) + one_far[PART:, :].astype(F32)
+    row = jnp.where(lower, tail, 0.0)
     value = grad[...]
     square = jnp.sum(jnp.sum(value * value, axis=0, keepdims=True), axis=1, keepdims=True)
     square = square + jnp.sum(jnp.sum(row * row, axis=0, keepdims=True), axis=1, keepdims=True)
@@ -909,6 +991,51 @@
         compiler_params=pltpu.CompilerParams(vmem_limit_bytes=12 * 2**20),
         cost_estimate=pl.CostEstimate(flops=10**7, bytes_accessed=2**22, transcendentals=10**6),
     )(*operands)
+
+
+def join_kernel(own_out, own_latent, pack, block_out, latent_out, out_wide, latent_wide, sem):
+    side = lax.axis_index("blk")
+    mine = pl.ds(side * MINE, MINE)
+    other = pl.ds((1 - side) * MINE, MINE)
+    half = SLOTS // 2
+    copies = [
+        pltpu.make_async_copy(own_out, block_out.at[mine], sem.at[0]),
+        pltpu.make_async_copy(own_latent, latent_out.at[mine], sem.at[1]),
+        pltpu.make_async_copy(out_wide, block_out.at[other], sem.at[2]),
+        pltpu.make_async_copy(latent_wide, latent_out.at[other], sem.at[3]),
+    ]
+    copies[0].start()
+    copies[1].start()
+    for image in range(MINE):
+        out_wide[image] = pack[image, :half, :].astype(F32)
+        latent_wide[image, :, :D] = pack[image, half : half + KMAX // 2, :].astype(F32)
+        last = pack[image, half + KMAX // 2 :, :].astype(F32)
+        latent_wide[image, : KMAX // 4, D:] = last[:, : DIN - D]
+        latent_wide[image, KMAX // 4 :, D:] = last[:, DIN - D :]
+    copies[2].start()
+    copies[3].start()
+    for copy in copies:
+        copy.wait()
+
+
+def join_call(own_out, own_latent, pack, images):
+    shape = jax.ShapeDtypeStruct
+    return pl.pallas_call(
+        join_kernel,
+        in_specs=[VMEM] * 3,
+        out_shape=(
+            shape((images, *own_out.shape[1:]), F32),
+            shape((images, *own_latent.shape[1:]), F32),
+        ),
+        out_specs=(ANY, ANY),
+        scratch_shapes=[
+            pltpu.VMEM(own_out.shape, F32),
+            pltpu.VMEM(own_latent.shape, F32),
+            pltpu.SemaphoreType.DMA((4,)),
+        ],
+        compiler_params=pltpu.CompilerParams(vmem_limit_bytes=4 * 2**20),
+        cost_estimate=pl.CostEstimate(flops=0, bytes_accessed=2**21, transcendentals=0),
+    )(own_out, own_latent, pack)
 
 
 def after(value, *others):
@@ -936,19 +1063,21 @@
     def trade(value):
         return lax.ppermute(value, "blk", [(0, 1), (1, 0)])
 
-    pieces, places = grid.gather(flat_weights.reshape(-1, LANES).astype(BF))
+    out_latents, out_cotangent, out_restore = pick_call(latents, cotangent, restore)
+    lines = grid.gather(flat_weights.reshape(-1, LANES).astype(BF))
     slot = (jnp.arange(SLOTS, dtype=jnp.int32) + side * (SLOTS // 2)) & (SLOTS - 1)
     position = position_rows(slot)
     my_latents, choice, my_position = prepare_call(
-        latents, trade(after(latents, pieces[0])), restore, trade(after(restore, pieces[0])), position
-    )
-    far_cotangent = trade(after(cotangent, *pieces[-2:]))
+        latents, trade(after(out_latents, *grid.early)), restore,
+        trade(after(out_restore, *grid.early)), position,
+    )
+    far_cotangent = trade(after(out_cotangent, *grid.late))
     (
-        probs, joint, normed, start, middle, mixed, embed_w, joint_w, output_w, high_lines,
-    ) = forward_call(bucket, my_latents, choice, my_position, vectors, pieces, places)
+        probs, shares, joint, normed, start, middle, mixed, embed_w, joint_w, output_w,
+    ) = forward_call(bucket, my_latents, choice, my_position, vectors, lines)
     (
         own_out, far_out, hat, scale, back_out, acc_back, head_lines, far_high, near_high, expand_b,
-    ) = middle_call(by_hand, bucket, middle, cotangent, far_cotangent, vectors, high_lines)
+    ) = middle_call(by_hand, bucket, middle, cotangent, far_cotangent, vectors, lines)
     if by_hand:
         high = Reduction(grid, far_high, near_high, 1)
     back_middle, back_mixed, out_lines, rows_b = branch_call(
@@ -956,43 +1085,34 @@
     )
     if by_hand:
         back_mixed = after(back_mixed, high.hop(back_mixed))
-    joint_back = attention_back_call(probs, joint, back_mixed)
+    joint_lines, back_start, rows_joint = attention_back_call(
+        probs, shares, joint, back_mixed, normed, start, back_middle, vectors, joint_w
+    )
     if by_hand:
-        joint_back = after(joint_back, high.hop(joint_back))
-    far_one, near_one, far_two, near_two, rows_c, own_latent, far_latent = input_back_call(
-        by_hand, joint_back, normed, start, back_middle, my_latents, choice,
-        vectors, embed_w, joint_w, out_lines, head_lines, rows_b, expand_b,
+        back_start = after(back_start, high.hop(back_start))
+    far_one, near_one, far_two, near_two, rows_c, own_latent, pack = input_back_call(
+        by_hand, back_start, my_latents, choice, embed_w, joint_lines, rows_joint, out_lines,
+        head_lines, rows_b, expand_b,
+        far_out,
     )
     if by_hand:
         one = Reduction(grid, far_one, near_one, 0)
         two = Reduction(grid, far_two, near_two, 0)
-        mark = high.hop(far_one)
-        mark = one.hop(mark)
-        mark = two.hop(mark)
-        mark = high.hop(mark)
-        high.last()
-        for _ in range(3):
-            mark = one.hop(mark)
-            mark = two.hop(mark)
-        one.last()
-        two.last()
-        far_out = after(far_out, mark)
-        far_latent = after(far_latent, mark)
-
-    def join(own, far):
-        other = trade(far).astype(F32)
-        return jnp.where(
-            side == 0,
-            jnp.concatenate([own, other], axis=0),
-            jnp.concatenate([other, own], axis=0),
-        )
-
-    block_out = join(own_out, far_out)
-    latent_out = join(own_latent, far_latent)
+        mark = far_one
+        for stream in (one, two, high, one, two, high, one, two, one, two):
+            mark = stream.hop(mark)
+            if stream is two:
+                pack_mark = mark
+        across = [
+            grid.send(cross_call(stream.head, high.head, at), 16)
+            for stream, at in ((one, 0), (two, PART))
+        ]
+        pack = after(pack, pack_mark)
+    block_out, latent_out = join_call(own_out, own_latent, trade(pack), latents.shape[0])
 
     if by_hand:
         grad, notes = finish_call(
-            grid.count, high.head, high.across, one.head, one.across, two.head, two.across
+            grid.count, high.head, one.head, across[0], two.head, across[1]
         )
         notes = lax.all_to_all(notes, grid.axes, 0, 0, tiled=True)
         lines = [value.reshape(-1, LANES) for value in (flat_first, flat_second, flat_weights)]

time: 174 us -> 154 us (0.89)
  starting transfers between devices: 49.8 us -> 35.3 us
  Pallas kernels: 52.5 us -> 44.3 us
  waiting for transfers between devices: 60.8 us -> 68.7 us
  other arithmetic: 5.06 us -> 2.09 us
  local copies, waits for them, and re-layouts: 4.04 us -> 2.12 us
    ppermute x46 -> x45, starting transfers between devices: 41.5 us -> 27.5 us  [send(): return lax.ppermute(value, self.axes, pairs)]
    ppermute x46 -> x45, waiting for transfers between devices: 50.6 us -> 60.6 us  [send(): return lax.ppermute(value, self.axes, pairs)]
    pallas_call x3 -> x8, Pallas kernels: 28 us -> 22.1 us  [the longest x1 8.61 us: attention_back_call(): pl.pallas_call(attention_back_kernel, in_specs=[VMEM] * len(operands), ou...]
    ppermute x5 -> x4, waiting for transfers between devices: 4.6 us -> 0.59 us  [trade(): return lax.ppermute(value, 'blk', [(0, 1), (1, 0)])]
    pallas_call x1, Pallas kernels: 4.67 us -> 2.67 us  [input_back_call(): pl.pallas_call(lambda *refs: input_back_kernel(by_hand, *refs), in_specs=...]
    unnamed x48 -> x34, local copies, waits for them, and re-layouts: 4.04 us -> 2.12 us
    select_n x2 -> x0, other arithmetic: 1.88 us -> none  [join(): jnp.where(side == 0, jnp.concatenate([own, other], axis=0), jnp.concatena...]
    all_to_all x1, waiting for transfers between devices: 5.67 us -> 7.48 us  [local(): notes = lax.all_to_all(notes, grid.axes, 0, 0, tiled=True)]
  transfers between devices with their start and end apart: 52 -> 50, of which waited for: 21 -> 22; matrix products, arithmetic and copies ran while one was open for 2% -> 1% of each run, Pallas kernels for 18% -> 17%
where the time goes in v3:
time: 154 us; the launch traced here: 153 us
  waiting for transfers between devices  68.7 us (45%)
  Pallas kernels  44.3 us (29%)
  starting transfers between devices  35.3 us (23%)
  local copies, waits for them, and re-layouts  2.12 us (1%)
  other arithmetic  2.09 us (1%)
    ppermute x45, waiting for transfers between devices, send(): return lax.ppermute(value, self.axes, pairs)  60.6 us
    ppermute x45, starting transfers between devices, send(): return lax.ppermute(value, self.axes, pairs)  27.5 us
    pallas_call x1, Pallas kernels, middle_call(): pl.pallas_call(lambda *refs: middle_kernel(by_hand, *refs), grid=(TILES,)...  14.4 us
    pallas_call x1, Pallas kernels, attention_back_call(): pl.pallas_call(attention_back_kernel, in_specs=[VMEM] * len(operands), ou...  8.61 us
    pallas_call x1, Pallas kernels, forward_call(): pl.pallas_call(forward_kernel, in_specs=[SMEM] + [VMEM] * (len(operands)...  7.7 us
    all_to_all x1, waiting for transfers between devices, local(): notes = lax.all_to_all(notes, grid.axes, 0, 0, tiled=True)  7.48 us
    ppermute x4, starting transfers between devices, trade(): return lax.ppermute(value, 'blk', [(0, 1), (1, 0)])  4.69 us
    all_to_all x1, starting transfers between devices, local(): notes = lax.all_to_all(notes, grid.axes, 0, 0, tiled=True)  3.12 us
  transfers between devices with their start and end apart: 50, of which 22 were waited for; matrix products, arithmetic and copies ran while one was open for 1% of the time, Pallas kernels for 17%

profile of v3, /device:TPU:0, one launch (start us, length us, event | category | flops | bytes accessed | tf_op | source)
XLA Modules:
  0.0 153.5 jit_solution(18362802535775161125)
XLA Ops:
  1.7 3.0 %collective-permute-start.10 = (bf16[864,128]{1,0:T(8,128)(2,1)S(1)}, bf16[864,128]{1,0:T(8,128)(2,1)S(1)}, u32[]{:S(2)}, u32[]{:S(2)}) collective-permute-start(bf16[864,128]{1,0:T(8,128)(2,1)S(1)} %bitcast_convert_fusion.refs_0_), channel_id=1, source_target_pairs={{0,1},{1,0},{2,6},{3,7},{4,5},{5,4},{6,2},{7,3},{8,9},{9,8},{10,14... | collective-permute-start | bytes 663560 | tf_op jit(solution)/shard_map/ppermute | solution.py:808
  7.8 2.6 %collective-permute-start = (bf16[864,128]{1,0:T(8,128)(2,1)S(1)}, bf16[864,128]{1,0:T(8,128)(2,1)S(1)}, u32[]{:S(2)}, u32[]{:S(2)}) collective-permute-start(bf16[864,128]{1,0:T(8,128)(2,1)S(1)} %bitcast_convert_fusion.refs_0_), channel_id=1, source_target_pairs={{0,16},{1,17},{2,18},{3,19},{4,20},{5,21},{6,22},{7,23},{8,24},{9,... | collective-permute-start | bytes 663560 | tf_op jit(solution)/shard_map/ppermute | solution.py:808
  10.7 2.3 %collective-permute-start.12 = (bf16[864,128]{1,0:T(8,128)(2,1)S(1)}, bf16[864,128]{1,0:T(8,128)(2,1)S(1)}, u32[]{:S(2)}, u32[]{:S(2)}) collective-permute-start(bf16[864,128]{1,0:T(8,128)(2,1)S(1)} %collective-permute-done.8.refs_2_), channel_id=1, source_target_pairs={{0,1},{1,0},{2,6},{3,7},{4,5},{5,4},{6,2},{7,3},{8,9},{9,8},{10,14... | collective-permute-start | bytes 663560 | tf_op jit(solution)/shard_map/ppermute | solution.py:808
  13.0 5.7 %collective-permute-done.2.refs_8_ = bf16[864,128]{1,0:T(8,128)(2,1)S(1)} collective-permute-done((bf16[864,128]{1,0:T(8,128)(2,1)S(1)}, bf16[864,128]{1,0:T(8,128)(2,1)S(1)}, u32[]{:S(2)}, u32[]{:S(2)}) %collective-permute-start.2) | collective-permute-done | bytes 221216 | tf_op jit(solution)/shard_map/ppermute | solution.py:808
  25.5 2.3 %collective-permute-done.3.refs_10_ = bf16[864,128]{1,0:T(8,128)(2,1)S(1)} collective-permute-done((bf16[864,128]{1,0:T(8,128)(2,1)S(1)}, bf16[864,128]{1,0:T(8,128)(2,1)S(1)}, u32[]{:S(2)}, u32[]{:S(2)}) %collective-permute-start.3) | collective-permute-done | bytes 221216 | tf_op jit(solution)/shard_map/ppermute | solution.py:808
  27.8 3.9 %collective-permute-done.21.refs_18_ = bf16[864,128]{1,0:T(8,128)(2,1)S(1)} collective-permute-done((bf16[864,128]{1,0:T(8,128)(2,1)S(1)}, bf16[864,128]{1,0:T(8,128)(2,1)S(1)}, u32[]{:S(2)}, u32[]{:S(2)}) %collective-permute-start.21) | collective-permute-done | bytes 221216 | tf_op jit(solution)/shard_map/ppermute | solution.py:808
  32.8 2.3 %collective-permute-done.18.refs_14_ = bf16[864,128]{1,0:T(8,128)(2,1)S(1)} collective-permute-done((bf16[864,128]{1,0:T(8,128)(2,1)S(1)}, bf16[864,128]{1,0:T(8,128)(2,1)S(1)}, u32[]{:S(2)}, u32[]{:S(2)}) %collective-permute-start.18) | collective-permute-done | bytes 221216 | tf_op jit(solution)/shard_map/ppermute | solution.py:808
  36.3 2.2 %collective-permute-done.25.refs_22_ = bf16[864,128]{1,0:T(8,128)(2,1)S(1)} collective-permute-done((bf16[864,128]{1,0:T(8,128)(2,1)S(1)}, bf16[864,128]{1,0:T(8,128)(2,1)S(1)}, u32[]{:S(2)}, u32[]{:S(2)}) %collective-permute-start.25) | collective-permute-done | bytes 221216 | tf_op jit(solution)/shard_map/ppermute | solution.py:808
  43.9 4.1 %collective-permute-done.29.refs_28_ = bf16[864,128]{1,0:T(8,128)(2,1)S(1)} collective-permute-done((bf16[864,128]{1,0:T(8,128)(2,1)S(1)}, bf16[864,128]{1,0:T(8,128)(2,1)S(1)}, u32[]{:S(2)}, u32[]{:S(2)}) %collective-permute-start.29) | collective-permute-done | bytes 221216 | tf_op jit(solution)/shard_map/ppermute | solution.py:808
  53.3 2.6 %shard_map.179.lines.refs_5_ = bf16[27648,128]{1,0:T(8,128)(2,1)S(1)} custom-call(bf16[864,128]{1,0:T(8,128)(2,1)S(1)} %bitcast_convert_fusion.refs_0_, bf16[864,128]{1,0:T(8,128)(2,1)S(1)} %collective-permute-done.7.refs_1_, bf16[864,128]{1,0:T(8,128)(2,1)S(1)} %collective-permute-done.8.refs_2_, bf16[864,128]{1,0:T(8,128)(2,1)S(1)} %collective-permute-done.9.refs_3_, ...), custom_call_target="tpu_custom_call" | custom-call | bytes 1048576 | tf_op jit(solution)/shard_map/pallas_call | solution.py:92
  56.0 7.7 %shard_map.180 = (bf16[32,256,256]{2,1,0:T(8,128)(2,1)S(1)}, f32[32,256]{1,0:T(8,128)S(1)}, bf16[512,1536]{1,0:T(8,128)(2,1)S(1)}, bf16[512,512]{1,0:T(8,128)(2,...) custom-call(s32[4]{0:T(128)S(1)} %copy-done.16, ...), custom_call_target="tpu_custom_call" | custom-call | flops 6000000000 | bytes 16777216 | tf_op jit(solution)/shard_map/pallas_call | solution.py:346
  63.7 14.4 %shard_map.181 = (f32[2,128,512]{2,1,0:T(8,128)S(1)}, bf16[2,128,512]{2,1,0:T(8,128)(2,1)S(1)}, f32[512,512]{1,0:T(8,128)S(1)}, f32[512,128]{1,0:T(8,128)S(1)}, ...) custom-call(s32[4]{0:T(128)S(1)} %copy-done.16, ...), custom_call_target="tpu_custom_call" | custom-call | flops 8000000000 | bytes 16777216 | tf_op jit(solution)/shard_map/pallas_call | solution.py:501
  79.7 2.1 %collective-permute-done.34.refs_1_ = bf16[6912,128]{1,0:T(8,128)(2,1)S(1)} collective-permute-done((bf16[6912,128]{1,0:T(8,128)(2,1)S(1)}, bf16[6912,128]{1,0:T(8,128)(2,1)S(1)}, u32[]{:S(2)}, u32[]{:S(2)}) %collective-permute-start.34) | collective-permute-done | bytes 1769504 | tf_op jit(solution)/shard_map/ppermute | solution.py:808
  82.6 8.6 %shard_map.184 = (bf16[6144,128]{1,0:T(8,128)(2,1)S(1)}, f32[512,512]{1,0:T(8,128)S(1)}, f32[8,512]{1,0:T(8,128)S(1)}) custom-call(bf16[32,256,256]{2,1,0:T(8,128)(2,1)S(1)} %get-tuple-element.96.probs, f32[32,256]{1,0:T(8,128)S(1)} %get-tuple-element.97.shares, bf16[512,1536]{1,0:T(8,128)(2,1)S(1)} %get-tuple-element.98.joint, ...), custom_call_target="tpu_custom_call" | custom-call | flops 8000000000 | bytes 4194304 | tf_op jit(solution)/shard_map/pallas_call | solution.py:652
  91.3 3.9 %collective-permute-done.35.refs_2_ = bf16[3456,128]{1,0:T(8,128)(2,1)S(1)} collective-permute-done((bf16[3456,128]{1,0:T(8,128)(2,1)S(1)}, bf16[3456,128]{1,0:T(8,128)(2,1)S(1)}, u32[]{:S(2)}, u32[]{:S(2)}) %collective-permute-start.35) | collective-permute-done | bytes 884768 | tf_op jit(solution)/shard_map/ppermute | solution.py:808
  95.3 2.7 %shard_map.186 = (bf16[3584,128]{1,0:T(8,128)(2,1)S(1)}, bf16[3584,128]{1,0:T(8,128)(2,1)S(1)}, bf16[3456,128]{1,0:T(8,128)(2,1)S(1)}, bf16[3456,128]{1,0:T(8,12...) custom-call(f32[512,512]{1,0:T(8,128)S(1)} %get-tuple-element.116.refs_0_, ...), custom_call_target="tpu_custom_call" | custom-call | flops 4000000000 | bytes 8388608 | tf_op jit(solution)/shard_map/pallas_call | solution.py:782
  103.4 10.9 %collective-permute-done.38.refs_3_ = bf16[1728,128]{1,0:T(8,128)(2,1)S(1)} collective-permute-done((bf16[1728,128]{1,0:T(8,128)(2,1)S(1)}, bf16[1728,128]{1,0:T(8,128)(2,1)S(1)}, u32[]{:S(2)}, u32[]{:S(2)}) %collective-permute-start.38) | collective-permute-done | bytes 442400 | tf_op jit(solution)/shard_map/ppermute | solution.py:808
  115.8 4.6 %collective-permute-done.40.refs_2_ = bf16[1728,128]{1,0:T(8,128)(2,1)S(1)} collective-permute-done((bf16[1728,128]{1,0:T(8,128)(2,1)S(1)}, bf16[1728,128]{1,0:T(8,128)(2,1)S(1)}, u32[]{:S(2)}, u32[]{:S(2)}) %collective-permute-start.40) | collective-permute-done | bytes 442400 | tf_op jit(solution)/shard_map/ppermute | solution.py:808
  122.1 4.4 %collective-permute-done.43.refs_3_ = bf16[864,128]{1,0:T(8,128)(2,1)S(1)} collective-permute-done((bf16[864,128]{1,0:T(8,128)(2,1)S(1)}, bf16[864,128]{1,0:T(8,128)(2,1)S(1)}, u32[]{:S(2)}, u32[]{:S(2)}) %collective-permute-start.43) | collective-permute-done | bytes 221216 | tf_op jit(solution)/shard_map/ppermute | solution.py:808
  127.1 2.8 %collective-permute-start.47 = (bf16[448,128]{1,0:T(8,128)(2,1)S(1)}, bf16[448,128]{1,0:T(8,128)(2,1)S(1)}, u32[]{:S(2)}, u32[]{:S(2)}) collective-permute-start(bf16[448,128]{1,0:T(8,128)(2,1)S(1)} %shard_map.198), channel_id=1, source_target_pairs={{0,16},{1,17},{2,18},{3,19},{4,20},{5,21},{6,22},{7,23},{8,24},{9,... | collective-permute-start | bytes 344072 | tf_op jit(solution)/shard_map/ppermute | solution.py:808
  129.9 3.4 %collective-permute-done.45.refs_4_ = bf16[432,128]{1,0:T(8,128)(2,1)S(1)} collective-permute-done((bf16[432,128]{1,0:T(8,128)(2,1)S(1)}, bf16[432,128]{1,0:T(8,128)(2,1)S(1)}, u32[]{:S(2)}, u32[]{:S(2)}) %collective-permute-start.45) | collective-permute-done | bytes 110624 | tf_op jit(solution)/shard_map/ppermute | solution.py:808
  134.9 4.3 %collective-permute-done.48.two_far = bf16[432,128]{1,0:T(8,128)(2,1)S(1)} collective-permute-done((bf16[432,128]{1,0:T(8,128)(2,1)S(1)}, bf16[432,128]{1,0:T(8,128)(2,1)S(1)}, u32[]{:S(2)}, u32[]{:S(2)}) %collective-permute-start.48) | collective-permute-done | bytes 110624 | tf_op jit(solution)/shard_map/ppermute | solution.py:808
  140.2 3.1 %all-to-all-start = ((f32[32,8,128]{2,1,0:T(8,128)}), f32[32,8,128]{2,1,0:T(8,128)S(1)}, u32[]{:S(2)}, u32[]{:S(2)}) async-start(f32[32,8,128]{2,1,0:T(8,128)} %get-tuple-element.145), calls=%async_computation | async-start | bytes 262144 | tf_op jit(solution)/shard_map/all_to_all | solution.py:1117
  144.4 7.5 %all-to-all-done.notes = f32[32,8,128]{2,1,0:T(8,128)S(1)} async-done(((f32[32,8,128]{2,1,0:T(8,128)}), f32[32,8,128]{2,1,0:T(8,128)S(1)}, u32[]{:S(2)}, u32[]{:S(2)}) %all-to-all-start) | async-done | bytes 131104 | tf_op jit(solution)/shard_map/all_to_all | solution.py:1117
  (140 shorter events, 40.9 us)
Async XLA Ops:
  1.7 8.8 %collective-permute-start.10 = (bf16[864,128]{1,0:T(8,128)(2,1)S(1)}, bf16[864,128]{1,0:T(8,128)(2,1)S(1)}, u32[]{:S(2)}, u32[]{:S(2)}) collective-permute-start(bf16[864,128]{1,0:T(8,128)(2,1)S(1)} %bitcast_convert_fusion.refs_0_), channel_id=1, source_target_pairs={{0,1},{1,0},{2,6},{3,7},{4,5},{5,4},{6,2},{7,3},{8,9},{9,8},{10,14... | collective-permute-start | bytes 663560 | tf_op jit(solution)/shard_map/ppermute | solution.py:808
  6.2 12.5 %collective-permute-start.2 = (bf16[864,128]{1,0:T(8,128)(2,1)S(1)}, bf16[864,128]{1,0:T(8,128)(2,1)S(1)}, u32[]{:S(2)}, u32[]{:S(2)}) collective-permute-start(bf16[864,128]{1,0:T(8,128)(2,1)S(1)} %bitcast_convert_fusion.refs_0_), channel_id=1, source_target_pairs={{0,8},{1,9},{2,10},{3,11},{4,12},{5,13},{6,14},{7,15},{8,0},{9,1},... | collective-permute-start | bytes 663560 | tf_op jit(solution)/shard_map/ppermute | solution.py:808
  7.8 13.2 %collective-permute-start = (bf16[864,128]{1,0:T(8,128)(2,1)S(1)}, bf16[864,128]{1,0:T(8,128)(2,1)S(1)}, u32[]{:S(2)}, u32[]{:S(2)}) collective-permute-start(bf16[864,128]{1,0:T(8,128)(2,1)S(1)} %bitcast_convert_fusion.refs_0_), channel_id=1, source_target_pairs={{0,16},{1,17},{2,18},{3,19},{4,20},{5,21},{6,22},{7,23},{8,24},{9,... | collective-permute-start | bytes 663560 | tf_op jit(solution)/shard_map/ppermute | solution.py:808
  10.5 10.6 %collective-permute-start.11 = (bf16[864,128]{1,0:T(8,128)(2,1)S(1)}, bf16[864,128]{1,0:T(8,128)(2,1)S(1)}, u32[]{:S(2)}, u32[]{:S(2)}) collective-permute-start(bf16[864,128]{1,0:T(8,128)(2,1)S(1)} %collective-permute-done.10.refs_4_), channel_id=1, source_target_pairs={{0,2},{1,3},{2,0},{3,1},{4,6},{5,7},{6,4},{7,5},{8,10},{9,11},{10,... | collective-permute-start | bytes 663560 | tf_op jit(solution)/shard_map/ppermute | solution.py:808
  10.7 10.9 %collective-permute-start.12 = (bf16[864,128]{1,0:T(8,128)(2,1)S(1)}, bf16[864,128]{1,0:T(8,128)(2,1)S(1)}, u32[]{:S(2)}, u32[]{:S(2)}) collective-permute-start(bf16[864,128]{1,0:T(8,128)(2,1)S(1)} %collective-permute-done.8.refs_2_), channel_id=1, source_target_pairs={{0,1},{1,0},{2,6},{3,7},{4,5},{5,4},{6,2},{7,3},{8,9},{9,8},{10,14... | collective-permute-start | bytes 663560 | tf_op jit(solution)/shard_map/ppermute | solution.py:808
  13.0 10.1 %collective-permute-start.9 = (bf16[864,128]{1,0:T(8,128)(2,1)S(1)}, bf16[864,128]{1,0:T(8,128)(2,1)S(1)}, u32[]{:S(2)}, u32[]{:S(2)}) collective-permute-start(bf16[864,128]{1,0:T(8,128)(2,1)S(1)} %collective-permute-done.8.refs_2_), channel_id=1, source_target_pairs={{0,2},{1,3},{2,0},{3,1},{4,6},{5,7},{6,4},{7,5},{8,10},{9,11},{10,... | collective-permute-start | bytes 663560 | tf_op jit(solution)/shard_map/ppermute | solution.py:808
  21.6 10.1 %collective-permute-start.21 = (bf16[864,128]{1,0:T(8,128)(2,1)S(1)}, bf16[864,128]{1,0:T(8,128)(2,1)S(1)}, u32[]{:S(2)}, u32[]{:S(2)}) collective-permute-start(bf16[864,128]{1,0:T(8,128)(2,1)S(1)} %collective-permute-done.refs_16_), channel_id=1, source_target_pairs={{0,4},{1,5},{2,3},{3,2},{4,0},{5,1},{6,7},{7,6},{8,12},{9,13},{10,... | collective-permute-start | bytes 663560 | tf_op jit(solution)/shard_map/ppermute | solution.py:808
  23.1 8.6 %collective-permute-start.1 = (bf16[864,128]{1,0:T(8,128)(2,1)S(1)}, bf16[864,128]{1,0:T(8,128)(2,1)S(1)}, u32[]{:S(2)}, u32[]{:S(2)}) collective-permute-start(bf16[864,128]{1,0:T(8,128)(2,1)S(1)} %collective-permute-done.refs_16_), channel_id=1, source_target_pairs={{0,8},{1,9},{2,10},{3,11},{4,12},{5,13},{6,14},{7,15},{8,0},{9,1},... | collective-permute-start | bytes 663560 | tf_op jit(solution)/shard_map/ppermute | solution.py:808
  25.0 7.2 %collective-permute-start.23 = (bf16[864,128]{1,0:T(8,128)(2,1)S(1)}, bf16[864,128]{1,0:T(8,128)(2,1)S(1)}, u32[]{:S(2)}, u32[]{:S(2)}) collective-permute-start(bf16[864,128]{1,0:T(8,128)(2,1)S(1)} %collective-permute-done.refs_16_), channel_id=1, source_target_pairs={{0,1},{1,0},{2,6},{3,7},{4,5},{5,4},{6,2},{7,3},{8,9},{9,8},{10,14... | collective-permute-start | bytes 663560 | tf_op jit(solution)/shard_map/ppermute | solution.py:808
  25.5 7.0 %collective-permute-start.20 = (bf16[864,128]{1,0:T(8,128)(2,1)S(1)}, bf16[864,128]{1,0:T(8,128)(2,1)S(1)}, u32[]{:S(2)}, u32[]{:S(2)}) collective-permute-start(bf16[864,128]{1,0:T(8,128)(2,1)S(1)} %collective-permute-done.refs_16_), channel_id=1, source_target_pairs={{0,2},{1,3},{2,0},{3,1},{4,6},{5,7},{6,4},{7,5},{8,10},{9,11},{10,... | collective-permute-start | bytes 663560 | tf_op jit(solution)/shard_map/ppermute | solution.py:808
  27.8 7.3 %collective-permute-start.18 = (bf16[864,128]{1,0:T(8,128)(2,1)S(1)}, bf16[864,128]{1,0:T(8,128)(2,1)S(1)}, u32[]{:S(2)}, u32[]{:S(2)}) collective-permute-start(bf16[864,128]{1,0:T(8,128)(2,1)S(1)} %collective-permute-done.12.refs_6_), channel_id=1, source_target_pairs={{0,8},{1,9},{2,10},{3,11},{4,12},{5,13},{6,14},{7,15},{8,0},{9,1},... | collective-permute-start | bytes 663560 | tf_op jit(solution)/shard_map/ppermute | solution.py:808
  31.7 6.8 %collective-permute-start.25 = (bf16[864,128]{1,0:T(8,128)(2,1)S(1)}, bf16[864,128]{1,0:T(8,128)(2,1)S(1)}, u32[]{:S(2)}, u32[]{:S(2)}) collective-permute-start(bf16[864,128]{1,0:T(8,128)(2,1)S(1)} %collective-permute-done.21.refs_18_), channel_id=1, source_target_pairs={{0,1},{1,0},{2,6},{3,7},{4,5},{5,4},{6,2},{7,3},{8,9},{9,8},{10,14... | collective-permute-start | bytes 663560 | tf_op jit(solution)/shard_map/ppermute | solution.py:808
  32.2 8.8 %collective-permute-start.17 = (bf16[864,128]{1,0:T(8,128)(2,1)S(1)}, bf16[864,128]{1,0:T(8,128)(2,1)}, u32[]{:S(2)}, u32[]{:S(2)}) collective-permute-start(bf16[864,128]{1,0:T(8,128)(2,1)S(1)} %collective-permute-done.16.refs_12_), channel_id=1, source_target_pairs={{0,2},{1,3},{2,0},{3,1},{4,6},{5,7},{6,4},{7,5},{8,10},{9,11},{10,... | collective-permute-start | bytes 663560 | tf_op jit(solution)/shard_map/ppermute | solution.py:808
  32.5 9.1 %collective-permute-start.15 = (bf16[864,128]{1,0:T(8,128)(2,1)S(1)}, bf16[864,128]{1,0:T(8,128)(2,1)}, u32[]{:S(2)}, u32[]{:S(2)}) collective-permute-start(bf16[864,128]{1,0:T(8,128)(2,1)S(1)} %collective-permute-done.3.refs_10_), channel_id=1, source_target_pairs={{0,2},{1,3},{2,0},{3,1},{4,6},{5,7},{6,4},{7,5},{8,10},{9,11},{10,... | collective-permute-start | bytes 663560 | tf_op jit(solution)/shard_map/ppermute | solution.py:808
  41.0 7.0 %collective-permute-start.29 = (bf16[864,128]{1,0:T(8,128)(2,1)S(1)}, bf16[864,128]{1,0:T(8,128)(2,1)S(1)}, u32[]{:S(2)}, u32[]{:S(2)}) collective-permute-start(bf16[864,128]{1,0:T(8,128)(2,1)S(1)} %collective-permute-done.1.refs_24_), channel_id=1, source_target_pairs={{0,1},{1,0},{2,6},{3,7},{4,5},{5,4},{6,2},{7,3},{8,9},{9,8},{10,14... | collective-permute-start | bytes 663560 | tf_op jit(solution)/shard_map/ppermute | solution.py:808
  41.6 8.0 %collective-permute-start.31 = (bf16[864,128]{1,0:T(8,128)(2,1)}, bf16[864,128]{1,0:T(8,128)(2,1)S(1)}, u32[]{:S(2)}, u32[]{:S(2)}) collective-permute-start(bf16[864,128]{1,0:T(8,128)(2,1)} %copy-done.8), channel_id=1, source_target_pairs={{0,8},{1,9},{2,10},{3,11},{4,12},{5,13},{6,14},{7,15},{8,0},{9,1},... | collective-permute-start | bytes 663560 | tf_op jit(solution)/shard_map/ppermute | solution.py:808
  51.7 12.0 %collective-permute-start.33 = (bf16[2,128,512]{2,1,0:T(8,128)(2,1)S(1)}, bf16[2,128,512]{2,1,0:T(8,128)(2,1)S(1)}, u32[]{:S(2)}, u32[]{:S(2)}) collective-permute-start(bf16[2,128,512]{2,1,0:T(8,128)(2,1)S(1)} %get-tuple-element.94), channel_id=1, source_target_pairs={{0,1},{1,0},{2,3},{3,2},{4,5},{5,4},{6,7},{7,6},{8,9},{9,8},{10,11... | collective-permute-start | bytes 786440 | tf_op jit(solution)/shard_map/ppermute | solution.py:1064
  82.1 13.1 %collective-permute-start.35 = (bf16[3456,128]{1,0:T(8,128)(2,1)S(1)}, bf16[3456,128]{1,0:T(8,128)(2,1)S(1)}, u32[]{:S(2)}, u32[]{:S(2)}) collective-permute-start(bf16[3456,128]{1,0:T(8,128)(2,1)S(1)} %shard_map.183), channel_id=1, source_target_pairs={{0,1},{1,0},{2,6},{3,7},{4,5},{5,4},{6,2},{7,3},{8,9},{9,8},{10,14... | collective-permute-start | bytes 2654216 | tf_op jit(solution)/shard_map/ppermute | solution.py:808
  100.6 13.8 %collective-permute-start.39 = (bf16[1792,128]{1,0:T(8,128)(2,1)S(1)}, bf16[1792,128]{1,0:T(8,128)(2,1)S(1)}, u32[]{:S(2)}, u32[]{:S(2)}) collective-permute-start(bf16[1792,128]{1,0:T(8,128)(2,1)S(1)} %shard_map.187), channel_id=1, source_target_pairs={{0,1},{1,0},{2,6},{3,7},{4,5},{5,4},{6,2},{7,3},{8,9},{9,8},{10,14... | collective-permute-start | bytes 1376264 | tf_op jit(solution)/shard_map/ppermute | solution.py:808
  101.2 13.1 %collective-permute-start.38 = (bf16[1728,128]{1,0:T(8,128)(2,1)S(1)}, bf16[1728,128]{1,0:T(8,128)(2,1)S(1)}, u32[]{:S(2)}, u32[]{:S(2)}) collective-permute-start(bf16[1728,128]{1,0:T(8,128)(2,1)S(1)} %shard_map.185), channel_id=1, source_target_pairs={{0,4},{1,5},{2,3},{3,2},{4,0},{5,1},{6,7},{7,6},{8,12},{9,13},{10,... | collective-permute-start | bytes 1327112 | tf_op jit(solution)/shard_map/ppermute | solution.py:808
  101.9 18.5 %collective-permute-start.40 = (bf16[1728,128]{1,0:T(8,128)(2,1)S(1)}, bf16[1728,128]{1,0:T(8,128)(2,1)S(1)}, u32[]{:S(2)}, u32[]{:S(2)}) collective-permute-start(bf16[1728,128]{1,0:T(8,128)(2,1)S(1)} %shard_map.188), channel_id=1, source_target_pairs={{0,1},{1,0},{2,6},{3,7},{4,5},{5,4},{6,2},{7,3},{8,9},{9,8},{10,14... | collective-permute-start | bytes 1327112 | tf_op jit(solution)/shard_map/ppermute | solution.py:808
  127.1 12.1 %collective-permute-start.47 = (bf16[448,128]{1,0:T(8,128)(2,1)S(1)}, bf16[448,128]{1,0:T(8,128)(2,1)S(1)}, u32[]{:S(2)}, u32[]{:S(2)}) collective-permute-start(bf16[448,128]{1,0:T(8,128)(2,1)S(1)} %shard_map.198), channel_id=1, source_target_pairs={{0,16},{1,17},{2,18},{3,19},{4,20},{5,21},{6,22},{7,23},{8,24},{9,... | collective-permute-start | bytes 344072 | tf_op jit(solution)/shard_map/ppermute | solution.py:808
  133.8 9.5 %collective-permute-start.46 = (bf16[2,176,512]{2,1,0:T(8,128)(2,1)S(1)}, bf16[2,176,512]{2,1,0:T(8,128)(2,1)S(1)}, u32[]{:S(2)}, u32[]{:S(2)}) collective-permute-start(bf16[2,176,512]{2,1,0:T(8,128)(2,1)S(1)} %get-tuple-element.141), channel_id=1, source_target_pairs={{0,1},{1,0},{2,3},{3,2},{4,5},{5,4},{6,7},{7,6},{8,9},{9,8},{10,11... | collective-permute-start | bytes 1081352 | tf_op jit(solution)/shard_map/ppermute | solution.py:1064
  140.2 11.7 %all-to-all-start = ((f32[32,8,128]{2,1,0:T(8,128)}), f32[32,8,128]{2,1,0:T(8,128)S(1)}, u32[]{:S(2)}, u32[]{:S(2)}) async-start(f32[32,8,128]{2,1,0:T(8,128)} %get-tuple-element.145), calls=%async_computation | async-start | bytes 262144 | tf_op jit(solution)/shard_map/all_to_all | solution.py:1117
  (43 other events, 361.6 us)

commit v4 on v3

--- a/solution.py
+++ b/solution.py
@@ -641,35 +641,6 @@
     rows_out[1:2, :] = total(grad)
     back_start[...] = back_middle[...] + norm_back(grad, hat, scale, vectors[2:3, :])
     joint_lines[...] = grads[...].astype(BF)
-
-
-def attention_back_call(*operands):
-    outs = (
-        pltpu.VMEM((OUTPUT_AT - JOINT_AT, LANES), BF),
-        pltpu.VMEM((TOKENS, D), F32),
-        pltpu.VMEM((8, D), F32),
-    )
-    return pl.pallas_call(
-        attention_back_kernel,
-        in_specs=[VMEM] * len(operands),
-        out_shape=outs,
-        out_specs=tuple(VMEM for _ in outs),
-        scratch_shapes=[
-            pltpu.VMEM((TOKENS, 3 * D), BF),
-            pltpu.VMEM((D, TOKENS), BF),
-            pltpu.VMEM((D, TOKENS), BF),
-            pltpu.VMEM((D, TOKENS), BF),
-            pltpu.VMEM((TOKENS, D), BF),
-            pltpu.VMEM((D, TOKENS), BF),
-            pltpu.VMEM((GROUP, SLOTS, SLOTS), F32),
-            pltpu.VMEM((GROUP, SLOTS, SLOTS), F32),
-            pltpu.VMEM((OUTPUT_AT - JOINT_AT, LANES), F32),
-        ],
-        compiler_params=pltpu.CompilerParams(vmem_limit_bytes=16 * 2**20),
-        cost_estimate=pl.CostEstimate(
-            flops=8 * 10**9, bytes_accessed=4 * 2**20, transcendentals=0
-        ),
-    )(*operands)
 
 
 def input_back_kernel(
@@ -768,7 +739,20 @@
         store(index, jnp.concatenate(parts, axis=0) if len(parts) > 1 else parts[0])
 
 
-def input_back_call(by_hand, *operands):
+def back_kernel(by_hand, *refs):
+    attention, (my_latents, choices, embed_w, out_lines, head_lines, rows_in, expand_in, far_out) = (
+        refs[:9], refs[9:17],
+    )
+    outs, scratch = refs[17:24], refs[24:]
+    joint_lines, back_start, rows_joint = scratch[:3]
+    attention_back_kernel(*attention, joint_lines, back_start, rows_joint, *scratch[3:12])
+    input_back_kernel(
+        by_hand, back_start, my_latents, choices, embed_w, joint_lines, rows_joint, out_lines,
+        head_lines, rows_in, expand_in, far_out, *outs, *scratch[12:],
+    )
+
+
+def back_call(by_hand, *operands):
     shape = jax.ShapeDtypeStruct
     outs = (
         pltpu.VMEM((8 * PARTS[0], LANES), BF),
@@ -780,11 +764,23 @@
         pltpu.VMEM((MINE, PACK, D), BF),
     )
     return pl.pallas_call(
-        lambda *refs: input_back_kernel(by_hand, *refs),
+        lambda *refs: back_kernel(by_hand, *refs),
         in_specs=[VMEM] * len(operands),
         out_shape=outs,
         out_specs=tuple(VMEM for _ in outs),
         scratch_shapes=[
+            pltpu.VMEM((OUTPUT_AT - JOINT_AT, LANES), BF),
+            pltpu.VMEM((TOKENS, D), F32),
+            pltpu.VMEM((8, D), F32),
+            pltpu.VMEM((TOKENS, 3 * D), BF),
+            pltpu.VMEM((D, TOKENS), BF),
+            pltpu.VMEM((D, TOKENS), BF),
+            pltpu.VMEM((D, TOKENS), BF),
+            pltpu.VMEM((TOKENS, D), BF),
+            pltpu.VMEM((D, TOKENS), BF),
+            pltpu.VMEM((GROUP, SLOTS, SLOTS), F32),
+            pltpu.VMEM((GROUP, SLOTS, SLOTS), F32),
+            pltpu.VMEM((OUTPUT_AT - JOINT_AT, LANES), F32),
             pltpu.VMEM((JOINT_AT, LANES), F32),
             pltpu.VMEM((ROWS * TAIL, LANES), F32),
         ],
@@ -838,16 +834,16 @@
         send("near8", "held8", 4, 1)
         send("side8", "held8", 1, 4)
         send("far8", "far0", 8)
-        send("far16", "near16", 1, 4)
-        send("near24", "held24", 4, 1, behind=("near8",))
-        send("side24", "held24", 1, 4, behind=("side8",))
-        send("far24", "far16", 8, behind=("far8",))
+        send("far16", "near16", 1, 4, behind=("far0",))
+        send("near24", "held24", 4, 1)
+        send("side24", "held24", 1, 4, behind=("near16",))
+        send("far24", "far16", 8)
         lines = put(
             None, "held0", "near0", "side0", "far0", "held8", "near8", "side8", "far8", "held16",
             "near16", "side16", "far16", "held24", "near24", "side24", "far24",
         )
         self.late = (got["side24"], got["far24"])
-        self.early = (got["near24"],)
+        self.early = (got["far8"], got["side24"])
         return lines
 
 
@@ -1085,21 +1081,15 @@
     )
     if by_hand:
         back_mixed = after(back_mixed, high.hop(back_mixed))
-    joint_lines, back_start, rows_joint = attention_back_call(
-        probs, shares, joint, back_mixed, normed, start, back_middle, vectors, joint_w
+    far_one, near_one, far_two, near_two, rows_c, own_latent, pack = back_call(
+        by_hand, probs, shares, joint, back_mixed, normed, start, back_middle, vectors, joint_w,
+        my_latents, choice, embed_w, out_lines, head_lines, rows_b, expand_b, far_out,
     )
     if by_hand:
-        back_start = after(back_start, high.hop(back_start))
-    far_one, near_one, far_two, near_two, rows_c, own_latent, pack = input_back_call(
-        by_hand, back_start, my_latents, choice, embed_w, joint_lines, rows_joint, out_lines,
-        head_lines, rows_b, expand_b,
-        far_out,
-    )
-    if by_hand:
-        one = Reduction(grid, far_one, near_one, 0)
-        two = Reduction(grid, far_two, near_two, 0)
-        mark = far_one
-        for stream in (one, two, high, one, two, high, one, two, one, two):
+        mark = high.hop(far_one)
+        one = Reduction(grid, after(far_one, mark), near_one, 0)
+        two = Reduction(grid, after(far_two, mark), near_two, 0)
+        for stream in (one, two, high, one, high, two, one, two, one, two):
             mark = stream.hop(mark)
             if stream is two:
                 pack_mark = mark

time: 154 us -> 149 us (0.968)
  waiting for transfers between devices: 68.7 us -> 49.1 us
  starting transfers between devices: 35.3 us -> 48.7 us
    ppermute x45, waiting for transfers between devices: 60.6 us -> 39 us  [send(): return lax.ppermute(value, self.axes, pairs)]
    ppermute x45, starting transfers between devices: 27.5 us -> 41.1 us  [send(): return lax.ppermute(value, self.axes, pairs)]
    ppermute x4, waiting for transfers between devices: 0.59 us -> 2.62 us  [trade(): return lax.ppermute(value, 'blk', [(0, 1), (1, 0)])]
    pallas_call x2 -> x1, Pallas kernels: 11.3 us -> 11.4 us  [back_call(): pl.pallas_call(lambda *refs: back_kernel(by_hand, *refs), in_specs=[VMEM]...]
  transfers between devices with their start and end apart: 50 -> 50, of which waited for: 22 -> 20; matrix products, arithmetic and copies ran while one was open for 1% -> 1% of each run, Pallas kernels for 17% -> 19%
where the time goes in v4:
time: 149 us
  waiting for transfers between devices  49.1 us (33%)
  starting transfers between devices  48.7 us (33%)
  Pallas kernels  44.8 us (30%)
  local copies, waits for them, and re-layouts  2.81 us (2%)
  other arithmetic  2.09 us (1%)
    ppermute x45, starting transfers between devices, send(): return lax.ppermute(value, self.axes, pairs)  41.1 us
    ppermute x45, waiting for transfers between devices, send(): return lax.ppermute(value, self.axes, pairs)  39 us
    pallas_call x1, Pallas kernels, middle_call(): pl.pallas_call(lambda *refs: middle_kernel(by_hand, *refs), grid=(TILES,)...  14.6 us
    pallas_call x1, Pallas kernels, back_call(): pl.pallas_call(lambda *refs: back_kernel(by_hand, *refs), in_specs=[VMEM]...  11.4 us
    pallas_call x1, Pallas kernels, forward_call(): pl.pallas_call(forward_kernel, in_specs=[SMEM] + [VMEM] * (len(operands)...  7.71 us
    all_to_all x1, waiting for transfers between devices, local(): notes = lax.all_to_all(notes, grid.axes, 0, 0, tiled=True)  7.48 us
    all_to_all x1, starting transfers between devices, local(): notes = lax.all_to_all(notes, grid.axes, 0, 0, tiled=True)  4.02 us
    ppermute x4, starting transfers between devices, trade(): return lax.ppermute(value, 'blk', [(0, 1), (1, 0)])  3.52 us
  transfers between devices with their start and end apart: 50, of which 20 were waited for; matrix products, arithmetic and copies ran while one was open for 1% of the time, Pallas kernels for 19%

profile of v4, /device:TPU:0, one launch (start us, length us, event | category | flops | bytes accessed | tf_op | source)
XLA Modules:
  0.0 148.5 jit_solution(2448005758797470454)
XLA Ops:
  1.7 3.1 %collective-permute-start.14 = (bf16[864,128]{1,0:T(8,128)(2,1)S(1)}, bf16[864,128]{1,0:T(8,128)(2,1)S(1)}, u32[]{:S(2)}, u32[]{:S(2)}) collective-permute-start(bf16[864,128]{1,0:T(8,128)(2,1)S(1)} %bitcast_convert_fusion.refs_0_), channel_id=1, source_target_pairs={{0,8},{1,9},{2,10},{3,11},{4,12},{5,13},{6,14},{7,15},{8,0},{9,1},... | collective-permute-start | bytes 663560 | tf_op jit(solution)/shard_map/ppermute | solution.py:804
  6.3 2.6 %collective-permute-start.3 = (bf16[864,128]{1,0:T(8,128)(2,1)S(1)}, bf16[864,128]{1,0:T(8,128)(2,1)S(1)}, u32[]{:S(2)}, u32[]{:S(2)}) collective-permute-start(bf16[864,128]{1,0:T(8,128)(2,1)S(1)} %bitcast_convert_fusion.refs_0_), channel_id=1, source_target_pairs={{0,16},{1,17},{2,18},{3,19},{4,20},{5,21},{6,22},{7,23},{8,24},{9,... | collective-permute-start | bytes 663560 | tf_op jit(solution)/shard_map/ppermute | solution.py:804
  10.4 4.5 %collective-permute-start.18 = (bf16[864,128]{1,0:T(8,128)(2,1)S(1)}, bf16[864,128]{1,0:T(8,128)(2,1)S(1)}, u32[]{:S(2)}, u32[]{:S(2)}) collective-permute-start(bf16[864,128]{1,0:T(8,128)(2,1)S(1)} %collective-permute-done.14.refs_8_), channel_id=1, source_target_pairs={{0,1},{1,0},{2,6},{3,7},{4,5},{5,4},{6,2},{7,3},{8,9},{9,8},{10,14... | collective-permute-start | bytes 663560 | tf_op jit(solution)/shard_map/ppermute | solution.py:804
  16.4 3.4 %collective-permute-done.3.refs_16_ = bf16[864,128]{1,0:T(8,128)(2,1)S(1)} collective-permute-done((bf16[864,128]{1,0:T(8,128)(2,1)S(1)}, bf16[864,128]{1,0:T(8,128)(2,1)S(1)}, u32[]{:S(2)}, u32[]{:S(2)}) %collective-permute-start.3) | collective-permute-done | bytes 221216 | tf_op jit(solution)/shard_map/ppermute | solution.py:804
  21.9 1.5 %collective-permute-start.1 = (bf16[864,128]{1,0:T(8,128)(2,1)S(1)}, bf16[864,128]{1,0:T(8,128)(2,1)S(1)}, u32[]{:S(2)}, u32[]{:S(2)}) collective-permute-start(bf16[864,128]{1,0:T(8,128)(2,1)S(1)} %collective-permute-done.refs_2_), channel_id=1, source_target_pairs={{0,1},{1,0},{2,6},{3,7},{4,5},{5,4},{6,2},{7,3},{8,9},{9,8},{10,14... | collective-permute-start | bytes 663560 | tf_op jit(solution)/shard_map/ppermute | solution.py:804
  23.4 4.0 %collective-permute-done.23.refs_20_ = bf16[864,128]{1,0:T(8,128)(2,1)S(1)} collective-permute-done((bf16[864,128]{1,0:T(8,128)(2,1)S(1)}, bf16[864,128]{1,0:T(8,128)(2,1)S(1)}, u32[]{:S(2)}, u32[]{:S(2)}) %collective-permute-start.23) | collective-permute-done | bytes 221216 | tf_op jit(solution)/shard_map/ppermute | solution.py:804
  37.7 2.2 %collective-permute-done.25.refs_22_ = bf16[864,128]{1,0:T(8,128)(2,1)} collective-permute-done((bf16[864,128]{1,0:T(8,128)(2,1)S(1)}, bf16[864,128]{1,0:T(8,128)(2,1)}, u32[]{:S(2)}, u32[]{:S(2)}) %collective-permute-start.25) | collective-permute-done | bytes 221216 | tf_op jit(solution)/shard_map/ppermute | solution.py:804
  44.5 1.6 %collective-permute-done.7.far_latents = bf16[2,32,768]{2,1,0:T(8,128)(2,1)S(1)} collective-permute-done((bf16[2,32,768]{2,1,0:T(8,128)(2,1)S(1)}, bf16[2,32,768]{2,1,0:T(8,128)(2,1)S(1)}, u32[]{:S(2)}, u32[]{:S(2)}) %collective-permute-start.7) | collective-permute-done | bytes 98336 | tf_op jit(solution)/shard_map/ppermute | solution.py:1060
  46.1 1.9 %collective-permute-done.31.refs_30_ = bf16[864,128]{1,0:T(8,128)(2,1)S(1)} collective-permute-done((bf16[864,128]{1,0:T(8,128)(2,1)}, bf16[864,128]{1,0:T(8,128)(2,1)S(1)}, u32[]{:S(2)}, u32[]{:S(2)}) %collective-permute-start.31) | collective-permute-done | bytes 221216 | tf_op jit(solution)/shard_map/ppermute | solution.py:804
  50.5 2.6 %shard_map.179.lines.refs_5_ = bf16[27648,128]{1,0:T(8,128)(2,1)S(1)} custom-call(bf16[864,128]{1,0:T(8,128)(2,1)S(1)} %bitcast_convert_fusion.refs_0_, bf16[864,128]{1,0:T(8,128)(2,1)S(1)} %collective-permute-done.9.refs_1_, bf16[864,128]{1,0:T(8,128)(2,1)S(1)} %collective-permute-done.refs_2_, bf16[864,128]{1,0:T(8,128)(2,1)S(1)} %collective-permute-done.10.refs_3_, ...), custom_call_target="tpu_custom_call" | custom-call | bytes 1048576 | tf_op jit(solution)/shard_map/pallas_call | solution.py:92
  53.1 7.7 %shard_map.180 = (bf16[32,256,256]{2,1,0:T(8,128)(2,1)S(1)}, f32[32,256]{1,0:T(8,128)S(1)}, bf16[512,1536]{1,0:T(8,128)(2,1)S(1)}, bf16[512,512]{1,0:T(8,128)(2,...) custom-call(s32[4]{0:T(128)S(1)} %copy-done.16, ...), custom_call_target="tpu_custom_call" | custom-call | flops 6000000000 | bytes 16777216 | tf_op jit(solution)/shard_map/pallas_call | solution.py:346
  60.9 14.6 %shard_map.181 = (f32[2,128,512]{2,1,0:T(8,128)S(1)}, bf16[2,128,512]{2,1,0:T(8,128)(2,1)S(1)}, f32[512,512]{1,0:T(8,128)S(1)}, f32[512,128]{1,0:T(8,128)S(1)}, ...) custom-call(s32[4]{0:T(128)S(1)} %copy-done.16, ...), custom_call_target="tpu_custom_call" | custom-call | flops 8000000000 | bytes 16777216 | tf_op jit(solution)/shard_map/pallas_call | solution.py:501
  77.2 2.0 %collective-permute-done.34.refs_1_ = bf16[6912,128]{1,0:T(8,128)(2,1)S(1)} collective-permute-done((bf16[6912,128]{1,0:T(8,128)(2,1)S(1)}, bf16[6912,128]{1,0:T(8,128)(2,1)S(1)}, u32[]{:S(2)}, u32[]{:S(2)}) %collective-permute-start.34) | collective-permute-done | bytes 1769504 | tf_op jit(solution)/shard_map/ppermute | solution.py:804
  79.5 1.7 %collective-permute-start.35 = (bf16[3456,128]{1,0:T(8,128)(2,1)S(1)}, bf16[3456,128]{1,0:T(8,128)(2,1)S(1)}, u32[]{:S(2)}, u32[]{:S(2)}) collective-permute-start(bf16[3456,128]{1,0:T(8,128)(2,1)S(1)} %shard_map.183), channel_id=1, source_target_pairs={{0,1},{1,0},{2,6},{3,7},{4,5},{5,4},{6,2},{7,3},{8,9},{9,8},{10,14... | collective-permute-start | bytes 2654216 | tf_op jit(solution)/shard_map/ppermute | solution.py:804
  81.2 11.4 %shard_map.184 = (bf16[3584,128]{1,0:T(8,128)(2,1)S(1)}, bf16[3584,128]{1,0:T(8,128)(2,1)S(1)}, bf16[3456,128]{1,0:T(8,128)(2,1)S(1)}, bf16[3456,128]{1,0:T(8,12...) custom-call(bf16[32,256,256]{2,1,0:T(8,128)(2,1)S(1)} %get-tuple-element.92.refs_0_, ...), custom_call_target="tpu_custom_call" | custom-call | flops 4000000000 | bytes 8388608 | tf_op jit(solution)/shard_map/pallas_call | solution.py:766
  95.4 1.7 %collective-permute-start.39 = (bf16[1792,128]{1,0:T(8,128)(2,1)S(1)}, bf16[1792,128]{1,0:T(8,128)(2,1)S(1)}, u32[]{:S(2)}, u32[]{:S(2)}) collective-permute-start(bf16[1792,128]{1,0:T(8,128)(2,1)S(1)} %shard_map.186), channel_id=1, source_target_pairs={{0,1},{1,0},{2,6},{3,7},{4,5},{5,4},{6,2},{7,3},{8,9},{9,8},{10,14... | collective-permute-start | bytes 1376264 | tf_op jit(solution)/shard_map/ppermute | solution.py:804
  98.4 6.7 %collective-permute-done.38.refs_3_ = bf16[1728,128]{1,0:T(8,128)(2,1)S(1)} collective-permute-done((bf16[1728,128]{1,0:T(8,128)(2,1)S(1)}, bf16[1728,128]{1,0:T(8,128)(2,1)S(1)}, u32[]{:S(2)}, u32[]{:S(2)}) %collective-permute-start.38) | collective-permute-done | bytes 442400 | tf_op jit(solution)/shard_map/ppermute | solution.py:804
  108.2 3.0 %collective-permute-done.40.refs_4_ = bf16[864,128]{1,0:T(8,128)(2,1)S(1)} collective-permute-done((bf16[864,128]{1,0:T(8,128)(2,1)S(1)}, bf16[864,128]{1,0:T(8,128)(2,1)S(1)}, u32[]{:S(2)}, u32[]{:S(2)}) %collective-permute-start.40) | collective-permute-done | bytes 221216 | tf_op jit(solution)/shard_map/ppermute | solution.py:804
  115.4 2.0 %collective-permute-done.43.refs_3_ = bf16[864,128]{1,0:T(8,128)(2,1)S(1)} collective-permute-done((bf16[864,128]{1,0:T(8,128)(2,1)S(1)}, bf16[864,128]{1,0:T(8,128)(2,1)S(1)}, u32[]{:S(2)}, u32[]{:S(2)}) %collective-permute-start.43) | collective-permute-done | bytes 221216 | tf_op jit(solution)/shard_map/ppermute | solution.py:804
  121.4 2.1 %collective-permute-done.45.refs_4_ = bf16[432,128]{1,0:T(8,128)(2,1)S(1)} collective-permute-done((bf16[432,128]{1,0:T(8,128)(2,1)S(1)}, bf16[432,128]{1,0:T(8,128)(2,1)S(1)}, u32[]{:S(2)}, u32[]{:S(2)}) %collective-permute-start.45) | collective-permute-done | bytes 110624 | tf_op jit(solution)/shard_map/ppermute | solution.py:804
  123.7 2.6 %collective-permute-start.48 = (bf16[432,128]{1,0:T(8,128)(2,1)S(1)}, bf16[432,128]{1,0:T(8,128)(2,1)S(1)}, u32[]{:S(2)}, u32[]{:S(2)}) collective-permute-start(bf16[432,128]{1,0:T(8,128)(2,1)S(1)} %shard_map.198), channel_id=1, source_target_pairs={{0,16},{1,17},{2,18},{3,19},{4,20},{5,21},{6,22},{7,23},{8,24},{9,... | collective-permute-start | bytes 331784 | tf_op jit(solution)/shard_map/ppermute | solution.py:804
  127.3 6.0 %collective-permute-done.48.two_far = bf16[432,128]{1,0:T(8,128)(2,1)S(1)} collective-permute-done((bf16[432,128]{1,0:T(8,128)(2,1)S(1)}, bf16[432,128]{1,0:T(8,128)(2,1)S(1)}, u32[]{:S(2)}, u32[]{:S(2)}) %collective-permute-start.48) | collective-permute-done | bytes 110624 | tf_op jit(solution)/shard_map/ppermute | solution.py:804
  134.3 4.0 %all-to-all-start = ((f32[32,8,128]{2,1,0:T(8,128)}), f32[32,8,128]{2,1,0:T(8,128)S(1)}, u32[]{:S(2)}, u32[]{:S(2)}) async-start(f32[32,8,128]{2,1,0:T(8,128)} %get-tuple-element.139), calls=%async_computation | async-start | bytes 262144 | tf_op jit(solution)/shard_map/all_to_all | solution.py:1107
  139.5 7.5 %all-to-all-done.notes = f32[32,8,128]{2,1,0:T(8,128)S(1)} async-done(((f32[32,8,128]{2,1,0:T(8,128)}), f32[32,8,128]{2,1,0:T(8,128)S(1)}, u32[]{:S(2)}, u32[]{:S(2)}) %all-to-all-start) | async-done | bytes 131104 | tf_op jit(solution)/shard_map/all_to_all | solution.py:1107
  (139 shorter events, 47.0 us)
Async XLA Ops:
  1.7 8.7 %collective-permute-start.14 = (bf16[864,128]{1,0:T(8,128)(2,1)S(1)}, bf16[864,128]{1,0:T(8,128)(2,1)S(1)}, u32[]{:S(2)}, u32[]{:S(2)}) collective-permute-start(bf16[864,128]{1,0:T(8,128)(2,1)S(1)} %bitcast_convert_fusion.refs_0_), channel_id=1, source_target_pairs={{0,8},{1,9},{2,10},{3,11},{4,12},{5,13},{6,14},{7,15},{8,0},{9,1},... | collective-permute-start | bytes 663560 | tf_op jit(solution)/shard_map/ppermute | solution.py:804
  4.8 10.1 %collective-permute-start.11 = (bf16[864,128]{1,0:T(8,128)(2,1)S(1)}, bf16[864,128]{1,0:T(8,128)(2,1)S(1)}, u32[]{:S(2)}, u32[]{:S(2)}) collective-permute-start(bf16[864,128]{1,0:T(8,128)(2,1)S(1)} %bitcast_convert_fusion.refs_0_), channel_id=1, source_target_pairs={{0,1},{1,0},{2,6},{3,7},{4,5},{5,4},{6,2},{7,3},{8,9},{9,8},{10,14... | collective-permute-start | bytes 663560 | tf_op jit(solution)/shard_map/ppermute | solution.py:804
  6.3 10.0 %collective-permute-start.9 = (bf16[864,128]{1,0:T(8,128)(2,1)S(1)}, bf16[864,128]{1,0:T(8,128)(2,1)S(1)}, u32[]{:S(2)}, u32[]{:S(2)}) collective-permute-start(bf16[864,128]{1,0:T(8,128)(2,1)S(1)} %bitcast_convert_fusion.refs_0_), channel_id=1, source_target_pairs={{0,2},{1,3},{2,0},{3,1},{4,6},{5,7},{6,4},{7,5},{8,10},{9,11},{10,... | collective-permute-start | bytes 663560 | tf_op jit(solution)/shard_map/ppermute | solution.py:804
  6.3 13.5 %collective-permute-start.3 = (bf16[864,128]{1,0:T(8,128)(2,1)S(1)}, bf16[864,128]{1,0:T(8,128)(2,1)S(1)}, u32[]{:S(2)}, u32[]{:S(2)}) collective-permute-start(bf16[864,128]{1,0:T(8,128)(2,1)S(1)} %bitcast_convert_fusion.refs_0_), channel_id=1, source_target_pairs={{0,16},{1,17},{2,18},{3,19},{4,20},{5,21},{6,22},{7,23},{8,24},{9,... | collective-permute-start | bytes 663560 | tf_op jit(solution)/shard_map/ppermute | solution.py:804
  8.9 10.9 %collective-permute-start = (bf16[864,128]{1,0:T(8,128)(2,1)S(1)}, bf16[864,128]{1,0:T(8,128)(2,1)S(1)}, u32[]{:S(2)}, u32[]{:S(2)}) collective-permute-start(bf16[864,128]{1,0:T(8,128)(2,1)S(1)} %bitcast_convert_fusion.refs_0_), channel_id=1, source_target_pairs={{0,4},{1,5},{2,3},{3,2},{4,0},{5,1},{6,7},{7,6},{8,12},{9,13},{10,... | collective-permute-start | bytes 663560 | tf_op jit(solution)/shard_map/ppermute | solution.py:804
  10.4 10.0 %collective-permute-start.18 = (bf16[864,128]{1,0:T(8,128)(2,1)S(1)}, bf16[864,128]{1,0:T(8,128)(2,1)S(1)}, u32[]{:S(2)}, u32[]{:S(2)}) collective-permute-start(bf16[864,128]{1,0:T(8,128)(2,1)S(1)} %collective-permute-done.14.refs_8_), channel_id=1, source_target_pairs={{0,1},{1,0},{2,6},{3,7},{4,5},{5,4},{6,2},{7,3},{8,9},{9,8},{10,14... | collective-permute-start | bytes 663560 | tf_op jit(solution)/shard_map/ppermute | solution.py:804
  19.8 7.6 %collective-permute-start.23 = (bf16[864,128]{1,0:T(8,128)(2,1)S(1)}, bf16[864,128]{1,0:T(8,128)(2,1)S(1)}, u32[]{:S(2)}, u32[]{:S(2)}) collective-permute-start(bf16[864,128]{1,0:T(8,128)(2,1)S(1)} %collective-permute-done.3.refs_16_), channel_id=1, source_target_pairs={{0,1},{1,0},{2,6},{3,7},{4,5},{5,4},{6,2},{7,3},{8,9},{9,8},{10,14... | collective-permute-start | bytes 663560 | tf_op jit(solution)/shard_map/ppermute | solution.py:804
  20.4 8.3 %collective-permute-start.5 = (bf16[864,128]{1,0:T(8,128)(2,1)S(1)}, bf16[864,128]{1,0:T(8,128)(2,1)S(1)}, u32[]{:S(2)}, u32[]{:S(2)}) collective-permute-start(bf16[864,128]{1,0:T(8,128)(2,1)S(1)} %collective-permute-done.3.refs_16_), channel_id=1, source_target_pairs={{0,4},{1,5},{2,3},{3,2},{4,0},{5,1},{6,7},{7,6},{8,12},{9,13},{10,... | collective-permute-start | bytes 663560 | tf_op jit(solution)/shard_map/ppermute | solution.py:804
  21.8 7.3 %collective-permute-start.4 = (bf16[864,128]{1,0:T(8,128)(2,1)S(1)}, bf16[864,128]{1,0:T(8,128)(2,1)S(1)}, u32[]{:S(2)}, u32[]{:S(2)}) collective-permute-start(bf16[864,128]{1,0:T(8,128)(2,1)S(1)} %collective-permute-done.3.refs_16_), channel_id=1, source_target_pairs={{0,8},{1,9},{2,10},{3,11},{4,12},{5,13},{6,14},{7,15},{8,0},{9,1},... | collective-permute-start | bytes 663560 | tf_op jit(solution)/shard_map/ppermute | solution.py:804
  21.9 8.6 %collective-permute-start.1 = (bf16[864,128]{1,0:T(8,128)(2,1)S(1)}, bf16[864,128]{1,0:T(8,128)(2,1)S(1)}, u32[]{:S(2)}, u32[]{:S(2)}) collective-permute-start(bf16[864,128]{1,0:T(8,128)(2,1)S(1)} %collective-permute-done.refs_2_), channel_id=1, source_target_pairs={{0,1},{1,0},{2,6},{3,7},{4,5},{5,4},{6,2},{7,3},{8,9},{9,8},{10,14... | collective-permute-start | bytes 663560 | tf_op jit(solution)/shard_map/ppermute | solution.py:804
  30.5 7.2 %collective-permute-start.6 = (bf16[864,128]{1,0:T(8,128)(2,1)S(1)}, bf16[864,128]{1,0:T(8,128)(2,1)}, u32[]{:S(2)}, u32[]{:S(2)}) collective-permute-start(bf16[864,128]{1,0:T(8,128)(2,1)S(1)} %collective-permute-done.4.refs_24_), channel_id=1, source_target_pairs={{0,1},{1,0},{2,6},{3,7},{4,5},{5,4},{6,2},{7,3},{8,9},{9,8},{10,14... | collective-permute-start | bytes 663560 | tf_op jit(solution)/shard_map/ppermute | solution.py:804
  31.1 8.8 %collective-permute-start.25 = (bf16[864,128]{1,0:T(8,128)(2,1)S(1)}, bf16[864,128]{1,0:T(8,128)(2,1)}, u32[]{:S(2)}, u32[]{:S(2)}) collective-permute-start(bf16[864,128]{1,0:T(8,128)(2,1)S(1)} %collective-permute-done.5.refs_18_), channel_id=1, source_target_pairs={{0,1},{1,0},{2,6},{3,7},{4,5},{5,4},{6,2},{7,3},{8,9},{9,8},{10,14... | collective-permute-start | bytes 663560 | tf_op jit(solution)/shard_map/ppermute | solution.py:804
  33.2 7.4 %collective-permute-start.2 = (bf16[864,128]{1,0:T(8,128)(2,1)S(1)}, bf16[864,128]{1,0:T(8,128)(2,1)}, u32[]{:S(2)}, u32[]{:S(2)}) collective-permute-start(bf16[864,128]{1,0:T(8,128)(2,1)S(1)} %collective-permute-done.1.refs_6_), channel_id=1, source_target_pairs={{0,8},{1,9},{2,10},{3,11},{4,12},{5,13},{6,14},{7,15},{8,0},{9,1},... | collective-permute-start | bytes 663560 | tf_op jit(solution)/shard_map/ppermute | solution.py:804
  40.6 7.4 %collective-permute-start.31 = (bf16[864,128]{1,0:T(8,128)(2,1)}, bf16[864,128]{1,0:T(8,128)(2,1)S(1)}, u32[]{:S(2)}, u32[]{:S(2)}) collective-permute-start(bf16[864,128]{1,0:T(8,128)(2,1)} %collective-permute-done.25.refs_22_), channel_id=1, source_target_pairs={{0,8},{1,9},{2,10},{3,11},{4,12},{5,13},{6,14},{7,15},{8,0},{9,1},... | collective-permute-start | bytes 663560 | tf_op jit(solution)/shard_map/ppermute | solution.py:804
  43.0 7.4 %collective-permute-start.26 = (bf16[864,128]{1,0:T(8,128)(2,1)}, bf16[864,128]{1,0:T(8,128)(2,1)S(1)}, u32[]{:S(2)}, u32[]{:S(2)}) collective-permute-start(bf16[864,128]{1,0:T(8,128)(2,1)} %collective-permute-done.25.refs_22_), channel_id=1, source_target_pairs={{0,2},{1,3},{2,0},{3,1},{4,6},{5,7},{6,4},{7,5},{8,10},{9,11},{10,... | collective-permute-start | bytes 663560 | tf_op jit(solution)/shard_map/ppermute | solution.py:804
  50.0 10.9 %collective-permute-start.33 = (bf16[2,128,512]{2,1,0:T(8,128)(2,1)S(1)}, bf16[2,128,512]{2,1,0:T(8,128)(2,1)S(1)}, u32[]{:S(2)}, u32[]{:S(2)}) collective-permute-start(bf16[2,128,512]{2,1,0:T(8,128)(2,1)S(1)} %get-tuple-element.90), channel_id=1, source_target_pairs={{0,1},{1,0},{2,3},{3,2},{4,5},{5,4},{6,7},{7,6},{8,9},{9,8},{10,11... | collective-permute-start | bytes 786440 | tf_op jit(solution)/shard_map/ppermute | solution.py:1060
  79.5 13.1 %collective-permute-start.35 = (bf16[3456,128]{1,0:T(8,128)(2,1)S(1)}, bf16[3456,128]{1,0:T(8,128)(2,1)S(1)}, u32[]{:S(2)}, u32[]{:S(2)}) collective-permute-start(bf16[3456,128]{1,0:T(8,128)(2,1)S(1)} %shard_map.183), channel_id=1, source_target_pairs={{0,1},{1,0},{2,6},{3,7},{4,5},{5,4},{6,2},{7,3},{8,9},{9,8},{10,14... | collective-permute-start | bytes 2654216 | tf_op jit(solution)/shard_map/ppermute | solution.py:804
  93.4 11.7 %collective-permute-start.38 = (bf16[1728,128]{1,0:T(8,128)(2,1)S(1)}, bf16[1728,128]{1,0:T(8,128)(2,1)S(1)}, u32[]{:S(2)}, u32[]{:S(2)}) collective-permute-start(bf16[1728,128]{1,0:T(8,128)(2,1)S(1)} %shard_map.185), channel_id=1, source_target_pairs={{0,4},{1,5},{2,3},{3,2},{4,0},{5,1},{6,7},{7,6},{8,12},{9,13},{10,... | collective-permute-start | bytes 1327112 | tf_op jit(solution)/shard_map/ppermute | solution.py:804
  95.4 11.3 %collective-permute-start.39 = (bf16[1792,128]{1,0:T(8,128)(2,1)S(1)}, bf16[1792,128]{1,0:T(8,128)(2,1)S(1)}, u32[]{:S(2)}, u32[]{:S(2)}) collective-permute-start(bf16[1792,128]{1,0:T(8,128)(2,1)S(1)} %shard_map.186), channel_id=1, source_target_pairs={{0,1},{1,0},{2,6},{3,7},{4,5},{5,4},{6,2},{7,3},{8,9},{9,8},{10,14... | collective-permute-start | bytes 1376264 | tf_op jit(solution)/shard_map/ppermute | solution.py:804
  97.2 14.1 %collective-permute-start.41 = (bf16[1728,128]{1,0:T(8,128)(2,1)S(1)}, bf16[1728,128]{1,0:T(8,128)(2,1)S(1)}, u32[]{:S(2)}, u32[]{:S(2)}) collective-permute-start(bf16[1728,128]{1,0:T(8,128)(2,1)S(1)} %shard_map.187), channel_id=1, source_target_pairs={{0,1},{1,0},{2,6},{3,7},{4,5},{5,4},{6,2},{7,3},{8,9},{9,8},{10,14... | collective-permute-start | bytes 1327112 | tf_op jit(solution)/shard_map/ppermute | solution.py:804
  120.0 13.3 %collective-permute-start.47 = (bf16[448,128]{1,0:T(8,128)(2,1)S(1)}, bf16[448,128]{1,0:T(8,128)(2,1)S(1)}, u32[]{:S(2)}, u32[]{:S(2)}) collective-permute-start(bf16[448,128]{1,0:T(8,128)(2,1)S(1)} %shard_map.197), channel_id=1, source_target_pairs={{0,16},{1,17},{2,18},{3,19},{4,20},{5,21},{6,22},{7,23},{8,24},{9,... | collective-permute-start | bytes 344072 | tf_op jit(solution)/shard_map/ppermute | solution.py:804
  123.7 9.7 %collective-permute-start.48 = (bf16[432,128]{1,0:T(8,128)(2,1)S(1)}, bf16[432,128]{1,0:T(8,128)(2,1)S(1)}, u32[]{:S(2)}, u32[]{:S(2)}) collective-permute-start(bf16[432,128]{1,0:T(8,128)(2,1)S(1)} %shard_map.198), channel_id=1, source_target_pairs={{0,16},{1,17},{2,18},{3,19},{4,20},{5,21},{6,22},{7,23},{8,24},{9,... | collective-permute-start | bytes 331784 | tf_op jit(solution)/shard_map/ppermute | solution.py:804
  126.3 12.1 %collective-permute-start.46 = (bf16[2,176,512]{2,1,0:T(8,128)(2,1)S(1)}, bf16[2,176,512]{2,1,0:T(8,128)(2,1)S(1)}, u32[]{:S(2)}, u32[]{:S(2)}) collective-permute-start(bf16[2,176,512]{2,1,0:T(8,128)(2,1)S(1)} %get-tuple-element.135), channel_id=1, source_target_pairs={{0,1},{1,0},{2,3},{3,2},{4,5},{5,4},{6,7},{7,6},{8,9},{9,8},{10,11... | collective-permute-start | bytes 1081352 | tf_op jit(solution)/shard_map/ppermute | solution.py:1060
  134.3 12.7 %all-to-all-start = ((f32[32,8,128]{2,1,0:T(8,128)}), f32[32,8,128]{2,1,0:T(8,128)S(1)}, u32[]{:S(2)}, u32[]{:S(2)}) async-start(f32[32,8,128]{2,1,0:T(8,128)} %get-tuple-element.139), calls=%async_computation | async-start | bytes 262144 | tf_op jit(solution)/shard_map/all_to_all | solution.py:1107
  (43 other events, 377.3 us)

commit v5 on v4

--- a/solution.py
+++ b/solution.py
@@ -453,7 +453,14 @@
         )
 
 
-def slot_of(index, by_hand):
+FIRST, SECOND, ALONG_Z = 0, 1, 2
+HOP_BITS = ((1, 4), (4, 1), (8, 8))
+HIGH_ORDER = (FIRST, ALONG_Z, SECOND)
+ONE_ORDER = (FIRST, SECOND, ALONG_Z)
+TWO_ORDER = (FIRST, SECOND, ALONG_Z)
+
+
+def slot_of(index, by_hand, order):
     if not by_hand:
         return index
     me = place()
@@ -463,13 +470,14 @@
     along_y, along_x, along_z = rel & 1, (rel >> 2) & 1, rel >> 3
     first = jnp.where(odd == 0, along_y, along_x)
     second = jnp.where(odd == 0, along_x, along_y)
-    slot = (1 - first) * 4 + (1 - second) * 2 + (1 - along_z)
+    bits = (first, second, along_z)
+    slot = (1 - bits[order[0]]) * 4 + (1 - bits[order[1]]) * 2 + (1 - bits[order[2]])
     return slot + jnp.where(other == 1, 0, 8)
 
 
 def put_blocks(by_hand, far_lines, near_lines, block_of):
     def body(index, carry):
-        slot = slot_of(index, by_hand)
+        slot = slot_of(index, by_hand, HIGH_ORDER)
         value = block_of(index)
 
         @pl.when(slot < 8)
@@ -706,22 +714,23 @@
             ]
 
     def store(index, value):
-        slot = slot_of(index, by_hand)
+        slot = slot_of(index, by_hand, ONE_ORDER)
+        late = slot_of(index, by_hand, TWO_ORDER)
         tail = tails[pl.ds(pl.multiple_of(index * TAIL, TAIL), TAIL), :].astype(BF)
 
-        def put(first, second, at):
+        def put(first, second, at, late_at):
             row = pl.multiple_of(at * PARTS[0], 16)
             first[pl.ds(row, PART), :] = value[:PART]
             first[pl.ds(row + PART, TAIL), :] = tail
-            second[pl.ds(pl.multiple_of(at * PART, 16), PART), :] = value[PART:]
+            second[pl.ds(pl.multiple_of(late_at * PART, 16), PART), :] = value[PART:]
 
         @pl.when(slot < 8)
         def _():
-            put(far_first, far_second, slot)
+            put(far_first, far_second, slot, late)
 
         @pl.when(slot >= 8)
         def _():
-            put(near_first, near_second, slot - 8)
+            put(near_first, near_second, slot - 8, late - 8)
 
     ranges = (
         (EMBED_AT, JOINT_AT, lambda low, high: grads[low:high, :].astype(BF)),
@@ -875,19 +884,17 @@
 
 
 class Reduction:
-    HOPS = ((2, 2), (1, 4), (4, 1), (8, 8))
-
-    def __init__(self, grid, far_lines, near_lines, half):
+    def __init__(self, grid, far_lines, near_lines, order):
         self.grid = grid
         self.near = near_lines
-        self.half = half
+        self.hops = ((2, 2), *(HOP_BITS[hop] for hop in order))
         self.rows = far_lines.shape[0] // 8
         self.head = far_lines
         self.came = []
 
     def hop(self, *behind):
         step = len(self.came)
-        self.came.append(self.grid.send(self.head, *self.HOPS[step]))
+        self.came.append(self.grid.send(self.head, *self.hops[step]))
         left = 8 >> (step + 1)
         count = max(left, 1) if step < 3 else 1
         begin = 8 - 2 * left if step < 3 else 7
@@ -1075,7 +1082,7 @@
         own_out, far_out, hat, scale, back_out, acc_back, head_lines, far_high, near_high, expand_b,
     ) = middle_call(by_hand, bucket, middle, cotangent, far_cotangent, vectors, lines)
     if by_hand:
-        high = Reduction(grid, far_high, near_high, 1)
+        high = Reduction(grid, far_high, near_high, HIGH_ORDER)
     back_middle, back_mixed, out_lines, rows_b = branch_call(
         hat, scale, back_out, acc_back, mixed, output_w, vectors
     )
@@ -1087,9 +1094,9 @@
     )
     if by_hand:
         mark = high.hop(far_one)
-        one = Reduction(grid, after(far_one, mark), near_one, 0)
-        two = Reduction(grid, after(far_two, mark), near_two, 0)
-        for stream in (one, two, high, one, high, two, one, two, one, two):
+        one = Reduction(grid, after(far_one, mark), near_one, ONE_ORDER)
+        two = Reduction(grid, after(far_two, mark), near_two, TWO_ORDER)
+        for stream in (one, two, one, high, two, one, high, two, one, two):
             mark = stream.hop(mark)
             if stream is two:
                 pack_mark = mark

time: 149 us -> 146 us (0.980)
  no operation moved by 1% of the time
where the time goes in v5:
time: 146 us
  waiting for transfers between devices  48 us (33%)
  starting transfers between devices  47.3 us (32%)
  Pallas kernels  44.8 us (31%)
  local copies, waits for them, and re-layouts  2.81 us (2%)
  other arithmetic  2.09 us (1%)
    ppermute x45, starting transfers between devices, send(): return lax.ppermute(value, self.axes, pairs)  39.7 us
    ppermute x45, waiting for transfers between devices, send(): return lax.ppermute(value, self.axes, pairs)  37.9 us
    pallas_call x1, Pallas kernels, middle_call(): pl.pallas_call(lambda *refs: middle_kernel(by_hand, *refs), grid=(TILES,)...  14.6 us
    pallas_call x1, Pallas kernels, back_call(): pl.pallas_call(lambda *refs: back_kernel(by_hand, *refs), in_specs=[VMEM]...  11.4 us
    pallas_call x1, Pallas kernels, forward_call(): pl.pallas_call(forward_kernel, in_specs=[SMEM] + [VMEM] * (len(operands)...  7.71 us
    all_to_all x1, waiting for transfers between devices, local(): notes = lax.all_to_all(notes, grid.axes, 0, 0, tiled=True)  7.48 us
    all_to_all x1, starting transfers between devices, local(): notes = lax.all_to_all(notes, grid.axes, 0, 0, tiled=True)  4.05 us
    ppermute x4, starting transfers between devices, trade(): return lax.ppermute(value, 'blk', [(0, 1), (1, 0)])  3.63 us
  transfers between devices with their start and end apart: 50, of which 20 were waited for; matrix products, arithmetic and copies ran while one was open for 1% of the time, Pallas kernels for 19%

profile of v5, /device:TPU:0, one launch (start us, length us, event | category | flops | bytes accessed | tf_op | source)
XLA Modules:
  0.0 146.1 jit_solution(4993156856534707060)
XLA Ops:
  1.7 3.1 %collective-permute-start.14 = (bf16[864,128]{1,0:T(8,128)(2,1)S(1)}, bf16[864,128]{1,0:T(8,128)(2,1)S(1)}, u32[]{:S(2)}, u32[]{:S(2)}) collective-permute-start(bf16[864,128]{1,0:T(8,128)(2,1)S(1)} %bitcast_convert_fusion.refs_0_), channel_id=1, source_target_pairs={{0,8},{1,9},{2,10},{3,11},{4,12},{5,13},{6,14},{7,15},{8,0},{9,1},... | collective-permute-start | bytes 663560 | tf_op jit(solution)/shard_map/ppermute | solution.py:813
  6.3 2.6 %collective-permute-start.3 = (bf16[864,128]{1,0:T(8,128)(2,1)S(1)}, bf16[864,128]{1,0:T(8,128)(2,1)S(1)}, u32[]{:S(2)}, u32[]{:S(2)}) collective-permute-start(bf16[864,128]{1,0:T(8,128)(2,1)S(1)} %bitcast_convert_fusion.refs_0_), channel_id=1, source_target_pairs={{0,16},{1,17},{2,18},{3,19},{4,20},{5,21},{6,22},{7,23},{8,24},{9,... | collective-permute-start | bytes 663560 | tf_op jit(solution)/shard_map/ppermute | solution.py:813
  10.4 4.5 %collective-permute-start.18 = (bf16[864,128]{1,0:T(8,128)(2,1)S(1)}, bf16[864,128]{1,0:T(8,128)(2,1)S(1)}, u32[]{:S(2)}, u32[]{:S(2)}) collective-permute-start(bf16[864,128]{1,0:T(8,128)(2,1)S(1)} %collective-permute-done.14.refs_8_), channel_id=1, source_target_pairs={{0,1},{1,0},{2,6},{3,7},{4,5},{5,4},{6,2},{7,3},{8,9},{9,8},{10,14... | collective-permute-start | bytes 663560 | tf_op jit(solution)/shard_map/ppermute | solution.py:813
  16.4 3.4 %collective-permute-done.3.refs_16_ = bf16[864,128]{1,0:T(8,128)(2,1)S(1)} collective-permute-done((bf16[864,128]{1,0:T(8,128)(2,1)S(1)}, bf16[864,128]{1,0:T(8,128)(2,1)S(1)}, u32[]{:S(2)}, u32[]{:S(2)}) %collective-permute-start.3) | collective-permute-done | bytes 221216 | tf_op jit(solution)/shard_map/ppermute | solution.py:813
  23.4 4.0 %collective-permute-done.23.refs_20_ = bf16[864,128]{1,0:T(8,128)(2,1)S(1)} collective-permute-done((bf16[864,128]{1,0:T(8,128)(2,1)S(1)}, bf16[864,128]{1,0:T(8,128)(2,1)S(1)}, u32[]{:S(2)}, u32[]{:S(2)}) %collective-permute-start.23) | collective-permute-done | bytes 221216 | tf_op jit(solution)/shard_map/ppermute | solution.py:813
  37.7 2.2 %collective-permute-done.25.refs_22_ = bf16[864,128]{1,0:T(8,128)(2,1)} collective-permute-done((bf16[864,128]{1,0:T(8,128)(2,1)S(1)}, bf16[864,128]{1,0:T(8,128)(2,1)}, u32[]{:S(2)}, u32[]{:S(2)}) %collective-permute-start.25) | collective-permute-done | bytes 221216 | tf_op jit(solution)/shard_map/ppermute | solution.py:813
  46.1 1.9 %collective-permute-done.31.refs_30_ = bf16[864,128]{1,0:T(8,128)(2,1)S(1)} collective-permute-done((bf16[864,128]{1,0:T(8,128)(2,1)}, bf16[864,128]{1,0:T(8,128)(2,1)S(1)}, u32[]{:S(2)}, u32[]{:S(2)}) %collective-permute-start.31) | collective-permute-done | bytes 221216 | tf_op jit(solution)/shard_map/ppermute | solution.py:813
  50.5 2.6 %shard_map.179.lines.refs_5_ = bf16[27648,128]{1,0:T(8,128)(2,1)S(1)} custom-call(bf16[864,128]{1,0:T(8,128)(2,1)S(1)} %bitcast_convert_fusion.refs_0_, bf16[864,128]{1,0:T(8,128)(2,1)S(1)} %collective-permute-done.9.refs_1_, bf16[864,128]{1,0:T(8,128)(2,1)S(1)} %collective-permute-done.refs_2_, bf16[864,128]{1,0:T(8,128)(2,1)S(1)} %collective-permute-done.10.refs_3_, ...), custom_call_target="tpu_custom_call" | custom-call | bytes 1048576 | tf_op jit(solution)/shard_map/pallas_call | solution.py:92
  53.1 7.7 %shard_map.180 = (bf16[32,256,256]{2,1,0:T(8,128)(2,1)S(1)}, f32[32,256]{1,0:T(8,128)S(1)}, bf16[512,1536]{1,0:T(8,128)(2,1)S(1)}, bf16[512,512]{1,0:T(8,128)(2,...) custom-call(s32[4]{0:T(128)S(1)} %copy-done.16, ...), custom_call_target="tpu_custom_call" | custom-call | flops 6000000000 | bytes 16777216 | tf_op jit(solution)/shard_map/pallas_call | solution.py:346
  60.9 14.6 %shard_map.181 = (f32[2,128,512]{2,1,0:T(8,128)S(1)}, bf16[2,128,512]{2,1,0:T(8,128)(2,1)S(1)}, f32[512,512]{1,0:T(8,128)S(1)}, f32[512,128]{1,0:T(8,128)S(1)}, ...) custom-call(s32[4]{0:T(128)S(1)} %copy-done.16, ...), custom_call_target="tpu_custom_call" | custom-call | flops 8000000000 | bytes 16777216 | tf_op jit(solution)/shard_map/pallas_call | solution.py:509
  77.2 2.0 %collective-permute-done.34.refs_1_ = bf16[6912,128]{1,0:T(8,128)(2,1)S(1)} collective-permute-done((bf16[6912,128]{1,0:T(8,128)(2,1)S(1)}, bf16[6912,128]{1,0:T(8,128)(2,1)S(1)}, u32[]{:S(2)}, u32[]{:S(2)}) %collective-permute-start.34) | collective-permute-done | bytes 1769504 | tf_op jit(solution)/shard_map/ppermute | solution.py:813
  79.5 1.7 %collective-permute-start.35 = (bf16[3456,128]{1,0:T(8,128)(2,1)S(1)}, bf16[3456,128]{1,0:T(8,128)(2,1)S(1)}, u32[]{:S(2)}, u32[]{:S(2)}) collective-permute-start(bf16[3456,128]{1,0:T(8,128)(2,1)S(1)} %shard_map.183), channel_id=1, source_target_pairs={{0,1},{1,0},{2,6},{3,7},{4,5},{5,4},{6,2},{7,3},{8,9},{9,8},{10,14... | collective-permute-start | bytes 2654216 | tf_op jit(solution)/shard_map/ppermute | solution.py:813
  81.2 11.4 %shard_map.184 = (bf16[3584,128]{1,0:T(8,128)(2,1)S(1)}, bf16[3584,128]{1,0:T(8,128)(2,1)S(1)}, bf16[3456,128]{1,0:T(8,128)(2,1)S(1)}, bf16[3456,128]{1,0:T(8,12...) custom-call(bf16[32,256,256]{2,1,0:T(8,128)(2,1)S(1)} %get-tuple-element.92.refs_0_, ...), custom_call_target="tpu_custom_call" | custom-call | flops 4000000000 | bytes 8388608 | tf_op jit(solution)/shard_map/pallas_call | solution.py:775
  93.4 2.0 %collective-permute-done.36.refs_1_ = bf16[3584,128]{1,0:T(8,128)(2,1)S(1)} collective-permute-done((bf16[3584,128]{1,0:T(8,128)(2,1)S(1)}, bf16[3584,128]{1,0:T(8,128)(2,1)S(1)}, u32[]{:S(2)}, u32[]{:S(2)}) %collective-permute-start.36) | collective-permute-done | bytes 917536 | tf_op jit(solution)/shard_map/ppermute | solution.py:813
  99.2 4.8 %collective-permute-done.38.refs_2_ = bf16[1792,128]{1,0:T(8,128)(2,1)S(1)} collective-permute-done((bf16[1792,128]{1,0:T(8,128)(2,1)S(1)}, bf16[1792,128]{1,0:T(8,128)(2,1)S(1)}, u32[]{:S(2)}, u32[]{:S(2)}) %collective-permute-start.38) | collective-permute-done | bytes 458784 | tf_op jit(solution)/shard_map/ppermute | solution.py:813
  105.6 3.3 %collective-permute-done.39.refs_3_ = bf16[1728,128]{1,0:T(8,128)(2,1)S(1)} collective-permute-done((bf16[1728,128]{1,0:T(8,128)(2,1)S(1)}, bf16[1728,128]{1,0:T(8,128)(2,1)S(1)}, u32[]{:S(2)}, u32[]{:S(2)}) %collective-permute-start.39) | collective-permute-done | bytes 442400 | tf_op jit(solution)/shard_map/ppermute | solution.py:813
  111.3 1.7 %collective-permute-start.43 = (bf16[864,128]{1,0:T(8,128)(2,1)S(1)}, bf16[864,128]{1,0:T(8,128)(2,1)S(1)}, u32[]{:S(2)}, u32[]{:S(2)}) collective-permute-start(bf16[864,128]{1,0:T(8,128)(2,1)S(1)} %shard_map.190), channel_id=1, source_target_pairs={{0,4},{1,5},{2,3},{3,2},{4,0},{5,1},{6,7},{7,6},{8,12},{9,13},{10,... | collective-permute-start | bytes 663560 | tf_op jit(solution)/shard_map/ppermute | solution.py:813
  115.1 2.2 %collective-permute-done.43.refs_3_ = bf16[864,128]{1,0:T(8,128)(2,1)S(1)} collective-permute-done((bf16[864,128]{1,0:T(8,128)(2,1)S(1)}, bf16[864,128]{1,0:T(8,128)(2,1)S(1)}, u32[]{:S(2)}, u32[]{:S(2)}) %collective-permute-start.43) | collective-permute-done | bytes 221216 | tf_op jit(solution)/shard_map/ppermute | solution.py:813
  119.0 2.1 %collective-permute-start.47 = (bf16[448,128]{1,0:T(8,128)(2,1)S(1)}, bf16[448,128]{1,0:T(8,128)(2,1)S(1)}, u32[]{:S(2)}, u32[]{:S(2)}) collective-permute-start(bf16[448,128]{1,0:T(8,128)(2,1)S(1)} %shard_map.197), channel_id=1, source_target_pairs={{0,16},{1,17},{2,18},{3,19},{4,20},{5,21},{6,22},{7,23},{8,24},{9,... | collective-permute-start | bytes 344072 | tf_op jit(solution)/shard_map/ppermute | solution.py:813
  121.1 1.9 %collective-permute-done.45.refs_4_ = bf16[432,128]{1,0:T(8,128)(2,1)S(1)} collective-permute-done((bf16[432,128]{1,0:T(8,128)(2,1)S(1)}, bf16[432,128]{1,0:T(8,128)(2,1)S(1)}, u32[]{:S(2)}, u32[]{:S(2)}) %collective-permute-start.45) | collective-permute-done | bytes 110624 | tf_op jit(solution)/shard_map/ppermute | solution.py:813
  123.3 1.9 %collective-permute-start.48 = (bf16[432,128]{1,0:T(8,128)(2,1)S(1)}, bf16[432,128]{1,0:T(8,128)(2,1)S(1)}, u32[]{:S(2)}, u32[]{:S(2)}) collective-permute-start(bf16[432,128]{1,0:T(8,128)(2,1)S(1)} %shard_map.198), channel_id=1, source_target_pairs={{0,16},{1,17},{2,18},{3,19},{4,20},{5,21},{6,22},{7,23},{8,24},{9,... | collective-permute-start | bytes 331784 | tf_op jit(solution)/shard_map/ppermute | solution.py:813
  126.3 4.5 %collective-permute-done.48.two_far = bf16[432,128]{1,0:T(8,128)(2,1)S(1)} collective-permute-done((bf16[432,128]{1,0:T(8,128)(2,1)S(1)}, bf16[432,128]{1,0:T(8,128)(2,1)S(1)}, u32[]{:S(2)}, u32[]{:S(2)}) %collective-permute-start.48) | collective-permute-done | bytes 110624 | tf_op jit(solution)/shard_map/ppermute | solution.py:813
  131.8 4.0 %all-to-all-start = ((f32[32,8,128]{2,1,0:T(8,128)}), f32[32,8,128]{2,1,0:T(8,128)S(1)}, u32[]{:S(2)}, u32[]{:S(2)}) async-start(f32[32,8,128]{2,1,0:T(8,128)} %get-tuple-element.139), calls=%async_computation | async-start | bytes 262144 | tf_op jit(solution)/shard_map/all_to_all | solution.py:1114
  137.0 7.5 %all-to-all-done.notes = f32[32,8,128]{2,1,0:T(8,128)S(1)} async-done(((f32[32,8,128]{2,1,0:T(8,128)}), f32[32,8,128]{2,1,0:T(8,128)S(1)}, u32[]{:S(2)}, u32[]{:S(2)}) %all-to-all-start) | async-done | bytes 131104 | tf_op jit(solution)/shard_map/all_to_all | solution.py:1114
  (139 shorter events, 47.2 us)
Async XLA Ops:
  1.7 8.7 %collective-permute-start.14 = (bf16[864,128]{1,0:T(8,128)(2,1)S(1)}, bf16[864,128]{1,0:T(8,128)(2,1)S(1)}, u32[]{:S(2)}, u32[]{:S(2)}) collective-permute-start(bf16[864,128]{1,0:T(8,128)(2,1)S(1)} %bitcast_convert_fusion.refs_0_), channel_id=1, source_target_pairs={{0,8},{1,9},{2,10},{3,11},{4,12},{5,13},{6,14},{7,15},{8,0},{9,1},... | collective-permute-start | bytes 663560 | tf_op jit(solution)/shard_map/ppermute | solution.py:813
  4.8 10.1 %collective-permute-start.11 = (bf16[864,128]{1,0:T(8,128)(2,1)S(1)}, bf16[864,128]{1,0:T(8,128)(2,1)S(1)}, u32[]{:S(2)}, u32[]{:S(2)}) collective-permute-start(bf16[864,128]{1,0:T(8,128)(2,1)S(1)} %bitcast_convert_fusion.refs_0_), channel_id=1, source_target_pairs={{0,1},{1,0},{2,6},{3,7},{4,5},{5,4},{6,2},{7,3},{8,9},{9,8},{10,14... | collective-permute-start | bytes 663560 | tf_op jit(solution)/shard_map/ppermute | solution.py:813
  6.3 10.0 %collective-permute-start.9 = (bf16[864,128]{1,0:T(8,128)(2,1)S(1)}, bf16[864,128]{1,0:T(8,128)(2,1)S(1)}, u32[]{:S(2)}, u32[]{:S(2)}) collective-permute-start(bf16[864,128]{1,0:T(8,128)(2,1)S(1)} %bitcast_convert_fusion.refs_0_), channel_id=1, source_target_pairs={{0,2},{1,3},{2,0},{3,1},{4,6},{5,7},{6,4},{7,5},{8,10},{9,11},{10,... | collective-permute-start | bytes 663560 | tf_op jit(solution)/shard_map/ppermute | solution.py:813
  6.3 13.5 %collective-permute-start.3 = (bf16[864,128]{1,0:T(8,128)(2,1)S(1)}, bf16[864,128]{1,0:T(8,128)(2,1)S(1)}, u32[]{:S(2)}, u32[]{:S(2)}) collective-permute-start(bf16[864,128]{1,0:T(8,128)(2,1)S(1)} %bitcast_convert_fusion.refs_0_), channel_id=1, source_target_pairs={{0,16},{1,17},{2,18},{3,19},{4,20},{5,21},{6,22},{7,23},{8,24},{9,... | collective-permute-start | bytes 663560 | tf_op jit(solution)/shard_map/ppermute | solution.py:813
  8.9 10.9 %collective-permute-start = (bf16[864,128]{1,0:T(8,128)(2,1)S(1)}, bf16[864,128]{1,0:T(8,128)(2,1)S(1)}, u32[]{:S(2)}, u32[]{:S(2)}) collective-permute-start(bf16[864,128]{1,0:T(8,128)(2,1)S(1)} %bitcast_convert_fusion.refs_0_), channel_id=1, source_target_pairs={{0,4},{1,5},{2,3},{3,2},{4,0},{5,1},{6,7},{7,6},{8,12},{9,13},{10,... | collective-permute-start | bytes 663560 | tf_op jit(solution)/shard_map/ppermute | solution.py:813
  10.4 10.0 %collective-permute-start.18 = (bf16[864,128]{1,0:T(8,128)(2,1)S(1)}, bf16[864,128]{1,0:T(8,128)(2,1)S(1)}, u32[]{:S(2)}, u32[]{:S(2)}) collective-permute-start(bf16[864,128]{1,0:T(8,128)(2,1)S(1)} %collective-permute-done.14.refs_8_), channel_id=1, source_target_pairs={{0,1},{1,0},{2,6},{3,7},{4,5},{5,4},{6,2},{7,3},{8,9},{9,8},{10,14... | collective-permute-start | bytes 663560 | tf_op jit(solution)/shard_map/ppermute | solution.py:813
  19.8 7.6 %collective-permute-start.23 = (bf16[864,128]{1,0:T(8,128)(2,1)S(1)}, bf16[864,128]{1,0:T(8,128)(2,1)S(1)}, u32[]{:S(2)}, u32[]{:S(2)}) collective-permute-start(bf16[864,128]{1,0:T(8,128)(2,1)S(1)} %collective-permute-done.3.refs_16_), channel_id=1, source_target_pairs={{0,1},{1,0},{2,6},{3,7},{4,5},{5,4},{6,2},{7,3},{8,9},{9,8},{10,14... | collective-permute-start | bytes 663560 | tf_op jit(solution)/shard_map/ppermute | solution.py:813
  20.4 8.3 %collective-permute-start.5 = (bf16[864,128]{1,0:T(8,128)(2,1)S(1)}, bf16[864,128]{1,0:T(8,128)(2,1)S(1)}, u32[]{:S(2)}, u32[]{:S(2)}) collective-permute-start(bf16[864,128]{1,0:T(8,128)(2,1)S(1)} %collective-permute-done.3.refs_16_), channel_id=1, source_target_pairs={{0,4},{1,5},{2,3},{3,2},{4,0},{5,1},{6,7},{7,6},{8,12},{9,13},{10,... | collective-permute-start | bytes 663560 | tf_op jit(solution)/shard_map/ppermute | solution.py:813
  21.8 7.3 %collective-permute-start.4 = (bf16[864,128]{1,0:T(8,128)(2,1)S(1)}, bf16[864,128]{1,0:T(8,128)(2,1)S(1)}, u32[]{:S(2)}, u32[]{:S(2)}) collective-permute-start(bf16[864,128]{1,0:T(8,128)(2,1)S(1)} %collective-permute-done.3.refs_16_), channel_id=1, source_target_pairs={{0,8},{1,9},{2,10},{3,11},{4,12},{5,13},{6,14},{7,15},{8,0},{9,1},... | collective-permute-start | bytes 663560 | tf_op jit(solution)/shard_map/ppermute | solution.py:813
  21.9 8.6 %collective-permute-start.1 = (bf16[864,128]{1,0:T(8,128)(2,1)S(1)}, bf16[864,128]{1,0:T(8,128)(2,1)S(1)}, u32[]{:S(2)}, u32[]{:S(2)}) collective-permute-start(bf16[864,128]{1,0:T(8,128)(2,1)S(1)} %collective-permute-done.refs_2_), channel_id=1, source_target_pairs={{0,1},{1,0},{2,6},{3,7},{4,5},{5,4},{6,2},{7,3},{8,9},{9,8},{10,14... | collective-permute-start | bytes 663560 | tf_op jit(solution)/shard_map/ppermute | solution.py:813
  31.1 8.8 %collective-permute-start.25 = (bf16[864,128]{1,0:T(8,128)(2,1)S(1)}, bf16[864,128]{1,0:T(8,128)(2,1)}, u32[]{:S(2)}, u32[]{:S(2)}) collective-permute-start(bf16[864,128]{1,0:T(8,128)(2,1)S(1)} %collective-permute-done.5.refs_18_), channel_id=1, source_target_pairs={{0,1},{1,0},{2,6},{3,7},{4,5},{5,4},{6,2},{7,3},{8,9},{9,8},{10,14... | collective-permute-start | bytes 663560 | tf_op jit(solution)/shard_map/ppermute | solution.py:813
  33.2 7.4 %collective-permute-start.2 = (bf16[864,128]{1,0:T(8,128)(2,1)S(1)}, bf16[864,128]{1,0:T(8,128)(2,1)}, u32[]{:S(2)}, u32[]{:S(2)}) collective-permute-start(bf16[864,128]{1,0:T(8,128)(2,1)S(1)} %collective-permute-done.1.refs_6_), channel_id=1, source_target_pairs={{0,8},{1,9},{2,10},{3,11},{4,12},{5,13},{6,14},{7,15},{8,0},{9,1},... | collective-permute-start | bytes 663560 | tf_op jit(solution)/shard_map/ppermute | solution.py:813
  40.6 7.4 %collective-permute-start.31 = (bf16[864,128]{1,0:T(8,128)(2,1)}, bf16[864,128]{1,0:T(8,128)(2,1)S(1)}, u32[]{:S(2)}, u32[]{:S(2)}) collective-permute-start(bf16[864,128]{1,0:T(8,128)(2,1)} %collective-permute-done.25.refs_22_), channel_id=1, source_target_pairs={{0,8},{1,9},{2,10},{3,11},{4,12},{5,13},{6,14},{7,15},{8,0},{9,1},... | collective-permute-start | bytes 663560 | tf_op jit(solution)/shard_map/ppermute | solution.py:813
  43.0 7.4 %collective-permute-start.26 = (bf16[864,128]{1,0:T(8,128)(2,1)}, bf16[864,128]{1,0:T(8,128)(2,1)S(1)}, u32[]{:S(2)}, u32[]{:S(2)}) collective-permute-start(bf16[864,128]{1,0:T(8,128)(2,1)} %collective-permute-done.25.refs_22_), channel_id=1, source_target_pairs={{0,2},{1,3},{2,0},{3,1},{4,6},{5,7},{6,4},{7,5},{8,10},{9,11},{10,... | collective-permute-start | bytes 663560 | tf_op jit(solution)/shard_map/ppermute | solution.py:813
  50.0 10.9 %collective-permute-start.33 = (bf16[2,128,512]{2,1,0:T(8,128)(2,1)S(1)}, bf16[2,128,512]{2,1,0:T(8,128)(2,1)S(1)}, u32[]{:S(2)}, u32[]{:S(2)}) collective-permute-start(bf16[2,128,512]{2,1,0:T(8,128)(2,1)S(1)} %get-tuple-element.90), channel_id=1, source_target_pairs={{0,1},{1,0},{2,3},{3,2},{4,5},{5,4},{6,7},{7,6},{8,9},{9,8},{10,11... | collective-permute-start | bytes 786440 | tf_op jit(solution)/shard_map/ppermute | solution.py:1067
  79.5 13.1 %collective-permute-start.35 = (bf16[3456,128]{1,0:T(8,128)(2,1)S(1)}, bf16[3456,128]{1,0:T(8,128)(2,1)S(1)}, u32[]{:S(2)}, u32[]{:S(2)}) collective-permute-start(bf16[3456,128]{1,0:T(8,128)(2,1)S(1)} %shard_map.183), channel_id=1, source_target_pairs={{0,1},{1,0},{2,6},{3,7},{4,5},{5,4},{6,2},{7,3},{8,9},{9,8},{10,14... | collective-permute-start | bytes 2654216 | tf_op jit(solution)/shard_map/ppermute | solution.py:813
  95.4 8.5 %collective-permute-start.38 = (bf16[1792,128]{1,0:T(8,128)(2,1)S(1)}, bf16[1792,128]{1,0:T(8,128)(2,1)S(1)}, u32[]{:S(2)}, u32[]{:S(2)}) collective-permute-start(bf16[1792,128]{1,0:T(8,128)(2,1)S(1)} %shard_map.186), channel_id=1, source_target_pairs={{0,1},{1,0},{2,6},{3,7},{4,5},{5,4},{6,2},{7,3},{8,9},{9,8},{10,14... | collective-permute-start | bytes 1376264 | tf_op jit(solution)/shard_map/ppermute | solution.py:813
  97.1 11.8 %collective-permute-start.39 = (bf16[1728,128]{1,0:T(8,128)(2,1)S(1)}, bf16[1728,128]{1,0:T(8,128)(2,1)S(1)}, u32[]{:S(2)}, u32[]{:S(2)}) collective-permute-start(bf16[1728,128]{1,0:T(8,128)(2,1)S(1)} %shard_map.185), channel_id=1, source_target_pairs={{0,8},{1,9},{2,10},{3,11},{4,12},{5,13},{6,14},{7,15},{8,0},{9,1},... | collective-permute-start | bytes 1327112 | tf_op jit(solution)/shard_map/ppermute | solution.py:813
  97.6 13.6 %collective-permute-start.40 = (bf16[1728,128]{1,0:T(8,128)(2,1)S(1)}, bf16[1728,128]{1,0:T(8,128)(2,1)S(1)}, u32[]{:S(2)}, u32[]{:S(2)}) collective-permute-start(bf16[1728,128]{1,0:T(8,128)(2,1)S(1)} %shard_map.187), channel_id=1, source_target_pairs={{0,1},{1,0},{2,6},{3,7},{4,5},{5,4},{6,2},{7,3},{8,9},{9,8},{10,14... | collective-permute-start | bytes 1327112 | tf_op jit(solution)/shard_map/ppermute | solution.py:813
  104.1 8.9 %collective-permute-start.41 = (bf16[896,128]{1,0:T(8,128)(2,1)S(1)}, bf16[896,128]{1,0:T(8,128)(2,1)S(1)}, u32[]{:S(2)}, u32[]{:S(2)}) collective-permute-start(bf16[896,128]{1,0:T(8,128)(2,1)S(1)} %shard_map.188), channel_id=1, source_target_pairs={{0,4},{1,5},{2,3},{3,2},{4,0},{5,1},{6,7},{7,6},{8,12},{9,13},{10,... | collective-permute-start | bytes 688136 | tf_op jit(solution)/shard_map/ppermute | solution.py:813
  119.0 11.9 %collective-permute-start.47 = (bf16[448,128]{1,0:T(8,128)(2,1)S(1)}, bf16[448,128]{1,0:T(8,128)(2,1)S(1)}, u32[]{:S(2)}, u32[]{:S(2)}) collective-permute-start(bf16[448,128]{1,0:T(8,128)(2,1)S(1)} %shard_map.197), channel_id=1, source_target_pairs={{0,16},{1,17},{2,18},{3,19},{4,20},{5,21},{6,22},{7,23},{8,24},{9,... | collective-permute-start | bytes 344072 | tf_op jit(solution)/shard_map/ppermute | solution.py:813
  123.3 7.6 %collective-permute-start.48 = (bf16[432,128]{1,0:T(8,128)(2,1)S(1)}, bf16[432,128]{1,0:T(8,128)(2,1)S(1)}, u32[]{:S(2)}, u32[]{:S(2)}) collective-permute-start(bf16[432,128]{1,0:T(8,128)(2,1)S(1)} %shard_map.198), channel_id=1, source_target_pairs={{0,16},{1,17},{2,18},{3,19},{4,20},{5,21},{6,22},{7,23},{8,24},{9,... | collective-permute-start | bytes 331784 | tf_op jit(solution)/shard_map/ppermute | solution.py:813
  125.2 10.7 %collective-permute-start.46 = (bf16[2,176,512]{2,1,0:T(8,128)(2,1)S(1)}, bf16[2,176,512]{2,1,0:T(8,128)(2,1)S(1)}, u32[]{:S(2)}, u32[]{:S(2)}) collective-permute-start(bf16[2,176,512]{2,1,0:T(8,128)(2,1)S(1)} %get-tuple-element.135), channel_id=1, source_target_pairs={{0,1},{1,0},{2,3},{3,2},{4,5},{5,4},{6,7},{7,6},{8,9},{9,8},{10,11... | collective-permute-start | bytes 1081352 | tf_op jit(solution)/shard_map/ppermute | solution.py:1067
  131.8 12.7 %all-to-all-start = ((f32[32,8,128]{2,1,0:T(8,128)}), f32[32,8,128]{2,1,0:T(8,128)S(1)}, u32[]{:S(2)}, u32[]{:S(2)}) async-start(f32[32,8,128]{2,1,0:T(8,128)} %get-tuple-element.139), calls=%async_computation | async-start | bytes 262144 | tf_op jit(solution)/shard_map/all_to_all | solution.py:1114
  (43 other events, 365.2 us)

commit v6 on v5

--- a/solution.py
+++ b/solution.py
@@ -41,7 +41,7 @@
 ROWS = 16
 PART = BLOCK // 2
 PARTS = (PART + TAIL, PART)
-TILE = 256
+TILE = 512
 TILES = FF // TILE
 GROUP = 4
 GROUPS = HEADS // GROUP
@@ -367,8 +367,7 @@
     by_hand, bucket, middle, cotangent, far_cotangent, vectors, lines, *rest
 ):
     (
-        own_out,
-        far_out,
+        acc,
         hat,
         scale,
         back_out,
@@ -382,7 +381,6 @@
         reduce_w,
         normed,
         normed_t,
-        acc,
         grads,
     ) = rest
     step = pl.program_id(0)
@@ -415,7 +413,7 @@
     columns = pl.ds(pl.multiple_of(step * TILE, TILE), TILE)
     expand = expand_w[:, columns]
     reduce = reduce_w[columns, :]
-    bias = vectors[pl.ds(10 + step // 2, 1), pl.ds(pl.multiple_of((step % 2) * TILE, TILE), TILE)]
+    bias = vectors[pl.ds(10 + step, 1), :]
     hidden = dot(normed[...], expand) + bias
     density = jnp.exp(hidden * hidden * -0.5) * (1.0 / math.sqrt(2.0 * math.pi))
     below = 0.5 + 0.5 * lax.erf(hidden * math.sqrt(0.5))
@@ -438,11 +436,6 @@
 
     @pl.when(step == TILES - 1)
     def _():
-        for image in range(MINE):
-            near = slice(image * SLOTS, image * SLOTS + SLOTS // 2)
-            far = slice(image * SLOTS + SLOTS // 2, (image + 1) * SLOTS)
-            own_out[image] = middle[near, :] + acc[near, :] + vectors[9:10, :]
-            far_out[image] = (middle[far, :] + acc[far, :] + vectors[9:10, :]).astype(BF)
         cut = HALF - EXPAND_AT
         head_lines[...] = grads[:cut, :].astype(BF)
         put_blocks(
@@ -495,8 +488,7 @@
 
 def middle_call(by_hand, *operands):
     outs = (
-        pltpu.VMEM((MINE, SLOTS // 2, D), F32),
-        pltpu.VMEM((MINE, SLOTS // 2, D), BF),
+        pltpu.VMEM((TOKENS, D), F32),
         pltpu.VMEM((TOKENS, D), F32),
         pltpu.VMEM((TOKENS, LANES), F32),
         pltpu.VMEM((TOKENS, D), BF),
@@ -518,10 +510,9 @@
             pltpu.VMEM((FF, D), BF),
             pltpu.VMEM((TOKENS, D), BF),
             pltpu.VMEM((D, TOKENS), BF),
-            pltpu.VMEM((TOKENS, D), F32),
             pltpu.VMEM((2 * D * 16, LANES), F32),
         ],
-        compiler_params=pltpu.CompilerParams(vmem_limit_bytes=20 * 2**20),
+        compiler_params=pltpu.CompilerParams(vmem_limit_bytes=26 * 2**20),
         cost_estimate=pl.CostEstimate(
             flops=8 * 10**9, bytes_accessed=16 * 2**20, transcendentals=2 * 10**6
         ),
@@ -529,9 +520,14 @@
 
 
 def branch_kernel(
-    hat, scale, back_out, acc_back, mixed, output_w, vectors,
-    back_middle, back_mixed, out_lines, rows_out, out_grads,
+    middle, acc, hat, scale, back_out, acc_back, mixed, output_w, vectors,
+    own_out, far_out, back_middle, back_mixed, out_lines, rows_out, out_grads,
 ):
+    for image in range(MINE):
+        near = slice(image * SLOTS, image * SLOTS + SLOTS // 2)
+        far = slice(image * SLOTS + SLOTS // 2, (image + 1) * SLOTS)
+        own_out[image] = middle[near, :] + acc[near, :] + vectors[9:10, :]
+        far_out[image] = (middle[far, :] + acc[far, :] + vectors[9:10, :]).astype(BF)
     grad = acc_back[...]
     rows_out[...] = jnp.zeros_like(rows_out)
     rows_out[1:2, :] = total(grad * hat[...])
@@ -550,8 +546,10 @@
     out_lines[...] = out_grads[...].astype(BF)
 
 
-def branch_call(hat, scale, back_out, acc_back, mixed, output_w, vectors):
+def branch_call(*operands):
     outs = (
+        pltpu.VMEM((MINE, SLOTS // 2, D), F32),
+        pltpu.VMEM((MINE, SLOTS // 2, D), BF),
         pltpu.VMEM((TOKENS, D), F32),
         pltpu.VMEM((TOKENS, D), BF),
         pltpu.VMEM((EXPAND_AT - OUTPUT_AT, LANES), BF),
@@ -559,7 +557,7 @@
     )
     return pl.pallas_call(
         branch_kernel,
-        in_specs=[VMEM] * 7,
+        in_specs=[VMEM] * len(operands),
         out_shape=outs,
         out_specs=tuple(VMEM for _ in outs),
         scratch_shapes=[pltpu.VMEM((D * 4, LANES), F32)],
@@ -567,12 +565,12 @@
         cost_estimate=pl.CostEstimate(
             flops=2 * 10**9, bytes_accessed=4 * 2**20, transcendentals=0
         ),
-    )(hat, scale, back_out, acc_back, mixed, output_w, vectors)
+    )(*operands)
 
 
 def attention_back_kernel(
     probs, shares, joint, back_mixed, normed, start, back_middle, vectors, joint_w,
-    joint_lines, back_start, rows_out,
+    back_start, rows_out,
     joint_back, key_t, back_t, shared_t, shared, query_back_t, even, odd, grads,
 ):
     key_t[...] = joint[:, D : 2 * D].T
@@ -648,7 +646,6 @@
     rows_out[0:1, :] = total(grad * hat)
     rows_out[1:2, :] = total(grad)
     back_start[...] = back_middle[...] + norm_back(grad, hat, scale, vectors[2:3, :])
-    joint_lines[...] = grads[...].astype(BF)
 
 
 def input_back_kernel(
@@ -704,8 +701,7 @@
         pack[image, SLOTS // 2 + KMAX // 2 :, DIN - D :] = far[KMAX // 4 :, D:]
     rows_out[6:10, :] = rows_in[0:4, :]
     for j in range(4):
-        rows_out[10 + j : 11 + j, :TILE] = expand_in[2 * j : 2 * j + 1, :]
-        rows_out[10 + j : 11 + j, TILE:] = expand_in[2 * j + 1 : 2 * j + 2, :]
+        rows_out[10 + j : 11 + j, :] = expand_in[j : j + 1, :]
     tails[...] = jnp.zeros_like(tails)
     for row in range(ROWS):
         for j in range(D // LANES):
@@ -734,7 +730,7 @@
 
     ranges = (
         (EMBED_AT, JOINT_AT, lambda low, high: grads[low:high, :].astype(BF)),
-        (JOINT_AT, OUTPUT_AT, lambda low, high: joint_lines[low:high, :]),
+        (JOINT_AT, OUTPUT_AT, lambda low, high: joint_lines[low:high, :].astype(BF)),
         (OUTPUT_AT, EXPAND_AT, lambda low, high: out_lines[low:high, :]),
         (EXPAND_AT, HALF, lambda low, high: head_lines[low:high, :]),
     )
@@ -753,11 +749,12 @@
         refs[:9], refs[9:17],
     )
     outs, scratch = refs[17:24], refs[24:]
-    joint_lines, back_start, rows_joint = scratch[:3]
-    attention_back_kernel(*attention, joint_lines, back_start, rows_joint, *scratch[3:12])
+    back_start, rows_joint = scratch[:2]
+    attention_back_kernel(*attention, back_start, rows_joint, *scratch[2:11])
+    joint_lines = scratch[10]
     input_back_kernel(
         by_hand, back_start, my_latents, choices, embed_w, joint_lines, rows_joint, out_lines,
-        head_lines, rows_in, expand_in, far_out, *outs, *scratch[12:],
+        head_lines, rows_in, expand_in, far_out, *outs, *scratch[11:],
     )
 
 
@@ -778,7 +775,6 @@
         out_shape=outs,
         out_specs=tuple(VMEM for _ in outs),
         scratch_shapes=[
-            pltpu.VMEM((OUTPUT_AT - JOINT_AT, LANES), BF),
             pltpu.VMEM((TOKENS, D), F32),
             pltpu.VMEM((8, D), F32),
             pltpu.VMEM((TOKENS, 3 * D), BF),
@@ -1079,12 +1075,12 @@
         probs, shares, joint, normed, start, middle, mixed, embed_w, joint_w, output_w,
     ) = forward_call(bucket, my_latents, choice, my_position, vectors, lines)
     (
-        own_out, far_out, hat, scale, back_out, acc_back, head_lines, far_high, near_high, expand_b,
+        acc, hat, scale, back_out, acc_back, head_lines, far_high, near_high, expand_b,
     ) = middle_call(by_hand, bucket, middle, cotangent, far_cotangent, vectors, lines)
     if by_hand:
         high = Reduction(grid, far_high, near_high, HIGH_ORDER)
-    back_middle, back_mixed, out_lines, rows_b = branch_call(
-        hat, scale, back_out, acc_back, mixed, output_w, vectors
+    own_out, far_out, back_middle, back_mixed, out_lines, rows_b = branch_call(
+        middle, acc, hat, scale, back_out, acc_back, mixed, output_w, vectors
     )
     if by_hand:
         back_mixed = after(back_mixed, high.hop(back_mixed))

time: 146 us -> 145 us (level)
  transfers between devices with their start and end apart: 50 -> 50, of which waited for: 20 -> 21; matrix products, arithmetic and copies ran while one was open for 1% -> 1% of each run, Pallas kernels for 19% -> 20%
where the time goes in v6:
time: 145 us
  waiting for transfers between devices  47.8 us (33%)
  starting transfers between devices  47.5 us (33%)
  Pallas kernels  43.6 us (30%)
  local copies, waits for them, and re-layouts  2.81 us (2%)
  other arithmetic  2.09 us (1%)
    ppermute x45, starting transfers between devices, send(): return lax.ppermute(value, self.axes, pairs)  39.7 us
    ppermute x45, waiting for transfers between devices, send(): return lax.ppermute(value, self.axes, pairs)  37.7 us
    pallas_call x1, Pallas kernels, middle_call(): pl.pallas_call(lambda *refs: middle_kernel(by_hand, *refs), grid=(TILES,)...  13.4 us
    pallas_call x1, Pallas kernels, back_call(): pl.pallas_call(lambda *refs: back_kernel(by_hand, *refs), in_specs=[VMEM]...  11.3 us
    pallas_call x1, Pallas kernels, forward_call(): pl.pallas_call(forward_kernel, in_specs=[SMEM] + [VMEM] * (len(operands)...  7.69 us
    all_to_all x1, waiting for transfers between devices, local(): notes = lax.all_to_all(notes, grid.axes, 0, 0, tiled=True)  7.48 us
    all_to_all x1, starting transfers between devices, local(): notes = lax.all_to_all(notes, grid.axes, 0, 0, tiled=True)  4.15 us
    ppermute x4, starting transfers between devices, trade(): return lax.ppermute(value, 'blk', [(0, 1), (1, 0)])  3.66 us
  transfers between devices with their start and end apart: 50, of which 21 were waited for; matrix products, arithmetic and copies ran while one was open for 1% of the time, Pallas kernels for 20%

profile of v6, /device:TPU:0, one launch (start us, length us, event | category | flops | bytes accessed | tf_op | source)
XLA Modules:
  0.0 144.8 jit_solution(9095800176857884501)
XLA Ops:
  1.7 3.1 %collective-permute-start.14 = (bf16[864,128]{1,0:T(8,128)(2,1)S(1)}, bf16[864,128]{1,0:T(8,128)(2,1)S(1)}, u32[]{:S(2)}, u32[]{:S(2)}) collective-permute-start(bf16[864,128]{1,0:T(8,128)(2,1)S(1)} %bitcast_convert_fusion.refs_0_), channel_id=1, source_target_pairs={{0,8},{1,9},{2,10},{3,11},{4,12},{5,13},{6,14},{7,15},{8,0},{9,1},... | collective-permute-start | bytes 663560 | tf_op jit(solution)/shard_map/ppermute | solution.py:809
  6.3 2.6 %collective-permute-start.3 = (bf16[864,128]{1,0:T(8,128)(2,1)S(1)}, bf16[864,128]{1,0:T(8,128)(2,1)S(1)}, u32[]{:S(2)}, u32[]{:S(2)}) collective-permute-start(bf16[864,128]{1,0:T(8,128)(2,1)S(1)} %bitcast_convert_fusion.refs_0_), channel_id=1, source_target_pairs={{0,16},{1,17},{2,18},{3,19},{4,20},{5,21},{6,22},{7,23},{8,24},{9,... | collective-permute-start | bytes 663560 | tf_op jit(solution)/shard_map/ppermute | solution.py:809
  10.4 4.5 %collective-permute-start.18 = (bf16[864,128]{1,0:T(8,128)(2,1)S(1)}, bf16[864,128]{1,0:T(8,128)(2,1)S(1)}, u32[]{:S(2)}, u32[]{:S(2)}) collective-permute-start(bf16[864,128]{1,0:T(8,128)(2,1)S(1)} %collective-permute-done.14.refs_8_), channel_id=1, source_target_pairs={{0,1},{1,0},{2,6},{3,7},{4,5},{5,4},{6,2},{7,3},{8,9},{9,8},{10,14... | collective-permute-start | bytes 663560 | tf_op jit(solution)/shard_map/ppermute | solution.py:809
  16.4 3.4 %collective-permute-done.3.refs_16_ = bf16[864,128]{1,0:T(8,128)(2,1)S(1)} collective-permute-done((bf16[864,128]{1,0:T(8,128)(2,1)S(1)}, bf16[864,128]{1,0:T(8,128)(2,1)S(1)}, u32[]{:S(2)}, u32[]{:S(2)}) %collective-permute-start.3) | collective-permute-done | bytes 221216 | tf_op jit(solution)/shard_map/ppermute | solution.py:809
  23.4 4.0 %collective-permute-done.23.refs_20_ = bf16[864,128]{1,0:T(8,128)(2,1)S(1)} collective-permute-done((bf16[864,128]{1,0:T(8,128)(2,1)S(1)}, bf16[864,128]{1,0:T(8,128)(2,1)S(1)}, u32[]{:S(2)}, u32[]{:S(2)}) %collective-permute-start.23) | collective-permute-done | bytes 221216 | tf_op jit(solution)/shard_map/ppermute | solution.py:809
  37.7 2.2 %collective-permute-done.25.refs_22_ = bf16[864,128]{1,0:T(8,128)(2,1)} collective-permute-done((bf16[864,128]{1,0:T(8,128)(2,1)S(1)}, bf16[864,128]{1,0:T(8,128)(2,1)}, u32[]{:S(2)}, u32[]{:S(2)}) %collective-permute-start.25) | collective-permute-done | bytes 221216 | tf_op jit(solution)/shard_map/ppermute | solution.py:809
  46.1 1.9 %collective-permute-done.31.refs_30_ = bf16[864,128]{1,0:T(8,128)(2,1)S(1)} collective-permute-done((bf16[864,128]{1,0:T(8,128)(2,1)}, bf16[864,128]{1,0:T(8,128)(2,1)S(1)}, u32[]{:S(2)}, u32[]{:S(2)}) %collective-permute-start.31) | collective-permute-done | bytes 221216 | tf_op jit(solution)/shard_map/ppermute | solution.py:809
  50.5 2.6 %shard_map.179.lines.refs_5_ = bf16[27648,128]{1,0:T(8,128)(2,1)S(1)} custom-call(bf16[864,128]{1,0:T(8,128)(2,1)S(1)} %bitcast_convert_fusion.refs_0_, bf16[864,128]{1,0:T(8,128)(2,1)S(1)} %collective-permute-done.9.refs_1_, bf16[864,128]{1,0:T(8,128)(2,1)S(1)} %collective-permute-done.refs_2_, bf16[864,128]{1,0:T(8,128)(2,1)S(1)} %collective-permute-done.10.refs_3_, ...), custom_call_target="tpu_custom_call" | custom-call | bytes 1048576 | tf_op jit(solution)/shard_map/pallas_call | solution.py:92
  53.1 7.7 %shard_map.180 = (bf16[32,256,256]{2,1,0:T(8,128)(2,1)S(1)}, f32[32,256]{1,0:T(8,128)S(1)}, bf16[512,1536]{1,0:T(8,128)(2,1)S(1)}, bf16[512,512]{1,0:T(8,128)(2,...) custom-call(s32[4]{0:T(128)S(1)} %copy-done.16, ...), custom_call_target="tpu_custom_call" | custom-call | flops 6000000000 | bytes 16777216 | tf_op jit(solution)/shard_map/pallas_call | solution.py:346
  60.9 13.4 %shard_map.181 = (f32[512,512]{1,0:T(8,128)S(1)}, f32[512,512]{1,0:T(8,128)S(1)}, f32[512,128]{1,0:T(8,128)S(1)}, bf16[512,512]{1,0:T(8,128)(2,1)S(1)}, f32[512,...) custom-call(s32[4]{0:T(128)S(1)} %copy-done.16, ...), custom_call_target="tpu_custom_call" | custom-call | flops 8000000000 | bytes 16777216 | tf_op jit(solution)/shard_map/pallas_call | solution.py:501
  76.2 1.8 %collective-permute-done.34.refs_1_ = bf16[6912,128]{1,0:T(8,128)(2,1)S(1)} collective-permute-done((bf16[6912,128]{1,0:T(8,128)(2,1)S(1)}, bf16[6912,128]{1,0:T(8,128)(2,1)S(1)}, u32[]{:S(2)}, u32[]{:S(2)}) %collective-permute-start.34) | collective-permute-done | bytes 1769504 | tf_op jit(solution)/shard_map/ppermute | solution.py:809
  78.2 1.7 %collective-permute-start.35 = (bf16[3456,128]{1,0:T(8,128)(2,1)S(1)}, bf16[3456,128]{1,0:T(8,128)(2,1)S(1)}, u32[]{:S(2)}, u32[]{:S(2)}) collective-permute-start(bf16[3456,128]{1,0:T(8,128)(2,1)S(1)} %shard_map.183), channel_id=1, source_target_pairs={{0,1},{1,0},{2,6},{3,7},{4,5},{5,4},{6,2},{7,3},{8,9},{9,8},{10,14... | collective-permute-start | bytes 2654216 | tf_op jit(solution)/shard_map/ppermute | solution.py:809
  79.9 11.3 %shard_map.184 = (bf16[3584,128]{1,0:T(8,128)(2,1)S(1)}, bf16[3584,128]{1,0:T(8,128)(2,1)S(1)}, bf16[3456,128]{1,0:T(8,128)(2,1)S(1)}, bf16[3456,128]{1,0:T(8,12...) custom-call(bf16[32,256,256]{2,1,0:T(8,128)(2,1)S(1)} %get-tuple-element.100.refs_0_, ...), custom_call_target="tpu_custom_call" | custom-call | flops 4000000000 | bytes 8388608 | tf_op jit(solution)/shard_map/pallas_call | solution.py:772
  92.0 2.0 %collective-permute-done.36.refs_1_ = bf16[3584,128]{1,0:T(8,128)(2,1)S(1)} collective-permute-done((bf16[3584,128]{1,0:T(8,128)(2,1)S(1)}, bf16[3584,128]{1,0:T(8,128)(2,1)S(1)}, u32[]{:S(2)}, u32[]{:S(2)}) %collective-permute-start.36) | collective-permute-done | bytes 917536 | tf_op jit(solution)/shard_map/ppermute | solution.py:809
  94.1 1.7 %collective-permute-start.38 = (bf16[1792,128]{1,0:T(8,128)(2,1)S(1)}, bf16[1792,128]{1,0:T(8,128)(2,1)S(1)}, u32[]{:S(2)}, u32[]{:S(2)}) collective-permute-start(bf16[1792,128]{1,0:T(8,128)(2,1)S(1)} %shard_map.186), channel_id=1, source_target_pairs={{0,1},{1,0},{2,6},{3,7},{4,5},{5,4},{6,2},{7,3},{8,9},{9,8},{10,14... | collective-permute-start | bytes 1376264 | tf_op jit(solution)/shard_map/ppermute | solution.py:809
  97.9 4.8 %collective-permute-done.38.refs_2_ = bf16[1792,128]{1,0:T(8,128)(2,1)S(1)} collective-permute-done((bf16[1792,128]{1,0:T(8,128)(2,1)S(1)}, bf16[1792,128]{1,0:T(8,128)(2,1)S(1)}, u32[]{:S(2)}, u32[]{:S(2)}) %collective-permute-start.38) | collective-permute-done | bytes 458784 | tf_op jit(solution)/shard_map/ppermute | solution.py:809
  104.3 3.3 %collective-permute-done.39.refs_3_ = bf16[1728,128]{1,0:T(8,128)(2,1)S(1)} collective-permute-done((bf16[1728,128]{1,0:T(8,128)(2,1)S(1)}, bf16[1728,128]{1,0:T(8,128)(2,1)S(1)}, u32[]{:S(2)}, u32[]{:S(2)}) %collective-permute-start.39) | collective-permute-done | bytes 442400 | tf_op jit(solution)/shard_map/ppermute | solution.py:809
  113.8 2.2 %collective-permute-done.43.refs_3_ = bf16[864,128]{1,0:T(8,128)(2,1)S(1)} collective-permute-done((bf16[864,128]{1,0:T(8,128)(2,1)S(1)}, bf16[864,128]{1,0:T(8,128)(2,1)S(1)}, u32[]{:S(2)}, u32[]{:S(2)}) %collective-permute-start.43) | collective-permute-done | bytes 221216 | tf_op jit(solution)/shard_map/ppermute | solution.py:809
  117.7 2.1 %collective-permute-start.47 = (bf16[448,128]{1,0:T(8,128)(2,1)S(1)}, bf16[448,128]{1,0:T(8,128)(2,1)S(1)}, u32[]{:S(2)}, u32[]{:S(2)}) collective-permute-start(bf16[448,128]{1,0:T(8,128)(2,1)S(1)} %shard_map.197), channel_id=1, source_target_pairs={{0,16},{1,17},{2,18},{3,19},{4,20},{5,21},{6,22},{7,23},{8,24},{9,... | collective-permute-start | bytes 344072 | tf_op jit(solution)/shard_map/ppermute | solution.py:809
  119.8 2.0 %collective-permute-done.45.refs_4_ = bf16[432,128]{1,0:T(8,128)(2,1)S(1)} collective-permute-done((bf16[432,128]{1,0:T(8,128)(2,1)S(1)}, bf16[432,128]{1,0:T(8,128)(2,1)S(1)}, u32[]{:S(2)}, u32[]{:S(2)}) %collective-permute-start.45) | collective-permute-done | bytes 110624 | tf_op jit(solution)/shard_map/ppermute | solution.py:809
  122.0 1.9 %collective-permute-start.48 = (bf16[432,128]{1,0:T(8,128)(2,1)S(1)}, bf16[432,128]{1,0:T(8,128)(2,1)S(1)}, u32[]{:S(2)}, u32[]{:S(2)}) collective-permute-start(bf16[432,128]{1,0:T(8,128)(2,1)S(1)} %shard_map.198), channel_id=1, source_target_pairs={{0,16},{1,17},{2,18},{3,19},{4,20},{5,21},{6,22},{7,23},{8,24},{9,... | collective-permute-start | bytes 331784 | tf_op jit(solution)/shard_map/ppermute | solution.py:809
  125.0 4.4 %collective-permute-done.48.two_far = bf16[432,128]{1,0:T(8,128)(2,1)S(1)} collective-permute-done((bf16[432,128]{1,0:T(8,128)(2,1)S(1)}, bf16[432,128]{1,0:T(8,128)(2,1)S(1)}, u32[]{:S(2)}, u32[]{:S(2)}) %collective-permute-start.48) | collective-permute-done | bytes 110624 | tf_op jit(solution)/shard_map/ppermute | solution.py:809
  130.5 4.1 %all-to-all-start = ((f32[32,8,128]{2,1,0:T(8,128)}), f32[32,8,128]{2,1,0:T(8,128)S(1)}, u32[]{:S(2)}, u32[]{:S(2)}) async-start(f32[32,8,128]{2,1,0:T(8,128)} %get-tuple-element.141), calls=%async_computation | async-start | bytes 262144 | tf_op jit(solution)/shard_map/all_to_all | solution.py:1110
  135.8 7.5 %all-to-all-done.notes = f32[32,8,128]{2,1,0:T(8,128)S(1)} async-done(((f32[32,8,128]{2,1,0:T(8,128)}), f32[32,8,128]{2,1,0:T(8,128)S(1)}, u32[]{:S(2)}, u32[]{:S(2)}) %all-to-all-start) | async-done | bytes 131104 | tf_op jit(solution)/shard_map/all_to_all | solution.py:1110
  (139 shorter events, 47.6 us)
Async XLA Ops:
  1.7 8.7 %collective-permute-start.14 = (bf16[864,128]{1,0:T(8,128)(2,1)S(1)}, bf16[864,128]{1,0:T(8,128)(2,1)S(1)}, u32[]{:S(2)}, u32[]{:S(2)}) collective-permute-start(bf16[864,128]{1,0:T(8,128)(2,1)S(1)} %bitcast_convert_fusion.refs_0_), channel_id=1, source_target_pairs={{0,8},{1,9},{2,10},{3,11},{4,12},{5,13},{6,14},{7,15},{8,0},{9,1},... | collective-permute-start | bytes 663560 | tf_op jit(solution)/shard_map/ppermute | solution.py:809
  4.8 10.1 %collective-permute-start.11 = (bf16[864,128]{1,0:T(8,128)(2,1)S(1)}, bf16[864,128]{1,0:T(8,128)(2,1)S(1)}, u32[]{:S(2)}, u32[]{:S(2)}) collective-permute-start(bf16[864,128]{1,0:T(8,128)(2,1)S(1)} %bitcast_convert_fusion.refs_0_), channel_id=1, source_target_pairs={{0,1},{1,0},{2,6},{3,7},{4,5},{5,4},{6,2},{7,3},{8,9},{9,8},{10,14... | collective-permute-start | bytes 663560 | tf_op jit(solution)/shard_map/ppermute | solution.py:809
  6.3 10.0 %collective-permute-start.9 = (bf16[864,128]{1,0:T(8,128)(2,1)S(1)}, bf16[864,128]{1,0:T(8,128)(2,1)S(1)}, u32[]{:S(2)}, u32[]{:S(2)}) collective-permute-start(bf16[864,128]{1,0:T(8,128)(2,1)S(1)} %bitcast_convert_fusion.refs_0_), channel_id=1, source_target_pairs={{0,2},{1,3},{2,0},{3,1},{4,6},{5,7},{6,4},{7,5},{8,10},{9,11},{10,... | collective-permute-start | bytes 663560 | tf_op jit(solution)/shard_map/ppermute | solution.py:809
  6.3 13.5 %collective-permute-start.3 = (bf16[864,128]{1,0:T(8,128)(2,1)S(1)}, bf16[864,128]{1,0:T(8,128)(2,1)S(1)}, u32[]{:S(2)}, u32[]{:S(2)}) collective-permute-start(bf16[864,128]{1,0:T(8,128)(2,1)S(1)} %bitcast_convert_fusion.refs_0_), channel_id=1, source_target_pairs={{0,16},{1,17},{2,18},{3,19},{4,20},{5,21},{6,22},{7,23},{8,24},{9,... | collective-permute-start | bytes 663560 | tf_op jit(solution)/shard_map/ppermute | solution.py:809
  8.9 10.9 %collective-permute-start = (bf16[864,128]{1,0:T(8,128)(2,1)S(1)}, bf16[864,128]{1,0:T(8,128)(2,1)S(1)}, u32[]{:S(2)}, u32[]{:S(2)}) collective-permute-start(bf16[864,128]{1,0:T(8,128)(2,1)S(1)} %bitcast_convert_fusion.refs_0_), channel_id=1, source_target_pairs={{0,4},{1,5},{2,3},{3,2},{4,0},{5,1},{6,7},{7,6},{8,12},{9,13},{10,... | collective-permute-start | bytes 663560 | tf_op jit(solution)/shard_map/ppermute | solution.py:809
  10.4 10.0 %collective-permute-start.18 = (bf16[864,128]{1,0:T(8,128)(2,1)S(1)}, bf16[864,128]{1,0:T(8,128)(2,1)S(1)}, u32[]{:S(2)}, u32[]{:S(2)}) collective-permute-start(bf16[864,128]{1,0:T(8,128)(2,1)S(1)} %collective-permute-done.14.refs_8_), channel_id=1, source_target_pairs={{0,1},{1,0},{2,6},{3,7},{4,5},{5,4},{6,2},{7,3},{8,9},{9,8},{10,14... | collective-permute-start | bytes 663560 | tf_op jit(solution)/shard_map/ppermute | solution.py:809
  19.8 7.6 %collective-permute-start.23 = (bf16[864,128]{1,0:T(8,128)(2,1)S(1)}, bf16[864,128]{1,0:T(8,128)(2,1)S(1)}, u32[]{:S(2)}, u32[]{:S(2)}) collective-permute-start(bf16[864,128]{1,0:T(8,128)(2,1)S(1)} %collective-permute-done.3.refs_16_), channel_id=1, source_target_pairs={{0,1},{1,0},{2,6},{3,7},{4,5},{5,4},{6,2},{7,3},{8,9},{9,8},{10,14... | collective-permute-start | bytes 663560 | tf_op jit(solution)/shard_map/ppermute | solution.py:809
  20.4 8.3 %collective-permute-start.5 = (bf16[864,128]{1,0:T(8,128)(2,1)S(1)}, bf16[864,128]{1,0:T(8,128)(2,1)S(1)}, u32[]{:S(2)}, u32[]{:S(2)}) collective-permute-start(bf16[864,128]{1,0:T(8,128)(2,1)S(1)} %collective-permute-done.3.refs_16_), channel_id=1, source_target_pairs={{0,4},{1,5},{2,3},{3,2},{4,0},{5,1},{6,7},{7,6},{8,12},{9,13},{10,... | collective-permute-start | bytes 663560 | tf_op jit(solution)/shard_map/ppermute | solution.py:809
  21.8 7.3 %collective-permute-start.4 = (bf16[864,128]{1,0:T(8,128)(2,1)S(1)}, bf16[864,128]{1,0:T(8,128)(2,1)S(1)}, u32[]{:S(2)}, u32[]{:S(2)}) collective-permute-start(bf16[864,128]{1,0:T(8,128)(2,1)S(1)} %collective-permute-done.3.refs_16_), channel_id=1, source_target_pairs={{0,8},{1,9},{2,10},{3,11},{4,12},{5,13},{6,14},{7,15},{8,0},{9,1},... | collective-permute-start | bytes 663560 | tf_op jit(solution)/shard_map/ppermute | solution.py:809
  21.9 8.6 %collective-permute-start.1 = (bf16[864,128]{1,0:T(8,128)(2,1)S(1)}, bf16[864,128]{1,0:T(8,128)(2,1)S(1)}, u32[]{:S(2)}, u32[]{:S(2)}) collective-permute-start(bf16[864,128]{1,0:T(8,128)(2,1)S(1)} %collective-permute-done.refs_2_), channel_id=1, source_target_pairs={{0,1},{1,0},{2,6},{3,7},{4,5},{5,4},{6,2},{7,3},{8,9},{9,8},{10,14... | collective-permute-start | bytes 663560 | tf_op jit(solution)/shard_map/ppermute | solution.py:809
  31.1 8.8 %collective-permute-start.25 = (bf16[864,128]{1,0:T(8,128)(2,1)S(1)}, bf16[864,128]{1,0:T(8,128)(2,1)}, u32[]{:S(2)}, u32[]{:S(2)}) collective-permute-start(bf16[864,128]{1,0:T(8,128)(2,1)S(1)} %collective-permute-done.5.refs_18_), channel_id=1, source_target_pairs={{0,1},{1,0},{2,6},{3,7},{4,5},{5,4},{6,2},{7,3},{8,9},{9,8},{10,14... | collective-permute-start | bytes 663560 | tf_op jit(solution)/shard_map/ppermute | solution.py:809
  33.2 7.4 %collective-permute-start.2 = (bf16[864,128]{1,0:T(8,128)(2,1)S(1)}, bf16[864,128]{1,0:T(8,128)(2,1)}, u32[]{:S(2)}, u32[]{:S(2)}) collective-permute-start(bf16[864,128]{1,0:T(8,128)(2,1)S(1)} %collective-permute-done.1.refs_6_), channel_id=1, source_target_pairs={{0,8},{1,9},{2,10},{3,11},{4,12},{5,13},{6,14},{7,15},{8,0},{9,1},... | collective-permute-start | bytes 663560 | tf_op jit(solution)/shard_map/ppermute | solution.py:809
  40.6 7.4 %collective-permute-start.31 = (bf16[864,128]{1,0:T(8,128)(2,1)}, bf16[864,128]{1,0:T(8,128)(2,1)S(1)}, u32[]{:S(2)}, u32[]{:S(2)}) collective-permute-start(bf16[864,128]{1,0:T(8,128)(2,1)} %collective-permute-done.25.refs_22_), channel_id=1, source_target_pairs={{0,8},{1,9},{2,10},{3,11},{4,12},{5,13},{6,14},{7,15},{8,0},{9,1},... | collective-permute-start | bytes 663560 | tf_op jit(solution)/shard_map/ppermute | solution.py:809
  43.0 7.4 %collective-permute-start.26 = (bf16[864,128]{1,0:T(8,128)(2,1)}, bf16[864,128]{1,0:T(8,128)(2,1)S(1)}, u32[]{:S(2)}, u32[]{:S(2)}) collective-permute-start(bf16[864,128]{1,0:T(8,128)(2,1)} %collective-permute-done.25.refs_22_), channel_id=1, source_target_pairs={{0,2},{1,3},{2,0},{3,1},{4,6},{5,7},{6,4},{7,5},{8,10},{9,11},{10,... | collective-permute-start | bytes 663560 | tf_op jit(solution)/shard_map/ppermute | solution.py:809
  50.0 10.8 %collective-permute-start.33 = (bf16[2,128,512]{2,1,0:T(8,128)(2,1)S(1)}, bf16[2,128,512]{2,1,0:T(8,128)(2,1)S(1)}, u32[]{:S(2)}, u32[]{:S(2)}) collective-permute-start(bf16[2,128,512]{2,1,0:T(8,128)(2,1)S(1)} %get-tuple-element.91), channel_id=1, source_target_pairs={{0,1},{1,0},{2,3},{3,2},{4,5},{5,4},{6,7},{7,6},{8,9},{9,8},{10,11... | collective-permute-start | bytes 786440 | tf_op jit(solution)/shard_map/ppermute | solution.py:1063
  78.2 13.1 %collective-permute-start.35 = (bf16[3456,128]{1,0:T(8,128)(2,1)S(1)}, bf16[3456,128]{1,0:T(8,128)(2,1)S(1)}, u32[]{:S(2)}, u32[]{:S(2)}) collective-permute-start(bf16[3456,128]{1,0:T(8,128)(2,1)S(1)} %shard_map.183), channel_id=1, source_target_pairs={{0,1},{1,0},{2,6},{3,7},{4,5},{5,4},{6,2},{7,3},{8,9},{9,8},{10,14... | collective-permute-start | bytes 2654216 | tf_op jit(solution)/shard_map/ppermute | solution.py:809
  94.1 8.5 %collective-permute-start.38 = (bf16[1792,128]{1,0:T(8,128)(2,1)S(1)}, bf16[1792,128]{1,0:T(8,128)(2,1)S(1)}, u32[]{:S(2)}, u32[]{:S(2)}) collective-permute-start(bf16[1792,128]{1,0:T(8,128)(2,1)S(1)} %shard_map.186), channel_id=1, source_target_pairs={{0,1},{1,0},{2,6},{3,7},{4,5},{5,4},{6,2},{7,3},{8,9},{9,8},{10,14... | collective-permute-start | bytes 1376264 | tf_op jit(solution)/shard_map/ppermute | solution.py:809
  95.8 11.7 %collective-permute-start.39 = (bf16[1728,128]{1,0:T(8,128)(2,1)S(1)}, bf16[1728,128]{1,0:T(8,128)(2,1)S(1)}, u32[]{:S(2)}, u32[]{:S(2)}) collective-permute-start(bf16[1728,128]{1,0:T(8,128)(2,1)S(1)} %shard_map.185), channel_id=1, source_target_pairs={{0,8},{1,9},{2,10},{3,11},{4,12},{5,13},{6,14},{7,15},{8,0},{9,1},... | collective-permute-start | bytes 1327112 | tf_op jit(solution)/shard_map/ppermute | solution.py:809
  96.4 13.5 %collective-permute-start.40 = (bf16[1728,128]{1,0:T(8,128)(2,1)S(1)}, bf16[1728,128]{1,0:T(8,128)(2,1)S(1)}, u32[]{:S(2)}, u32[]{:S(2)}) collective-permute-start(bf16[1728,128]{1,0:T(8,128)(2,1)S(1)} %shard_map.187), channel_id=1, source_target_pairs={{0,1},{1,0},{2,6},{3,7},{4,5},{5,4},{6,2},{7,3},{8,9},{9,8},{10,14... | collective-permute-start | bytes 1327112 | tf_op jit(solution)/shard_map/ppermute | solution.py:809
  102.7 8.9 %collective-permute-start.41 = (bf16[896,128]{1,0:T(8,128)(2,1)S(1)}, bf16[896,128]{1,0:T(8,128)(2,1)S(1)}, u32[]{:S(2)}, u32[]{:S(2)}) collective-permute-start(bf16[896,128]{1,0:T(8,128)(2,1)S(1)} %shard_map.188), channel_id=1, source_target_pairs={{0,4},{1,5},{2,3},{3,2},{4,0},{5,1},{6,7},{7,6},{8,12},{9,13},{10,... | collective-permute-start | bytes 688136 | tf_op jit(solution)/shard_map/ppermute | solution.py:809
  117.7 11.8 %collective-permute-start.47 = (bf16[448,128]{1,0:T(8,128)(2,1)S(1)}, bf16[448,128]{1,0:T(8,128)(2,1)S(1)}, u32[]{:S(2)}, u32[]{:S(2)}) collective-permute-start(bf16[448,128]{1,0:T(8,128)(2,1)S(1)} %shard_map.197), channel_id=1, source_target_pairs={{0,16},{1,17},{2,18},{3,19},{4,20},{5,21},{6,22},{7,23},{8,24},{9,... | collective-permute-start | bytes 344072 | tf_op jit(solution)/shard_map/ppermute | solution.py:809
  122.0 7.5 %collective-permute-start.48 = (bf16[432,128]{1,0:T(8,128)(2,1)S(1)}, bf16[432,128]{1,0:T(8,128)(2,1)S(1)}, u32[]{:S(2)}, u32[]{:S(2)}) collective-permute-start(bf16[432,128]{1,0:T(8,128)(2,1)S(1)} %shard_map.198), channel_id=1, source_target_pairs={{0,16},{1,17},{2,18},{3,19},{4,20},{5,21},{6,22},{7,23},{8,24},{9,... | collective-permute-start | bytes 331784 | tf_op jit(solution)/shard_map/ppermute | solution.py:809
  123.9 10.7 %collective-permute-start.46 = (bf16[2,176,512]{2,1,0:T(8,128)(2,1)S(1)}, bf16[2,176,512]{2,1,0:T(8,128)(2,1)S(1)}, u32[]{:S(2)}, u32[]{:S(2)}) collective-permute-start(bf16[2,176,512]{2,1,0:T(8,128)(2,1)S(1)} %get-tuple-element.137), channel_id=1, source_target_pairs={{0,1},{1,0},{2,3},{3,2},{4,5},{5,4},{6,7},{7,6},{8,9},{9,8},{10,11... | collective-permute-start | bytes 1081352 | tf_op jit(solution)/shard_map/ppermute | solution.py:1063
  130.5 12.8 %all-to-all-start = ((f32[32,8,128]{2,1,0:T(8,128)}), f32[32,8,128]{2,1,0:T(8,128)S(1)}, u32[]{:S(2)}, u32[]{:S(2)}) async-start(f32[32,8,128]{2,1,0:T(8,128)} %get-tuple-element.141), calls=%async_computation | async-start | bytes 262144 | tf_op jit(solution)/shard_map/all_to_all | solution.py:1110
  (43 other events, 365.1 us)
